TPU v7x, 32 devices: a whole 2x2x4 slice. The times are simulated.
32 devices in a mesh: frame: 4 (over z), height: 8 (over y, x, core).
Axes of the slice: x: 2, y: 2, z: 4, core: 2. Of those that a mesh axis runs over, the one named last changes fastest.
Arguments:
- video: bfloat16 [33, 16, 32, 256], P(None, 'height', 'frame'), may hold values from -48 to 48
- frame_counts: int32 [4], replicated, may hold values from 1 to 18, 33 in all
- temporal_weight: bfloat16 [6912, 256], replicated, may hold values from -0.125 to 0.125
- temporal_bias: float32 [256], replicated, may hold values from -4 to 4
- first_gain: float32 [256], replicated, may hold values from 0.1 to 1.9
- first_shift: float32 [256], replicated, may hold values from -3 to 3
- first_weight: bfloat16 [2304, 256], P('height'), may hold values from -0.125 to 0.125
- first_bias: float32 [256], replicated, may hold values from -4 to 4
- second_gain: float32 [256], replicated, may hold values from 0.1 to 1.9
- second_shift: float32 [256], replicated, may hold values from -3 to 3
- second_weight: bfloat16 [2304, 256], P('height'), may hold values from -0.125 to 0.125
- second_bias: float32 [256], replicated, may hold values from -4 to 4
Outputs:
- owned: bfloat16 [72, 16, 32, 256], P('frame', 'height')
Inputs may be any that keep to these rules, and one draw needn't show every extreme that they name: frame_counts[k] consecutive frames belong to index k of frame; the counts add up to 33 and the largest is exactly 18.
All inputs are finite; a program needn't handle non-finite values.
Results may differ from a plain program's by a relative error of at most 0.0055.
Values may be sent and summed in bfloat16 or wider, within the bound.
No kernel may reach another device: no remote copies, remote signals or barrier semaphores. Data moves between devices by JAX's collectives and lax.ppermute only.
A program may use at most 64 MiB of HBM per device.

v0:
```python
import jax
import jax.numpy as jnp
from jax import lax
from jax.sharding import PartitionSpec as P

GROUPS = 32


def with_halo(array, sides, width):
    for axis, dim in sides:
        size, length = (lax.axis_size(axis), array.shape[dim])
        up = [(i, (i + 1) % size) for i in range(size - 1)]
        down = [(j, i) for i, j in up]
        last = lax.slice_in_dim(array, length - width, length, axis=dim)
        first = lax.slice_in_dim(array, 0, width, axis=dim)
        before = lax.ppermute(last, axis, up)
        after = lax.ppermute(first, axis, down)
        array = jnp.concatenate([before, array, after], axis=dim)
    return array


def spatial_patches(padded, row_count, col_count):
    pieces = []
    for row_tap in range(3):
        for col_tap in range(3):
            pieces.append(
                padded[:, row_tap : row_tap + row_count, col_tap : col_tap + col_count, :]
            )
    return jnp.concatenate(pieces, axis=-1)


def group_act(tensor, gain_row, shift_row, totals, cell_count):
    frame_slots, row_count, col_count, channels = tensor.shape
    width_group = channels // GROUPS
    grouped = tensor.astype(jnp.float32).reshape(
        frame_slots, row_count, col_count, GROUPS, width_group
    )
    part_sum = jnp.sum(grouped, axis=(1, 2, 4))
    part_sq = jnp.sum(grouped * grouped, axis=(1, 2, 4))
    total_sum, total_sq = totals(part_sum, part_sq)
    sample = float(cell_count * width_group)
    group_mean = total_sum / sample
    group_var = total_sq / sample - group_mean * group_mean
    inverse = lax.rsqrt(group_var + 1e-06)
    normed = (grouped - group_mean[:, None, None, :, None]) * inverse[:, None, None, :, None]
    normed = normed.reshape(frame_slots, row_count, col_count, channels) * gain_row + shift_row
    return jax.nn.silu(normed).astype(jnp.bfloat16)


def convolve(padded, weight_shard, offset_bias):
    frame_slots, row_span, col_span, channels = padded.shape
    row_count = row_span - 2
    col_count = col_span - 2
    patches = spatial_patches(padded, row_count, col_count).reshape(
        frame_slots * row_count * col_count, 9 * channels
    )
    accumulated = jnp.dot(
        patches,
        lax.all_gather(weight_shard, "height", axis=0, tiled=True),
        preferred_element_type=jnp.float32,
    )
    return (accumulated + offset_bias).reshape(frame_slots, row_count, col_count, channels)


def resnet(
    tensor,
    extend,
    totals,
    cell_count,
    first_gain,
    first_shift,
    first_weight,
    first_bias,
    second_gain,
    second_shift,
    second_weight,
    second_bias,
):
    first_in = group_act(tensor, first_gain, first_shift, totals, cell_count)
    first_out = convolve(extend(first_in), first_weight, first_bias).astype(jnp.bfloat16)
    second_in = group_act(first_out, second_gain, second_shift, totals, cell_count)
    return (
        tensor.astype(jnp.float32) + convolve(extend(second_in), second_weight, second_bias)
    ).astype(jnp.bfloat16)


def per_device(
    video,
    frame_counts,
    temporal_weight,
    temporal_bias,
    first_gain,
    first_shift,
    first_weight,
    first_bias,
    second_gain,
    second_shift,
    second_weight,
    second_bias,
):
    frames, row_count, col_count, channels = video.shape
    n_frame = lax.axis_size("frame")
    n_height = lax.axis_size("height")
    capacity = min(2 * ((frames + n_frame - 1) // n_frame), frames - n_frame + 1)
    activated = jax.nn.silu(video.astype(jnp.float32)).astype(jnp.bfloat16)
    bordered = with_halo(activated, (("frame", 2), ("height", 1)), 1)
    causal = jnp.pad(bordered, ((2, 0), (0, 0), (0, 0), (0, 0)))
    accumulated = jnp.zeros((frames * row_count * col_count, channels), jnp.float32)
    for tap_time in range(3):
        patches = spatial_patches(causal[tap_time : tap_time + frames], row_count, col_count)
        patches = patches.reshape(frames * row_count * col_count, 9 * channels)
        accumulated = accumulated + jnp.dot(
            patches,
            temporal_weight[tap_time * 9 * channels : (tap_time + 1) * 9 * channels],
            preferred_element_type=jnp.float32,
        )
    blended = (video.astype(jnp.float32) + accumulated.reshape(video.shape) + temporal_bias).astype(
        jnp.bfloat16
    )
    offsets = jnp.cumsum(frame_counts) - frame_counts
    peer_ids = jnp.arange(n_frame, dtype=jnp.int32)
    cell_count = row_count * n_height * col_count * n_frame

    def extend(tensor):
        extended = with_halo(tensor, (("height", 1),), 1)
        return jnp.pad(extended, ((0, 0), (0, 0), (1, 1), (0, 0)))

    def totals(part_sum, part_sq):
        return lax.psum((part_sum, part_sq), "height")

    slot_ids = jnp.arange(n_frame * capacity, dtype=jnp.int32)
    owner_idx = slot_ids // capacity
    within = slot_ids - owner_idx * capacity
    matches = owner_idx[:, None] == peer_ids[None, :]
    first_frame = jnp.sum(jnp.where(matches, offsets[None, :], 0), axis=1)
    frame_total = jnp.sum(jnp.where(matches, frame_counts[None, :], 0), axis=1)
    source_idx = jnp.clip(first_frame + within, 0, frames - 1)
    picked = jnp.take(blended, source_idx, axis=0)
    retained = jnp.where(
        (within < frame_total)[:, None, None, None], picked, jnp.zeros_like(picked)
    )
    owned_frames = lax.all_to_all(retained, "frame", split_axis=0, concat_axis=2, tiled=True)
    decoded = resnet(
        owned_frames,
        extend,
        totals,
        cell_count,
        first_gain,
        first_shift,
        first_weight,
        first_bias,
        second_gain,
        second_shift,
        second_weight,
        second_bias,
    )
    my_count = jnp.sum(jnp.where(peer_ids == lax.axis_index("frame"), frame_counts, 0))
    live_slots = jnp.arange(capacity, dtype=jnp.int32) < my_count
    return jnp.where(live_slots[:, None, None, None], decoded, jnp.zeros_like(decoded))


def solution(mesh):
    placed = (
        P(None, "height", "frame", None),
        P(),
        P(),
        P(),
        P(),
        P(),
        P("height", None),
        P(),
        P(),
        P(),
        P("height", None),
        P(),
    )
    return jax.shard_map(
        per_device,
        mesh=mesh,
        in_specs=placed,
        out_specs=P("frame", "height", None, None),
        check_vma=False,
    )
```

profile of v0, /device:TPU:0, one launch (start us, length us, event | category | flops | bytes accessed | tf_op | source)
XLA Modules:
  0.0 198.8 jit_solution(10991419762594612236)
XLA Ops:
  6.5 1.1 fusion.34
  7.8 4.9 %collective-permute-start = (bf16[33,2,1,256]{3,2,1,0:T(2,128)(2,1)S(1)}, bf16[33,2,1,256]{3,2,1,0:T(2,128)(2,1)S(1)}, u32[]{:S(2)}, u32[]{:S(2)}) collective-permute-start(bf16[33,2,1,256]{3,2,1,0:T(2,128)(2,1)S(1)} %get-tuple-element.41), channel_id=1, source_target_pairs={{0,8},{8,16},{16,24},{1,9},{9,17},{17,25},{2,10},{10,18},{18,26},{... | collective-permute-start | bytes 101384 | tf_op jit(solution)/shard_map/ppermute | solution.py:16
  12.7 1.3 collective-permute-start.1
  14.0 0.8 reduce-window.9
  14.8 1.4 fusion.42
  17.0 1.9 collective-permute-done.1
  19.3 1.3 collective-permute-start.2
  20.6 1.3 collective-permute-start.3
  21.9 3.8 %collective-permute-done.3 = bf16[33,1,10,256]{3,2,1,0:T(8,128)(2,1)S(1)} collective-permute-done((bf16[33,1,10,256]{3,2,1,0:T(8,128)(2,1)S(1)}, bf16[33,1,10,256]{3,2,1,0:T(8,128)(2,1)S(1)}, u32[]{:S(2)}, u32[]{:S(2)}) %collective-permute-start.3) | collective-permute-done | bytes 168992 | tf_op jit(solution)/shard_map/ppermute | solution.py:17
  25.7 0.9 pad_maximum_fusion
  28.7 1.7 copy-done.10
  32.0 0.8 convolution_add_fusion.2
  33.8 19.2 %all_to_all.4 = bf16[72,2,8,256]{3,2,1,0:T(8,128)(2,1)S(1)} all-to-all(bf16[72,2,8,256]{3,2,1,0:T(8,128)(2,1)S(1)} %select_select_fusion), channel_id=1, replica_groups=mesh['frame'=4,'height'=8] {'frame'}, dimensions={0} | all-to-all | bytes 1179648 | tf_op jit(solution)/shard_map/all_to_all | solution.py:142
  53.4 26.9 %all-reduce.4 = (f32[18,32]{0,1:T(8,128)S(1)}, f32[18,32]{0,1:T(8,128)S(1)}) all-reduce(f32[18,32]{0,1:T(8,128)S(1)} %bitcast_reduce_fusion.1, f32[18,32]{0,1:T(8,128)S(1)} %bitcast_reduce_fusion.2), channel_id=1, replica_groups=mesh['frame'=4,'height'=8] {'height'}, use_global_device_ids=true, to_apply=%region_9.10 | all-reduce | flops 1152 | bytes 9216 | tf_op jit(solution)/shard_map/psum | solution.py:129
  81.1 1.3 collective-permute-start.4
  82.4 1.3 collective-permute-start.5
  83.9 2.4 %collective-permute-done.5 = bf16[18,1,32,256]{3,2,1,0:T(8,128)(2,1)S(1)} collective-permute-done((bf16[18,1,32,256]{3,2,1,0:T(8,128)(2,1)S(1)}, bf16[18,1,32,256]{3,2,1,0:T(8,128)(2,1)S(1)}, u32[]{:S(2)}, u32[]{:S(2)}) %collective-permute-start.5) | collective-permute-done | bytes 294944 | tf_op jit(solution)/shard_map/ppermute | solution.py:17
  86.4 0.8 fusion.12
  87.2 0.9 slice_dynamic-update-slice_fusion.11
  88.1 0.9 fusion.30
  89.0 1.2 slice_dynamic-update-slice_fusion.10
  90.2 1.0 slice_dynamic-update-slice_fusion.9
  91.2 1.3 constant_dynamic-update-slice_fusion.1
  92.4 1.2 slice_dynamic-update-slice_fusion.8
  93.6 0.9 slice_dynamic-update-slice_fusion.7
  94.5 0.9 fusion.29
  95.4 1.1 slice_dynamic-update-slice_fusion.6
  96.6 14.6 %all-gather.3.cloned.1.call-done = bf16[2304,256]{1,0:T(8,128)(2,1)} async-done(((bf16[288,256]{1,0:T(8,128)(2,1)}), bf16[2304,256]{1,0:T(8,128)(2,1)}) %all-gather.3.cloned.1.call-update) | async-done | bytes 1179664 | tf_op jit(solution)/shard_map/all_gather | solution.py:59
  111.1 4.4 %fusion.2 = f32[1152,256]{1,0:T(8,128)S(1)} fusion(bf16[1152,2304]{1,0:T(8,128)(2,1)} %bitcast.16, bf16[2304,256]{1,0:T(8,128)(2,1)} %all-gather.3.cloned.1.call-done, f32[256]{0:T(256)S(1)} %copy-done.11), kind=kOutput, calls=%fused_computation.8 | convolution fusion | flops 1359839232 | bytes 7668736 | tf_op jit(solution)/shard_map/dot_general | solution.py:57
  115.9 5.2 %reshape.191 = f32[18,2,32,32,8]{2,1,0,4,3:T(2,128)} reshape(f32[1152,256]{0,1:T(8,128)S(1)} %copy.33) | data formatting | bytes 2359296 | tf_op jit(solution)/shard_map/convert_element_type | solution.py:35
  121.1 10.3 %fusion.45 = (f32[18,32]{0,1:T(8,128)S(1)}, f32[18,32]{0,1:T(8,128)S(1)}) fusion(f32[18,2,32,32,8]{2,1,0,4,3:T(2,128)} %reshape.191), kind=kLoop, calls=%fused_computation.143 | loop fusion | flops 883584 | bytes 1184256 | tf_op jit(solution)/shard_map/reduce_sum | solution.py:38
  131.4 23.5 %all-reduce.3 = (f32[18,32]{0,1:T(8,128)S(1)}, f32[18,32]{0,1:T(8,128)S(1)}) all-reduce(f32[18,32]{0,1:T(8,128)S(1)} %get-tuple-element.6, f32[18,32]{0,1:T(8,128)S(1)} %get-tuple-element.5), channel_id=1, replica_groups=mesh['frame'=4,'height'=8] {'height'}, use_global_device_ids=true, to_apply=%region_13.14 | all-reduce | flops 1152 | bytes 9216 | tf_op jit(solution)/shard_map/psum | solution.py:129
  155.6 1.3 collective-permute-start.6
  156.9 1.5 collective-permute-start.7
  159.2 1.2 collective-permute-done.7
  160.4 0.8 select_maximum_fusion
  161.2 0.9 slice_dynamic-update-slice_fusion.5
  162.2 0.9 fusion.28
  163.1 1.2 slice_dynamic-update-slice_fusion.4
  164.2 1.0 slice_dynamic-update-slice_fusion.3
  165.2 1.2 constant_dynamic-update-slice_fusion.2
  166.5 1.2 slice_dynamic-update-slice_fusion.2
  167.6 0.9 slice_dynamic-update-slice_fusion.1
  168.5 0.9 fusion.27
  169.4 1.1 slice_dynamic-update-slice_fusion
  170.6 16.0 %all-gather.5.cloned.1.call-done = bf16[2304,256]{1,0:T(8,128)(2,1)} async-done(((bf16[288,256]{1,0:T(8,128)(2,1)}), bf16[2304,256]{1,0:T(8,128)(2,1)}) %all-gather.5.cloned.1.call-update) | async-done | bytes 1179664 | tf_op jit(solution)/shard_map/all_gather | solution.py:59
  186.6 4.4 %convolution_add_fusion = f32[1152,256]{1,0:T(8,128)S(1)} fusion(bf16[1152,2304]{1,0:T(8,128)(2,1)} %bitcast.20, bf16[2304,256]{1,0:T(8,128)(2,1)} %all-gather.5.cloned.1.call-done, f32[256]{0:T(256)S(1)} %copy-done.12), kind=kOutput, calls=%fused_computation.5 | convolution fusion | flops 1359249408 | bytes 7668736 | tf_op jit(solution)/shard_map/dot_general | solution.py:57
  191.0 1.0 fusion.26
  (86 shorter events, 8.9 us)
Async XLA Ops:
  6.5 104.6 %all-gather.3.cloned.1.call-start = ((), (), s32[]{:S(2)}) async-start(), calls=%async_computation.1 | async-start | bytes 1327104 | tf_op jit(solution)/shard_map/all_gather | solution.py:59
  7.8 9.2 %collective-permute-start = (bf16[33,2,1,256]{3,2,1,0:T(2,128)(2,1)S(1)}, bf16[33,2,1,256]{3,2,1,0:T(2,128)(2,1)S(1)}, u32[]{:S(2)}, u32[]{:S(2)}) collective-permute-start(bf16[33,2,1,256]{3,2,1,0:T(2,128)(2,1)S(1)} %get-tuple-element.41), channel_id=1, source_target_pairs={{0,8},{8,16},{16,24},{1,9},{9,17},{17,25},{2,10},{10,18},{18,26},{... | collective-permute-start | bytes 101384 | tf_op jit(solution)/shard_map/ppermute | solution.py:16
  12.7 6.2 %collective-permute-start.1 = (bf16[33,2,1,256]{3,2,1,0:T(2,128)(2,1)S(1)}, bf16[33,2,1,256]{3,2,1,0:T(2,128)(2,1)S(1)}, u32[]{:S(2)}, u32[]{:S(2)}) collective-permute-start(bf16[33,2,1,256]{3,2,1,0:T(2,128)(2,1)S(1)} %get-tuple-element.42), channel_id=1, source_target_pairs={{8,0},{16,8},{24,16},{9,1},{17,9},{25,17},{10,2},{18,10},{26,18},{... | collective-permute-start | bytes 101384 | tf_op jit(solution)/shard_map/ppermute | solution.py:17
  19.3 2.7 %collective-permute-start.2 = (bf16[33,1,10,256]{3,2,1,0:T(8,128)(2,1)S(1)}, bf16[33,1,10,256]{3,2,1,0:T(8,128)(2,1)S(1)}, u32[]{:S(2)}, u32[]{:S(2)}) collective-permute-start(bf16[33,1,10,256]{3,2,1,0:T(8,128)(2,1)S(1)} %get-tuple-element.37), channel_id=1, source_target_pairs={{0,1},{1,2},{2,3},{3,4},{4,5},{5,6},{6,7},{8,9},{9,10},{10,11},{11... | collective-permute-start | bytes 506888 | tf_op jit(solution)/shard_map/ppermute | solution.py:16
  20.6 5.2 %collective-permute-start.3 = (bf16[33,1,10,256]{3,2,1,0:T(8,128)(2,1)S(1)}, bf16[33,1,10,256]{3,2,1,0:T(8,128)(2,1)S(1)}, u32[]{:S(2)}, u32[]{:S(2)}) collective-permute-start(bf16[33,1,10,256]{3,2,1,0:T(8,128)(2,1)S(1)} %get-tuple-element.38), channel_id=1, source_target_pairs={{1,0},{2,1},{3,2},{4,3},{5,4},{6,5},{7,6},{9,8},{10,9},{11,10},{12... | collective-permute-start | bytes 506888 | tf_op jit(solution)/shard_map/ppermute | solution.py:17
  21.9 5.0 %copy-start = (bf16[33,2,8,256]{3,2,1,0:T(8,128)(2,1)S(1)}, bf16[33,2,8,256]{3,2,1,0:T(8,128)(2,1)}, u32[]{:S(2)}) copy-start(bf16[33,2,8,256]{3,2,1,0:T(8,128)(2,1)} %param.12) | copy-start | bytes 811012
  28.3 2.0 %copy-start.10 = (bf16[6912,256]{1,0:T(8,128)(2,1)S(1)}, bf16[6912,256]{1,0:T(8,128)(2,1)}, u32[]{:S(2)}) copy-start(bf16[6912,256]{1,0:T(8,128)(2,1)} %param.14) | copy-start | bytes 10616836
  32.0 0.8 copy-start.9
  33.5 47.1 %copy-start.5 = (f32[256]{0:T(256)S(1)}, f32[256]{0:T(256)}, u32[]{:S(2)}) copy-start(f32[256]{0:T(256)} %param.17) | copy-start | bytes 3076
  33.5 47.1 %copy-start.6 = (f32[256]{0:T(256)S(1)}, f32[256]{0:T(256)}, u32[]{:S(2)}) copy-start(f32[256]{0:T(256)} %param.16) | copy-start | bytes 3076
  81.1 2.9 %collective-permute-start.4 = (bf16[18,1,32,256]{3,2,1,0:T(8,128)(2,1)S(1)}, bf16[18,1,32,256]{3,2,1,0:T(8,128)(2,1)S(1)}, u32[]{:S(2)}, u32[]{:S(2)}) collective-permute-start(bf16[18,1,32,256]{3,2,1,0:T(8,128)(2,1)S(1)} %get-tuple-element.35), channel_id=1, source_target_pairs={{0,1},{1,2},{2,3},{3,4},{4,5},{5,6},{6,7},{8,9},{9,10},{10,11},{11... | collective-permute-start | bytes 884744 | tf_op jit(solution)/shard_map/ppermute | solution.py:16
  82.4 4.0 %collective-permute-start.5 = (bf16[18,1,32,256]{3,2,1,0:T(8,128)(2,1)S(1)}, bf16[18,1,32,256]{3,2,1,0:T(8,128)(2,1)S(1)}, u32[]{:S(2)}, u32[]{:S(2)}) collective-permute-start(bf16[18,1,32,256]{3,2,1,0:T(8,128)(2,1)S(1)} %get-tuple-element.36), channel_id=1, source_target_pairs={{1,0},{2,1},{3,2},{4,3},{5,4},{6,5},{7,6},{9,8},{10,9},{11,10},{12... | collective-permute-start | bytes 884744 | tf_op jit(solution)/shard_map/ppermute | solution.py:17
  83.7 102.9 %all-gather.5.cloned.1.call-start = ((), (), s32[]{:S(2)}) async-start(), calls=%async_computation.2 | async-start | bytes 1327104 | tf_op jit(solution)/shard_map/all_gather | solution.py:59
  92.4 18.7 %copy-start.11 = (f32[256]{0:T(256)S(1)}, f32[256]{0:T(256)}, u32[]{:S(2)}) copy-start(f32[256]{0:T(256)} %param.19) | copy-start | bytes 3076
  121.1 34.0 %copy-start.7 = (f32[256]{0:T(256)S(1)}, f32[256]{0:T(256)}, u32[]{:S(2)}) copy-start(f32[256]{0:T(256)} %param.21) | copy-start | bytes 3076
  121.1 34.0 %copy-start.8 = (f32[256]{0:T(256)S(1)}, f32[256]{0:T(256)}, u32[]{:S(2)}) copy-start(f32[256]{0:T(256)} %param.20) | copy-start | bytes 3076
  155.0 1.9 copy-start.1
  155.1 1.8 copy-start.3
  155.6 3.6 %collective-permute-start.6 = (bf16[18,1,32,256]{3,2,1,0:T(8,128)(2,1)S(1)}, bf16[18,1,32,256]{3,2,1,0:T(8,128)(2,1)S(1)}, u32[]{:S(2)}, u32[]{:S(2)}) collective-permute-start(bf16[18,1,32,256]{3,2,1,0:T(8,128)(2,1)S(1)} %get-tuple-element.33), channel_id=1, source_target_pairs={{0,1},{1,2},{2,3},{3,4},{4,5},{5,6},{6,7},{8,9},{9,10},{10,11},{11... | collective-permute-start | bytes 884744 | tf_op jit(solution)/shard_map/ppermute | solution.py:16
  156.9 3.5 %collective-permute-start.7 = (bf16[18,1,32,256]{3,2,1,0:T(8,128)(2,1)S(1)}, bf16[18,1,32,256]{3,2,1,0:T(8,128)(2,1)S(1)}, u32[]{:S(2)}, u32[]{:S(2)}) collective-permute-start(bf16[18,1,32,256]{3,2,1,0:T(8,128)(2,1)S(1)} %get-tuple-element.34), channel_id=1, source_target_pairs={{1,0},{2,1},{3,2},{4,3},{5,4},{6,5},{7,6},{9,8},{10,9},{11,10},{12... | collective-permute-start | bytes 884744 | tf_op jit(solution)/shard_map/ppermute | solution.py:17
  161.2 4.0 %copy-start.2 = (f32[18,256]{1,0:T(8,128)S(1)}, f32[18,256]{1,0:T(8,128)}, u32[]{:S(2)}) copy-start(f32[18,256]{1,0:T(8,128)} %copy-done.1) | copy-start | bytes 55300
  161.2 4.0 %copy-start.4 = (f32[18,256]{1,0:T(8,128)S(1)}, f32[18,256]{1,0:T(8,128)}, u32[]{:S(2)}) copy-start(f32[18,256]{1,0:T(8,128)} %copy-done.3) | copy-start | bytes 55300
  166.5 20.1 %copy-start.12 = (f32[256]{0:T(256)S(1)}, f32[256]{0:T(256)}, u32[]{:S(2)}) copy-start(f32[256]{0:T(256)} %param.23) | copy-start | bytes 3076
Sparse Core Ops, SparseCore 0:
  83.8 27.2 all-gather.2
  158.6 27.9 all-gather.4
where the time goes:
time: 199 us
  blocking collectives  69.6 us (35%)
  waiting for transfers between devices  40 us (20%)
  other arithmetic  27.3 us (14%)
  local copies, waits for them, and re-layouts  22.3 us (11%)
  starting transfers between devices  14.5 us (7%)
  between operations  13.9 us (7%)
  matrix products  11.2 us (6%)
    psum x2, blocking collectives, totals(): return lax.psum((part_sum, part_sq), 'height')  50.4 us
    all_gather x2, waiting for transfers between devices, convolve(): lax.all_gather(weight_shard, 'height', axis=0, tiled=True)  30.6 us
    all_to_all x1, blocking collectives, per_device(): lax.all_to_all(retained, 'frame', split_axis=0, concat_axis=2, tiled=True)  19.2 us
    unnamed x49, local copies, waits for them, and re-layouts  12.9 us
    reduce_sum x3, other arithmetic, group_act(): part_sum = jnp.sum(grouped, axis=(1, 2, 4))  10.5 us
    ppermute x4, waiting for transfers between devices, with_halo(): after = lax.ppermute(first, axis, down)  9.37 us
    ppermute x4, starting transfers between devices, with_halo(): before = lax.ppermute(last, axis, up)  8.85 us
    dot_general x2, matrix products, convolve(): jnp.dot(patches, lax.all_gather(weight_shard, 'height', axis=0, tiled=Tru...  8.78 us
  transfers between devices with their start and end apart: 10, of which 6 were waited for; matrix products, arithmetic and copies ran while one was open for 12% of the time, Pallas kernels for 0%

commit v1 on v0

v1 whole, which is shorter than its diff:
```python
import functools

import jax
import jax.numpy as jnp
from jax import lax
from jax.experimental import pallas as pl
from jax.experimental.pallas import tpu as pltpu
from jax.sharding import Mesh, PartitionSpec as P

GROUPS = 32
EPS = 1e-06
VMEM = pl.BlockSpec(memory_space=pltpu.VMEM)
SMEM = pl.BlockSpec(memory_space=pltpu.SMEM)
F32, BF16 = jnp.float32, jnp.bfloat16


def up_to(number, multiple):
    return -(-number // multiple) * multiple


def silu(values):
    half = 0.5 * values
    return half + half * jnp.tanh(half)


def with_column_taps(values):
    axis, width = values.ndim - 2, values.shape[-2]
    column = lax.broadcasted_iota(jnp.int32, values.shape, axis)
    before = jnp.where(column == 0, 0.0, pltpu.roll(values, 1, axis))
    after = jnp.where(column == width - 1, 0.0, pltpu.roll(values, width - 1, axis))
    return jnp.concatenate([before.astype(BF16), values.astype(BF16), after.astype(BF16)], axis=-1)


def frame_offset(counts_ref, owner):
    offset = jnp.int32(0)
    for index in range(counts_ref.shape[0]):
        offset = offset + jnp.where(index < owner, counts_ref[index], 0)
    return offset


def pick_body(halves, frames_each, counts_ref, video_ref, out_ref):
    frames = video_ref.shape[0]
    slots = out_ref.shape[1]
    for owner in range(counts_ref.shape[0]):
        offset = frame_offset(counts_ref, owner)
        for half in range(halves):
            for slot in range(slots):
                frame = offset + (half * frames_each + slot - 2)
                values = video_ref[jnp.clip(frame, 0, frames - 1)]
                out_ref[owner * halves + half, slot] = jnp.where(
                    frame >= 0, values, jnp.zeros_like(values)
                )


def temporal_body(halves, rows, part_ref, weight_ref, bias_ref, total_ref, taps_ref):
    peers, slots, cells, channels = part_ref.shape
    columns = cells // rows
    frames_each, all_rows, width = total_ref.shape[:3]

    def place(slot, _):
        for half in range(halves):
            for row in range(rows):
                values = jnp.concatenate(
                    [
                        part_ref[peer * halves + half, slot].astype(F32)[
                            row * columns : (row + 1) * columns
                        ]
                        for peer in range(peers // halves)
                    ],
                    axis=0,
                )
                at = half * rows + row
                taps_ref[slot, at] = with_column_taps(silu(values))

                @pl.when(slot >= 2)
                def _():
                    total_ref[slot - 2, at] = values + bias_ref[...]

        return 0

    lax.fori_loop(0, slots, place, 0)
    depth = 3 * channels
    for row_tap in range(3):
        low, high = max(0, 1 - row_tap), min(all_rows, all_rows + 1 - row_tap)
        for time_tap in range(3):
            patches = taps_ref[
                time_tap : time_tap + frames_each, low + row_tap - 1 : high + row_tap - 1
            ]
            start = (time_tap * 3 + row_tap) * depth
            product = jnp.dot(
                patches.reshape(frames_each * (high - low) * width, depth),
                weight_ref[start : start + depth],
                preferred_element_type=F32,
            )
            total_ref[:, low:high] += product.reshape(frames_each, high - low, width, channels)


def write_stats(field_ref, stats_ref):
    frames_each, rows, width, channels = field_ref.shape
    span = stats_ref.shape[0] // 3
    sums, squares = [], []
    for frame in range(frames_each):
        values = field_ref[frame].astype(F32).reshape(rows * width, channels)
        part_sum = jnp.sum(values, axis=0, keepdims=True)
        centered = values - part_sum * (1.0 / (rows * width))
        sums.append(part_sum)
        squares.append(jnp.sum(centered * centered, axis=0, keepdims=True))
    pad = [jnp.zeros((span - 2 * frames_each, channels), F32)] if span > 2 * frames_each else []
    rest = jnp.concatenate(sums + squares + pad, axis=0)
    for piece in range(3):
        rounded = rest.astype(BF16)
        stats_ref[piece * span : (piece + 1) * span] = rounded
        rest = rest - rounded.astype(F32)


def write_messages(field_ref, down_ref, up_ref, stats_ref):
    frames_each, rows, width, channels = field_ref.shape
    write_stats(field_ref, stats_ref)
    edge = frames_each * width
    down_ref[:edge] = field_ref[:, rows - 1].reshape(edge, channels)
    up_ref[:edge] = field_ref[:, 0].reshape(edge, channels)
    down_ref[edge:] = stats_ref[...]
    up_ref[edge:] = stats_ref[...]


def borders_body(
    n_pair,
    total_ref,
    above_ref,
    below_ref,
    weight_ref,
    blended_ref,
    down_ref,
    up_ref,
    stats_ref,
    taps_ref,
):
    frames_each, rows, width, channels = total_ref.shape
    slots = above_ref.shape[0]
    depth = 3 * channels

    def place(slot, _):
        taps_ref[0, slot] = with_column_taps(silu(above_ref[slot].astype(F32)))
        taps_ref[1, slot] = with_column_taps(silu(below_ref[slot].astype(F32)))
        return 0

    lax.fori_loop(0, slots, place, 0)
    for side, row, row_tap in ((0, 0, 0), (1, rows - 1, 2)):
        summed = total_ref[:, row].reshape(frames_each * width, channels)
        for time_tap in range(3):
            patches = taps_ref[side, time_tap : time_tap + frames_each]
            start = (time_tap * 3 + row_tap) * depth
            summed = summed + jnp.dot(
                patches.reshape(frames_each * width, depth),
                weight_ref[start : start + depth],
                preferred_element_type=F32,
            )
        blended_ref[:, row] = summed.reshape(frames_each, width, channels).astype(BF16)
    blended_ref[:, 1 : rows - 1] = total_ref[:, 1 : rows - 1].astype(BF16)
    write_messages(blended_ref, down_ref, up_ref, stats_ref)


def group_total(values, width_group):
    lane = lax.broadcasted_iota(jnp.int32, values.shape, 1)
    size, step = values.shape[1], 1
    while step < width_group:
        upper = (lane // step) % 2 == 1
        values = values + jnp.where(
            upper, pltpu.roll(values, step, 1), pltpu.roll(values, size - step, 1)
        )
        step *= 2
    return values


def scale_and_offset(frames_each, cells, stats, gain_ref, shift_ref):
    channels = stats[0].shape[1]
    width_group = channels // GROUPS
    span = stats[0].shape[0] // 3
    parts = []
    for packed in stats:
        pieces = [packed[i * span : (i + 1) * span].astype(F32) for i in range(3)]
        parts.append(pieces[0] + (pieces[1] + pieces[2]))
    sums = [part[:frames_each] for part in parts]
    squares = [part[frames_each : 2 * frames_each] for part in parts]
    sample = float(cells * len(parts) * width_group)
    mean = group_total(functools.reduce(jnp.add, sums), width_group) * (1.0 / sample)
    spread = functools.reduce(jnp.add, squares)
    for part_sum in sums:
        apart = part_sum * (1.0 / cells) - mean
        spread = spread + float(cells) * apart * apart
    variance = group_total(spread, width_group) * (1.0 / sample)
    scale = lax.rsqrt(variance + EPS) * gain_ref[...]
    return scale, shift_ref[...] - mean * scale


def normed_taps(
    n_pair, index_ref, field_ref, above_ref, below_ref, stats, gain_ref, shift_ref, taps_ref,
    scale_ref, offset_ref,
):
    frames_each, rows, width, channels = field_ref.shape
    scale, offset = scale_and_offset(frames_each, rows * width, stats, gain_ref, shift_ref)
    for frame in range(frames_each):
        scale_ref[frame] = scale[frame : frame + 1]
        offset_ref[frame] = offset[frame : frame + 1]
    pair = index_ref[0]
    top = jnp.where(pair > 0, 1.0, 0.0)
    bottom = jnp.where(pair < n_pair - 1, 1.0, 0.0)

    def place(frame, _):
        scale_row, offset_row = scale_ref[frame], offset_ref[frame]
        for row in range(rows):
            values = field_ref[frame, row].astype(F32) * scale_row + offset_row
            taps_ref[frame, row + 1] = with_column_taps(silu(values))
        edge = pl.ds(pl.multiple_of(frame * width, width), width)
        values = silu(above_ref[edge].astype(F32) * scale_row + offset_row) * top
        taps_ref[frame, 0] = with_column_taps(values)
        values = silu(below_ref[edge].astype(F32) * scale_row + offset_row) * bottom
        taps_ref[frame, rows + 1] = with_column_taps(values)
        return 0

    lax.fori_loop(0, frames_each, place, 0)


def gather_weight(n_pair, which, index_ref, same_ref, other_ref, weight_ref):
    depth = weight_ref.shape[0] // (2 * n_pair)
    if same_ref.shape[0] != n_pair:
        weight_ref[...] = same_ref[which]
        return
    pair, core = index_ref[0], index_ref[1]
    for step in range(n_pair):
        source = lax.rem(pair - step + n_pair, n_pair)
        for parts_ref, of_core in ((same_ref, core), (other_ref, 1 - core)):
            shard = source * 2 + of_core
            rows = pl.ds(pl.multiple_of(shard * depth, depth), depth)
            weight_ref[rows] = parts_ref[step, which * depth : (which + 1) * depth]


def convolved(rows, row, taps_ref, weight_ref):
    frames_each, _, width, depth = taps_ref.shape
    summed = None
    for row_tap in range(3):
        patches = taps_ref[:, row + row_tap : row + row_tap + rows]
        product = jnp.dot(
            patches.reshape(frames_each * rows * width, depth),
            weight_ref[row_tap * depth : (row_tap + 1) * depth],
            preferred_element_type=F32,
        )
        summed = product if summed is None else summed + product
    return summed


def first_body(
    n_pair,
    n_others,
    index_ref,
    blended_ref,
    from_above_ref,
    from_below_ref,
    own_ref,
    *refs,
):
    others, refs = refs[:n_others], refs[n_others:]
    (
        same_ref, other_ref, gain_ref, shift_ref, bias_ref,
        out_ref, down_ref, up_ref, stats_ref,
        taps_ref, weight_ref, scale_ref, offset_ref,
    ) = refs
    frames_each, rows, width, channels = blended_ref.shape
    edge = frames_each * width
    stats = [own_ref[...], from_above_ref[edge:]]
    if n_pair > 2:
        stats.append(from_below_ref[edge:])
    stats = stats + [ref[...] for ref in others]
    normed_taps(
        n_pair, index_ref, blended_ref, from_above_ref, from_below_ref, stats,
        gain_ref, shift_ref, taps_ref, scale_ref, offset_ref,
    )
    gather_weight(n_pair, 0, index_ref, same_ref, other_ref, weight_ref)
    summed = convolved(rows, 0, taps_ref, weight_ref) + bias_ref[...]
    out_ref[...] = summed.astype(BF16).reshape(frames_each, rows, width, channels)
    write_messages(out_ref, down_ref, up_ref, stats_ref)


def second_body(
    n_pair,
    n_others,
    index_ref,
    field_ref,
    from_above_ref,
    from_below_ref,
    own_ref,
    *refs,
):
    others, refs = refs[:n_others], refs[n_others:]
    (
        same_ref, other_ref, gain_ref, shift_ref, bias_ref, blended_ref,
        kept_ref, sent_ref,
        taps_ref, weight_ref, scale_ref, offset_ref, whole_ref,
    ) = refs
    frames_each, rows, width, channels = field_ref.shape
    edge = frames_each * width
    stats = [own_ref[...], from_above_ref[edge:]]
    if n_pair > 2:
        stats.append(from_below_ref[edge:])
    stats = stats + [ref[...] for ref in others]
    normed_taps(
        n_pair, index_ref, field_ref, from_above_ref, from_below_ref, stats,
        gain_ref, shift_ref, taps_ref, scale_ref, offset_ref,
    )
    gather_weight(n_pair, 1, index_ref, same_ref, other_ref, weight_ref)
    core, count = index_ref[1], index_ref[2]
    summed = convolved(rows, 0, taps_ref, weight_ref) + bias_ref[...]
    summed = summed.reshape(frames_each, rows, width, channels) + blended_ref[...].astype(F32)
    half = rows // 2
    for frame in range(frames_each):
        live = core * frames_each + frame < count
        whole_ref[frame] = jnp.where(live, summed[frame], 0.0).astype(BF16)
    kept_ref[...] = whole_ref[:, pl.ds(core * half, half)]
    sent_ref[...] = whole_ref[:, pl.ds((1 - core) * half, half)]


def per_device(
    video,
    frame_counts,
    temporal_weight,
    temporal_bias,
    first_gain,
    first_shift,
    first_weight,
    first_bias,
    second_gain,
    second_shift,
    second_weight,
    second_bias,
):
    frames, rows, columns, channels = video.shape
    n_frame, n_pair = lax.axis_size("frame"), lax.axis_size("pair")
    width = columns * n_frame
    capacity = min(2 * ((frames + n_frame - 1) // n_frame), frames - n_frame + 1)
    frames_each = up_to(capacity, 2) // 2
    slots = frames_each + 2
    all_rows = 2 * rows
    edge = frames_each * width
    span = up_to(2 * frames_each, 16)
    params = pltpu.CompilerParams(vmem_limit_bytes=48 * 1024 * 1024)

    def ring(step):
        return [(i, (i + step) % n_pair) for i in range(n_pair)]

    def line(step):
        return [(i, i + step) for i in range(n_pair) if 0 <= i + step < n_pair]

    def struct(shape, dtype=BF16):
        return jax.ShapeDtypeStruct(shape, dtype)

    def row_of(vector):
        return vector.reshape(1, channels)

    pair, core = lax.axis_index("pair"), lax.axis_index("core")
    owner = lax.axis_index("frame")
    my_count = lax.dynamic_index_in_dim(frame_counts, owner, keepdims=False)
    index = jnp.stack([pair, core, my_count]).astype(jnp.int32)

    picked = pl.pallas_call(
        functools.partial(pick_body, 2, frames_each),
        out_shape=struct((n_frame * 2, slots, rows * columns, channels)),
        in_specs=[SMEM, VMEM],
        out_specs=VMEM,
        compiler_params=params,
        name="pick",
    )(frame_counts, video.reshape(frames, rows * columns, channels))
    parts = lax.all_to_all(picked, ("frame", "core"), split_axis=0, concat_axis=0)

    if first_weight.shape[0] % 16 == 0 and n_pair > 2:
        own_weights = jnp.concatenate([first_weight, second_weight], axis=0)
        same = jnp.stack(
            [own_weights]
            + [lax.ppermute(own_weights, "pair", ring(step)) for step in range(1, n_pair)]
        )
        other = lax.ppermute(same, "core", [(0, 1), (1, 0)])
    else:
        both = (first_weight, second_weight)
        same = jnp.stack([lax.all_gather(w, ("pair", "core"), tiled=True) for w in both])
        other = jnp.zeros((16, channels), BF16)

    by_place = parts.reshape(n_frame, 2, slots, rows, columns, channels)

    def edge_row(array):
        return array.transpose(1, 0, 2, 3).reshape(slots, width, channels)

    above = lax.ppermute(edge_row(by_place[:, 1, :, rows - 1]), "pair", line(1))
    below = lax.ppermute(edge_row(by_place[:, 0, :, 0]), "pair", line(-1))

    total = pl.pallas_call(
        functools.partial(temporal_body, 2, rows),
        out_shape=struct((frames_each, all_rows, width, channels), F32),
        in_specs=[VMEM] * 3,
        out_specs=VMEM,
        scratch_shapes=[pltpu.VMEM((slots, all_rows, width, 3 * channels), BF16)],
        compiler_params=params,
        name="temporal",
    )(parts, temporal_weight, row_of(temporal_bias))

    field = struct((frames_each, all_rows, width, channels))
    message = struct((edge + 3 * span, channels))
    stats_struct = struct((3 * span, channels))

    blended, down, up, stats = pl.pallas_call(
        functools.partial(borders_body, n_pair),
        out_shape=(field, message, message, stats_struct),
        in_specs=[VMEM] * 4,
        out_specs=(VMEM,) * 4,
        scratch_shapes=[pltpu.VMEM((2, slots, width, 3 * channels), BF16)],
        compiler_params=params,
        name="borders",
    )(total, above, below, temporal_weight)

    def exchange(down, up, stats):
        from_above = lax.ppermute(down, "pair", ring(1))
        from_below = lax.ppermute(up, "pair", ring(-1))
        others = [lax.ppermute(stats, "pair", ring(step)) for step in range(2, n_pair - 1)]
        return from_above, from_below, others

    def scratch():
        return [
            pltpu.VMEM((frames_each, all_rows + 2, width, 3 * channels), BF16),
            pltpu.VMEM((9 * channels, channels), BF16),
            pltpu.VMEM((frames_each, 1, channels), F32),
            pltpu.VMEM((frames_each, 1, channels), F32),
        ]

    from_above, from_below, others = exchange(down, up, stats)
    first_out, down, up, stats = pl.pallas_call(
        functools.partial(first_body, n_pair, len(others)),
        out_shape=(field, message, message, stats_struct),
        in_specs=[SMEM] + [VMEM] * (9 + len(others)),
        out_specs=(VMEM,) * 4,
        scratch_shapes=scratch(),
        compiler_params=params,
        name="first",
    )(
        index, blended, from_above, from_below, stats, *others, same, other,
        row_of(first_gain), row_of(first_shift), row_of(first_bias),
    )

    from_above, from_below, others = exchange(down, up, stats)
    half = struct((frames_each, rows, width, channels))
    kept, sent = pl.pallas_call(
        functools.partial(second_body, n_pair, len(others)),
        out_shape=(half, half),
        in_specs=[SMEM] + [VMEM] * (10 + len(others)),
        out_specs=(VMEM,) * 2,
        scratch_shapes=scratch() + [pltpu.VMEM(field.shape, BF16)],
        compiler_params=params,
        name="second",
    )(
        index, first_out, from_above, from_below, stats, *others, same, other,
        row_of(second_gain), row_of(second_shift), row_of(second_bias), blended,
    )
    received = lax.ppermute(sent, "core", [(0, 1), (1, 0)])
    early = jnp.where(core == 0, kept, received)
    late = jnp.where(core == 0, received, kept)
    return jnp.concatenate([early, late], axis=0)[:capacity]


def solution(mesh):
    n_frame, n_height = mesh.devices.shape
    split = Mesh(mesh.devices.reshape(n_frame, n_height // 2, 2), ("frame", "pair", "core"))
    height = ("pair", "core")
    placed = (
        P(None, height, "frame", None),
        P(),
        P(),
        P(),
        P(),
        P(),
        P(height, None),
        P(),
        P(),
        P(),
        P(height, None),
        P(),
    )
    return jax.shard_map(
        per_device,
        mesh=split,
        in_specs=placed,
        out_specs=P("frame", height, None, None),
        check_vma=False,
    )
```

time: 199 us -> 80.9 us (0.41)
  blocking collectives: 69.6 us -> 0 us
  other arithmetic: 27.3 us -> 2.85 us
  Pallas kernels: 0 us -> 18.9 us
  local copies, waits for them, and re-layouts: 22.3 us -> 6.69 us
  between operations: 13.9 us -> 0.2 us
  matrix products: 11.2 us -> 0 us
  waiting for transfers between devices: 40 us -> 29.5 us
  starting transfers between devices: 14.5 us -> 22.3 us
    psum x2 -> x0, blocking collectives: 50.4 us -> none  [totals(): return lax.psum((part_sum, part_sq), 'height')]
    all_gather x2 -> x0, waiting for transfers between devices: 30.6 us -> none  [convolve(): lax.all_gather(weight_shard, 'height', axis=0, tiled=True)]
    ppermute x8 -> x13, waiting for transfers between devices: 9.38 us -> 29 us  [the longest x3 14.4 us: per_device(): lax.ppermute(own_weights, 'pair', ring(step))]
    all_to_all x1 -> x0, blocking collectives: 19.2 us -> none  [per_device(): lax.all_to_all(retained, 'frame', split_axis=0, concat_axis=2, tiled=True)]
    pallas_call x0 -> x5, Pallas kernels: none -> 18.9 us  [the longest x1 5.7 us: per_device(): pl.pallas_call(functools.partial(temporal_body, 2, rows), out_shape=struc...]
    reduce_sum x6 -> x0, other arithmetic: 12.6 us -> none  [the longest x3 10.5 us: group_act(): part_sum = jnp.sum(grouped, axis=(1, 2, 4))]
    dot_general x5 -> x0, matrix products: 11.2 us -> none  [the longest x2 8.78 us: convolve(): jnp.dot(patches, lax.all_gather(weight_shard, 'height', axis=0, tiled=Tru...]
    unnamed x49 -> x37, local copies, waits for them, and re-layouts: 12.9 us -> 4.98 us
  transfers between devices with their start and end apart: 10 -> 14, of which waited for: 6 -> 10; matrix products, arithmetic and copies ran while one was open for 12% -> 5% of each run, Pallas kernels for 0% -> 10%
where the time goes in v1:
time: 80.9 us; the launch traced here: 80.4 us
  waiting for transfers between devices  29.5 us (36%)
  starting transfers between devices  22.3 us (28%)
  Pallas kernels  18.9 us (23%)
  local copies, waits for them, and re-layouts  6.69 us (8%)
  other arithmetic  2.85 us (4%)
    ppermute x3, waiting for transfers between devices, per_device(): lax.ppermute(own_weights, 'pair', ring(step))  14.4 us
    ppermute x2, waiting for transfers between devices, exchange(): lax.ppermute(stats, 'pair', ring(step))  7.58 us
    all_to_all x1, starting transfers between devices, per_device(): lax.all_to_all(picked, ('frame', 'core'), split_axis=0, concat_axis=0)  6.33 us
    pallas_call x1, Pallas kernels, per_device(): pl.pallas_call(functools.partial(temporal_body, 2, rows), out_shape=struc...  5.7 us
    unnamed x37, local copies, waits for them, and re-layouts  4.98 us
    pallas_call x1, Pallas kernels, per_device(): pl.pallas_call(functools.partial(first_body, n_pair, len(others)), out_sh...  4.74 us
    pallas_call x1, Pallas kernels, per_device(): pl.pallas_call(functools.partial(second_body, n_pair, len(others)), out_s...  4.64 us
    ppermute x2, starting transfers between devices, exchange(): from_below = lax.ppermute(up, 'pair', ring(-1))  3.76 us
  transfers between devices with their start and end apart: 14, of which 10 were waited for; matrix products, arithmetic and copies ran while one was open for 5% of the time, Pallas kernels for 10%

profile of v1, /device:TPU:0, one launch (start us, length us, event | category | flops | bytes accessed | tf_op | source)
XLA Modules:
  0.0 80.4 jit_solution(8519261984069705131)
XLA Ops:
  0.0 1.0 %copy-done.3 = bf16[33,2,8,256]{3,2,1,0:T(8,128)(2,1)S(1)} copy-done((bf16[33,2,8,256]{3,2,1,0:T(8,128)(2,1)S(1)}, bf16[33,2,8,256]{3,2,1,0:T(8,128)(2,1)}, u32[]{:S(2)}) %copy-start.3) | copy-done | bytes 270360
  1.0 0.7 copy-done.13
  1.6 1.6 %pick.1 = bf16[8,11,16,256]{3,2,1,0:T(8,128)(2,1)} custom-call(s32[4]{0:T(128)S(1)} %copy-done.13, bf16[33,16,256]{2,1,0:T(8,128)(2,1)S(1)} %bitcast.29), custom_call_target="tpu_custom_call" | custom-call | tf_op jit(solution)/shard_map/pick/pallas_call | solution.py:364
  3.2 6.3 %all-to-all-start = ((bf16[8,11,16,256]{3,2,1,0:T(8,128)(2,1)}), bf16[8,11,16,256]{3,2,1,0:T(8,128)(2,1)}, u32[]{:S(2)}, u32[]{:S(2)}) async-start(bf16[8,11,16,256]{3,2,1,0:T(8,128)(2,1)} %pick.1), calls=%async_computation | async-start | bytes 1441792 | tf_op jit(solution)/shard_map/all_to_all | solution.py:372
  9.6 2.5 %collective-permute-start.7 = (bf16[576,256]{1,0:T(8,128)(2,1)S(1)}, bf16[576,256]{1,0:T(8,128)(2,1)S(1)}, u32[]{:S(2)}, u32[]{:S(2)}) collective-permute-start(bf16[576,256]{1,0:T(8,128)(2,1)S(1)} %constant_dynamic-update-slice_fusion), channel_id=1, source_target_pairs={{0,6},{2,0},{4,2},{6,4},{1,7},{3,1},{5,3},{7,5},{8,14},{10,8},{12,... | collective-permute-start | bytes 884744 | tf_op jit(solution)/shard_map/ppermute | solution.py:378
  12.1 0.5 collective-permute-start.6
  12.6 0.6 collective-permute-start.5
  13.2 6.3 %collective-permute-done.7 = bf16[576,256]{1,0:T(8,128)(2,1)S(1)} collective-permute-done((bf16[576,256]{1,0:T(8,128)(2,1)S(1)}, bf16[576,256]{1,0:T(8,128)(2,1)S(1)}, u32[]{:S(2)}, u32[]{:S(2)}) %collective-permute-start.7) | collective-permute-done | bytes 294944 | tf_op jit(solution)/shard_map/ppermute | solution.py:378
  19.4 8.1 %collective-permute-done.6 = bf16[576,256]{1,0:T(8,128)(2,1)S(1)} collective-permute-done((bf16[576,256]{1,0:T(8,128)(2,1)S(1)}, bf16[576,256]{1,0:T(8,128)(2,1)S(1)}, u32[]{:S(2)}, u32[]{:S(2)}) %collective-permute-start.6) | collective-permute-done | bytes 294944 | tf_op jit(solution)/shard_map/ppermute | solution.py:378
  27.5 0.0 collective-permute-done.5
  27.5 1.2 %pad_maximum_fusion.refs_1_ = bf16[4,576,256]{2,1,0:T(8,128)(2,1)} fusion(bf16[1,576,256]{2,1,0:T(8,128)(2,1)S(1)} %bitcast.38, bf16[1,576,256]{2,1,0:T(8,128)(2,1)S(1)} %bitcast.39, bf16[1,576,256]{2,1,0:T(8,128)(2,1)S(1)} %bitcast.40, bf16[1,576,256]{2,1,0:T(8,128)(2,1)S(1)} %bitcast.37), kind=kLoop, calls=%fused_computation | loop fusion | flops 1769472 | bytes 2359296 | tf_op jit(solution)/shard_map/stack | solution.py:376
  28.7 0.0 collective-permute-start.8
  28.7 0.5 all-to-all-done.part_ref
  29.2 1.0 %fusion = (bf16[4,1,11,1,8,256]{5,4,3,2,1,0:T(8,128)(2,1)S(1)}, bf16[4,1,11,1,8,256]{5,4,3,2,1,0:T(8,128)(2,1)S(1)}) fusion(bf16[4,2,11,2,8,256]{5,4,3,2,1,0:T(8,128)(2,1)} %bitcast.4), kind=kLoop, calls=%fused_computation.9 | loop fusion | bytes 720896 | tf_op jit(solution)/shard_map/slice | solution.py:392
  30.3 3.4 %collective-permute-start = (bf16[11,32,256]{2,1,0:T(8,128)(2,1)S(1)}, bf16[11,32,256]{2,1,0:T(8,128)(2,1)S(1)}, u32[]{:S(2)}, u32[]{:S(2)}) collective-permute-start(bf16[11,32,256]{2,1,0:T(8,128)(2,1)S(1)} %bitcast.42), channel_id=1, source_target_pairs={{0,2},{2,4},{4,6},{1,3},{3,5},{5,7},{8,10},{10,12},{12,14},{9,11},... | collective-permute-start | bytes 540680 | tf_op jit(solution)/shard_map/ppermute | solution.py:391
  33.7 1.3 %collective-permute-start.1 = (bf16[11,32,256]{2,1,0:T(8,128)(2,1)S(1)}, bf16[11,32,256]{2,1,0:T(8,128)(2,1)S(1)}, u32[]{:S(2)}, u32[]{:S(2)}) collective-permute-start(bf16[11,32,256]{2,1,0:T(8,128)(2,1)S(1)} %bitcast.41), channel_id=1, source_target_pairs={{2,0},{4,2},{6,4},{3,1},{5,3},{7,5},{10,8},{12,10},{14,12},{11,9},... | collective-permute-start | bytes 540680 | tf_op jit(solution)/shard_map/ppermute | solution.py:392
  35.0 5.7 %temporal.1.total_ref = f32[9,4,32,256]{3,2,1,0:T(8,128)S(1)} custom-call(bf16[8,11,16,256]{3,2,1,0:T(8,128)(2,1)} %all-to-all-done.part_ref, bf16[6912,256]{1,0:T(8,128)(2,1)S(1)} %copy-done, f32[1,256]{1,0:T(1,128)S(1)} %bitcast.30), custom_call_target="tpu_custom_call" | custom-call | tf_op jit(solution)/shard_map/temporal/pallas_call | solution.py:394
  40.7 0.0 copy-start.14
  40.7 0.0 copy-start.7
  40.7 0.0 copy-start.8
  40.8 0.0 copy-start.9
  40.8 0.0 collective-permute-done.above_ref
  40.8 2.3 %collective-permute-done.1.below_ref = bf16[11,32,256]{2,1,0:T(8,128)(2,1)S(1)} collective-permute-done((bf16[11,32,256]{2,1,0:T(8,128)(2,1)S(1)}, bf16[11,32,256]{2,1,0:T(8,128)(2,1)S(1)}, u32[]{:S(2)}, u32[]{:S(2)}) %collective-permute-start.1) | collective-permute-done | bytes 180256 | tf_op jit(solution)/shard_map/ppermute | solution.py:392
  43.1 2.2 %borders.1 = (bf16[9,4,32,256]{3,2,1,0:T(8,128)(2,1)S(1)}, bf16[384,256]{1,0:T(8,128)(2,1)}, bf16[384,256]{1,0:T(8,128)(2,1)}, bf16[96,256]{1,0:T(8,128)(2,1)S(1)}) custom-call(f32[9,4,32,256]{3,2,1,0:T(8,128)S(1)} %temporal.1.total_ref, bf16[11,32,256]{2,1,0:T(8,128)(2,1)S(1)} %collective-permute-done.above_ref, ...), custom_call_target="tpu_custom_call" | custom-call | tf_op jit(solution)/shard_map/borders/pallas_call | solution.py:408
  45.3 0.8 %copy-done.1 = bf16[9,4,32,256]{3,2,1,0:T(8,128)(2,1)} copy-done((bf16[9,4,32,256]{3,2,1,0:T(8,128)(2,1)}, bf16[9,4,32,256]{3,2,1,0:T(8,128)(2,1)S(1)}, u32[]{:S(2)}) %copy-start.1) | copy-done | bytes 589848
  46.1 0.6 copy-done.4
  46.7 1.5 %collective-permute-start.2 = (bf16[384,256]{1,0:T(8,128)(2,1)}, bf16[384,256]{1,0:T(8,128)(2,1)S(1)}, u32[]{:S(2)}, u32[]{:S(2)}) collective-permute-start(bf16[384,256]{1,0:T(8,128)(2,1)} %get-tuple-element.16), channel_id=1, source_target_pairs={{0,2},{2,4},{4,6},{6,0},{1,3},{3,5},{5,7},{7,1},{8,10},{10,12},{12... | collective-permute-start | bytes 589832 | tf_op jit(solution)/shard_map/ppermute | solution.py:419
  48.2 1.4 %collective-permute-start.3 = (bf16[384,256]{1,0:T(8,128)(2,1)}, bf16[384,256]{1,0:T(8,128)(2,1)S(1)}, u32[]{:S(2)}, u32[]{:S(2)}) collective-permute-start(bf16[384,256]{1,0:T(8,128)(2,1)} %get-tuple-element.17), channel_id=1, source_target_pairs={{0,6},{2,0},{4,2},{6,4},{1,7},{3,1},{5,3},{7,5},{8,14},{10,8},{12,... | collective-permute-start | bytes 589832 | tf_op jit(solution)/shard_map/ppermute | solution.py:420
  49.6 0.7 dynamic_slice.4
  50.3 1.3 %collective-permute-start.4 = (bf16[96,256]{1,0:T(8,128)(2,1)}, bf16[96,256]{1,0:T(8,128)(2,1)S(1)}, u32[]{:S(2)}, u32[]{:S(2)}) collective-permute-start(bf16[96,256]{1,0:T(8,128)(2,1)} %copy-done.4), channel_id=1, source_target_pairs={{0,4},{2,6},{4,0},{6,2},{1,5},{3,7},{5,1},{7,3},{8,12},{10,14},{12... | collective-permute-start | bytes 147464 | tf_op jit(solution)/shard_map/ppermute | solution.py:421
  51.6 0.8 pad_add_fusion.index_ref
  52.3 0.0 collective-permute-done.8.refs_2_
  52.3 2.8 %collective-permute-done.4.refs_0_ = bf16[96,256]{1,0:T(8,128)(2,1)S(1)} collective-permute-done((bf16[96,256]{1,0:T(8,128)(2,1)}, bf16[96,256]{1,0:T(8,128)(2,1)S(1)}, u32[]{:S(2)}, u32[]{:S(2)}) %collective-permute-start.4) | collective-permute-done | bytes 49184 | tf_op jit(solution)/shard_map/ppermute | solution.py:421
  55.1 0.3 collective-permute-done.2.from_above_ref
  55.5 2.3 %collective-permute-done.3.from_below_ref = bf16[384,256]{1,0:T(8,128)(2,1)S(1)} collective-permute-done((bf16[384,256]{1,0:T(8,128)(2,1)}, bf16[384,256]{1,0:T(8,128)(2,1)S(1)}, u32[]{:S(2)}, u32[]{:S(2)}) %collective-permute-start.3) | collective-permute-done | bytes 196640 | tf_op jit(solution)/shard_map/ppermute | solution.py:420
  57.7 0.0 copy-start.2
  57.8 1.1 %copy-done.2 = bf16[9,4,32,256]{3,2,1,0:T(8,128)(2,1)S(1)} copy-done((bf16[9,4,32,256]{3,2,1,0:T(8,128)(2,1)S(1)}, bf16[9,4,32,256]{3,2,1,0:T(8,128)(2,1)}, u32[]{:S(2)}) %copy-start.2) | copy-done | bytes 589848
  58.8 0.8 copy-done.5
  59.6 4.7 %first.1 = (bf16[9,4,32,256]{3,2,1,0:T(8,128)(2,1)S(1)}, bf16[384,256]{1,0:T(8,128)(2,1)S(1)}, bf16[384,256]{1,0:T(8,128)(2,1)S(1)}, bf16[96,256]{1,0:T(8,128)(2,1)S(1)}) custom-call(s32[3]{0:T(128)S(1)} %pad_add_fusion.index_ref, bf16[9,4,32,256]{3,2,1,0:T(8,128)(2,1)S(1)} %copy-done.2, bf16[384,256]{1,0:T(8,128)(2,1)S(1)} %collective-permute-done.2.from_above_ref, ...), custom_call_target="tpu_custom_call" | custom-call | tf_op jit(solution)/shard_map/first/pallas_call | solution.py:433
  64.4 0.7 collective-permute-start.9
  65.0 2.3 %collective-permute-start.10 = (bf16[384,256]{1,0:T(8,128)(2,1)S(1)}, bf16[384,256]{1,0:T(8,128)(2,1)S(1)}, u32[]{:S(2)}, u32[]{:S(2)}) collective-permute-start(bf16[384,256]{1,0:T(8,128)(2,1)S(1)} %get-tuple-element.21), channel_id=1, source_target_pairs={{0,6},{2,0},{4,2},{6,4},{1,7},{3,1},{5,3},{7,5},{8,14},{10,8},{12,... | collective-permute-start | bytes 589832 | tf_op jit(solution)/shard_map/ppermute | solution.py:420
  67.3 0.4 collective-permute-start.11
  67.8 4.8 %collective-permute-done.11.refs_0_ = bf16[96,256]{1,0:T(8,128)(2,1)S(1)} collective-permute-done((bf16[96,256]{1,0:T(8,128)(2,1)S(1)}, bf16[96,256]{1,0:T(8,128)(2,1)S(1)}, u32[]{:S(2)}, u32[]{:S(2)}) %collective-permute-start.11) | collective-permute-done | bytes 49184 | tf_op jit(solution)/shard_map/ppermute | solution.py:421
  72.6 0.6 collective-permute-done.10.from_below_ref
  73.2 4.6 %second.1 = (bf16[9,2,32,256]{3,2,1,0:T(8,128)(2,1)S(1)}, bf16[9,2,32,256]{3,2,1,0:T(8,128)(2,1)S(1)}) custom-call(s32[3]{0:T(128)S(1)} %pad_add_fusion.index_ref, bf16[9,4,32,256]{3,2,1,0:T(8,128)(2,1)S(1)} %get-tuple-element.19.field_ref, bf16[384,256]{1,0:T(8,128)(2,1)S(1)} %collective-permute-done.9.from_above_ref, ...), custom_call_target="tpu_custom_call" | custom-call | tf_op jit(solution)/shard_map/second/pallas_call | solution.py:448
  77.8 0.1 collective-permute-start.12
  77.9 1.6 %collective-permute-done.12 = bf16[9,2,32,256]{3,2,1,0:T(8,128)(2,1)S(1)} collective-permute-done((bf16[9,2,32,256]{3,2,1,0:T(8,128)(2,1)S(1)}, bf16[9,2,32,256]{3,2,1,0:T(8,128)(2,1)S(1)}, u32[]{:S(2)}, u32[]{:S(2)}) %collective-permute-start.12) | collective-permute-done | bytes 294944 | tf_op jit(solution)/shard_map/ppermute | solution.py:460
  79.5 0.9 %pad_maximum_fusion.1 = bf16[18,2,32,256]{3,2,1,0:T(8,128)(2,1)} fusion(bf16[9,2,32,256]{3,2,1,0:T(8,128)(2,1)S(1)} %get-tuple-element.28, bf16[9,2,32,256]{3,2,1,0:T(8,128)(2,1)S(1)} %get-tuple-element.27), kind=kLoop, calls=%fused_computation.1 | loop fusion | flops 294912 | bytes 1179648 | tf_op jit(solution)/shard_map/concatenate | solution.py:463
  (29 shorter events, 0.1 us)
Async XLA Ops:
  0.0 1.0 %copy-start.3 = (bf16[33,2,8,256]{3,2,1,0:T(8,128)(2,1)S(1)}, bf16[33,2,8,256]{3,2,1,0:T(8,128)(2,1)}, u32[]{:S(2)}) copy-start(bf16[33,2,8,256]{3,2,1,0:T(8,128)(2,1)} %param.12) | copy-start | bytes 811012
  1.0 0.7 copy-start.13
  1.6 7.9 %copy-start.15 = (bf16[288,256]{1,0:T(8,128)(2,1)S(1)}, bf16[288,256]{1,0:T(8,128)(2,1)}, u32[]{:S(2)}) copy-start(bf16[288,256]{1,0:T(8,128)(2,1)} %param.18) | copy-start | bytes 442372
  1.6 7.9 %copy-start.16 = (bf16[288,256]{1,0:T(8,128)(2,1)S(1)}, bf16[288,256]{1,0:T(8,128)(2,1)}, u32[]{:S(2)}) copy-start(bf16[288,256]{1,0:T(8,128)(2,1)} %param.22) | copy-start | bytes 442372
  3.2 26.0 %all-to-all-start = ((bf16[8,11,16,256]{3,2,1,0:T(8,128)(2,1)}), bf16[8,11,16,256]{3,2,1,0:T(8,128)(2,1)}, u32[]{:S(2)}, u32[]{:S(2)}) async-start(bf16[8,11,16,256]{3,2,1,0:T(8,128)(2,1)} %pick.1), calls=%async_computation | async-start | bytes 1441792 | tf_op jit(solution)/shard_map/all_to_all | solution.py:372
  9.6 9.9 %collective-permute-start.7 = (bf16[576,256]{1,0:T(8,128)(2,1)S(1)}, bf16[576,256]{1,0:T(8,128)(2,1)S(1)}, u32[]{:S(2)}, u32[]{:S(2)}) collective-permute-start(bf16[576,256]{1,0:T(8,128)(2,1)S(1)} %constant_dynamic-update-slice_fusion), channel_id=1, source_target_pairs={{0,6},{2,0},{4,2},{6,4},{1,7},{3,1},{5,3},{7,5},{8,14},{10,8},{12,... | collective-permute-start | bytes 884744 | tf_op jit(solution)/shard_map/ppermute | solution.py:378
  12.1 15.5 %collective-permute-start.6 = (bf16[576,256]{1,0:T(8,128)(2,1)S(1)}, bf16[576,256]{1,0:T(8,128)(2,1)S(1)}, u32[]{:S(2)}, u32[]{:S(2)}) collective-permute-start(bf16[576,256]{1,0:T(8,128)(2,1)S(1)} %constant_dynamic-update-slice_fusion), channel_id=1, source_target_pairs={{0,4},{2,6},{4,0},{6,2},{1,5},{3,7},{5,1},{7,3},{8,12},{10,14},{12... | collective-permute-start | bytes 884744 | tf_op jit(solution)/shard_map/ppermute | solution.py:378
  12.6 14.9 %collective-permute-start.5 = (bf16[576,256]{1,0:T(8,128)(2,1)S(1)}, bf16[576,256]{1,0:T(8,128)(2,1)S(1)}, u32[]{:S(2)}, u32[]{:S(2)}) collective-permute-start(bf16[576,256]{1,0:T(8,128)(2,1)S(1)} %constant_dynamic-update-slice_fusion), channel_id=1, source_target_pairs={{0,2},{2,4},{4,6},{6,0},{1,3},{3,5},{5,7},{7,1},{8,10},{10,12},{12... | collective-permute-start | bytes 884744 | tf_op jit(solution)/shard_map/ppermute | solution.py:378
  27.5 7.5 %copy-start = (bf16[6912,256]{1,0:T(8,128)(2,1)S(1)}, bf16[6912,256]{1,0:T(8,128)(2,1)}, u32[]{:S(2)}) copy-start(bf16[6912,256]{1,0:T(8,128)(2,1)} %weight_ref.3) | copy-start | bytes 10616836
  28.7 6.3 %copy-start.6 = (f32[256]{0:T(256)S(1)}, f32[256]{0:T(256)}, u32[]{:S(2)}) copy-start(f32[256]{0:T(256)} %param.15) | copy-start | bytes 3076
  28.7 23.6 %collective-permute-start.8 = (bf16[4,576,256]{2,1,0:T(8,128)(2,1)}, bf16[4,576,256]{2,1,0:T(8,128)(2,1)}, u32[]{:S(2)}, u32[]{:S(2)}) collective-permute-start(bf16[4,576,256]{2,1,0:T(8,128)(2,1)} %pad_maximum_fusion.refs_1_), channel_id=1, source_target_pairs={{0,1},{1,0},{2,3},{3,2},{4,5},{5,4},{6,7},{7,6},{8,9},{9,8},{10,11... | collective-permute-start | bytes 3538952 | tf_op jit(solution)/shard_map/ppermute | solution.py:380
  30.3 10.5 %collective-permute-start = (bf16[11,32,256]{2,1,0:T(8,128)(2,1)S(1)}, bf16[11,32,256]{2,1,0:T(8,128)(2,1)S(1)}, u32[]{:S(2)}, u32[]{:S(2)}) collective-permute-start(bf16[11,32,256]{2,1,0:T(8,128)(2,1)S(1)} %bitcast.42), channel_id=1, source_target_pairs={{0,2},{2,4},{4,6},{1,3},{3,5},{5,7},{8,10},{10,12},{12,14},{9,11},... | collective-permute-start | bytes 540680 | tf_op jit(solution)/shard_map/ppermute | solution.py:391
  33.7 9.4 %collective-permute-start.1 = (bf16[11,32,256]{2,1,0:T(8,128)(2,1)S(1)}, bf16[11,32,256]{2,1,0:T(8,128)(2,1)S(1)}, u32[]{:S(2)}, u32[]{:S(2)}) collective-permute-start(bf16[11,32,256]{2,1,0:T(8,128)(2,1)S(1)} %bitcast.41), channel_id=1, source_target_pairs={{2,0},{4,2},{6,4},{3,1},{5,3},{7,5},{10,8},{12,10},{14,12},{11,9},... | collective-permute-start | bytes 540680 | tf_op jit(solution)/shard_map/ppermute | solution.py:392
  40.7 8.9 %copy-start.14 = (s32[4]{0:T(128)S(1)}, s32[4]{0:T(128)}, u32[]{:S(2)}) copy-start(s32[4]{0:T(128)} %counts_ref.1) | copy-start | bytes 52
  40.7 17.0 %copy-start.7 = (f32[256]{0:T(256)S(1)}, f32[256]{0:T(256)}, u32[]{:S(2)}) copy-start(f32[256]{0:T(256)} %param.16) | copy-start | bytes 3076
  40.7 17.0 %copy-start.8 = (f32[256]{0:T(256)S(1)}, f32[256]{0:T(256)}, u32[]{:S(2)}) copy-start(f32[256]{0:T(256)} %param.17) | copy-start | bytes 3076
  40.8 17.0 %copy-start.9 = (f32[256]{0:T(256)S(1)}, f32[256]{0:T(256)}, u32[]{:S(2)}) copy-start(f32[256]{0:T(256)} %param.19) | copy-start | bytes 3076
  45.3 0.8 %copy-start.1 = (bf16[9,4,32,256]{3,2,1,0:T(8,128)(2,1)}, bf16[9,4,32,256]{3,2,1,0:T(8,128)(2,1)S(1)}, u32[]{:S(2)}) copy-start(bf16[9,4,32,256]{3,2,1,0:T(8,128)(2,1)S(1)} %get-tuple-element.15.blended_ref.refs_6_) | copy-start | bytes 1769476
  46.1 0.6 copy-start.4
  46.7 8.8 %collective-permute-start.2 = (bf16[384,256]{1,0:T(8,128)(2,1)}, bf16[384,256]{1,0:T(8,128)(2,1)S(1)}, u32[]{:S(2)}, u32[]{:S(2)}) collective-permute-start(bf16[384,256]{1,0:T(8,128)(2,1)} %get-tuple-element.16), channel_id=1, source_target_pairs={{0,2},{2,4},{4,6},{6,0},{1,3},{3,5},{5,7},{7,1},{8,10},{10,12},{12... | collective-permute-start | bytes 589832 | tf_op jit(solution)/shard_map/ppermute | solution.py:419
  48.2 9.5 %collective-permute-start.3 = (bf16[384,256]{1,0:T(8,128)(2,1)}, bf16[384,256]{1,0:T(8,128)(2,1)S(1)}, u32[]{:S(2)}, u32[]{:S(2)}) collective-permute-start(bf16[384,256]{1,0:T(8,128)(2,1)} %get-tuple-element.17), channel_id=1, source_target_pairs={{0,6},{2,0},{4,2},{6,4},{1,7},{3,1},{5,3},{7,5},{8,14},{10,8},{12,... | collective-permute-start | bytes 589832 | tf_op jit(solution)/shard_map/ppermute | solution.py:420
  50.3 4.8 %collective-permute-start.4 = (bf16[96,256]{1,0:T(8,128)(2,1)}, bf16[96,256]{1,0:T(8,128)(2,1)S(1)}, u32[]{:S(2)}, u32[]{:S(2)}) collective-permute-start(bf16[96,256]{1,0:T(8,128)(2,1)} %copy-done.4), channel_id=1, source_target_pairs={{0,4},{2,6},{4,0},{6,2},{1,5},{3,7},{5,1},{7,3},{8,12},{10,14},{12... | collective-permute-start | bytes 147464 | tf_op jit(solution)/shard_map/ppermute | solution.py:421
  57.7 1.1 %copy-start.2 = (bf16[9,4,32,256]{3,2,1,0:T(8,128)(2,1)S(1)}, bf16[9,4,32,256]{3,2,1,0:T(8,128)(2,1)}, u32[]{:S(2)}) copy-start(bf16[9,4,32,256]{3,2,1,0:T(8,128)(2,1)} %copy-done.1) | copy-start | bytes 1769476
  58.8 0.8 copy-start.5
  59.6 13.5 %copy-start.10 = (f32[256]{0:T(256)S(1)}, f32[256]{0:T(256)}, u32[]{:S(2)}) copy-start(f32[256]{0:T(256)} %param.20) | copy-start | bytes 3076
  59.6 13.5 %copy-start.11 = (f32[256]{0:T(256)S(1)}, f32[256]{0:T(256)}, u32[]{:S(2)}) copy-start(f32[256]{0:T(256)} %param.21) | copy-start | bytes 3076
  59.6 13.5 %copy-start.12 = (f32[256]{0:T(256)S(1)}, f32[256]{0:T(256)}, u32[]{:S(2)}) copy-start(f32[256]{0:T(256)} %param.23) | copy-start | bytes 3076
  64.4 8.2 %collective-permute-start.9 = (bf16[384,256]{1,0:T(8,128)(2,1)S(1)}, bf16[384,256]{1,0:T(8,128)(2,1)S(1)}, u32[]{:S(2)}, u32[]{:S(2)}) collective-permute-start(bf16[384,256]{1,0:T(8,128)(2,1)S(1)} %get-tuple-element.20), channel_id=1, source_target_pairs={{0,2},{2,4},{4,6},{6,0},{1,3},{3,5},{5,7},{7,1},{8,10},{10,12},{12... | collective-permute-start | bytes 589832 | tf_op jit(solution)/shard_map/ppermute | solution.py:419
  65.0 8.1 %collective-permute-start.10 = (bf16[384,256]{1,0:T(8,128)(2,1)S(1)}, bf16[384,256]{1,0:T(8,128)(2,1)S(1)}, u32[]{:S(2)}, u32[]{:S(2)}) collective-permute-start(bf16[384,256]{1,0:T(8,128)(2,1)S(1)} %get-tuple-element.21), channel_id=1, source_target_pairs={{0,6},{2,0},{4,2},{6,4},{1,7},{3,1},{5,3},{7,5},{8,14},{10,8},{12,... | collective-permute-start | bytes 589832 | tf_op jit(solution)/shard_map/ppermute | solution.py:420
  67.3 5.2 %collective-permute-start.11 = (bf16[96,256]{1,0:T(8,128)(2,1)S(1)}, bf16[96,256]{1,0:T(8,128)(2,1)S(1)}, u32[]{:S(2)}, u32[]{:S(2)}) collective-permute-start(bf16[96,256]{1,0:T(8,128)(2,1)S(1)} %get-tuple-element.22.own_ref), channel_id=1, source_target_pairs={{0,4},{2,6},{4,0},{6,2},{1,5},{3,7},{5,1},{7,3},{8,12},{10,14},{12... | collective-permute-start | bytes 147464 | tf_op jit(solution)/shard_map/ppermute | solution.py:421
  77.8 1.6 %collective-permute-start.12 = (bf16[9,2,32,256]{3,2,1,0:T(8,128)(2,1)S(1)}, bf16[9,2,32,256]{3,2,1,0:T(8,128)(2,1)S(1)}, u32[]{:S(2)}, u32[]{:S(2)}) collective-permute-start(bf16[9,2,32,256]{3,2,1,0:T(8,128)(2,1)S(1)} %get-tuple-element.24), channel_id=1, source_target_pairs={{0,1},{1,0},{2,3},{3,2},{4,5},{5,4},{6,7},{7,6},{8,9},{9,8},{10,11... | collective-permute-start | bytes 884744 | tf_op jit(solution)/shard_map/ppermute | solution.py:460

commit v2 on v1

--- a/solution.py
+++ b/solution.py
@@ -11,11 +11,16 @@
 EPS = 1e-06
 VMEM = pl.BlockSpec(memory_space=pltpu.VMEM)
 SMEM = pl.BlockSpec(memory_space=pltpu.SMEM)
+HBM = pl.BlockSpec(memory_space=pl.ANY)
 F32, BF16 = jnp.float32, jnp.bfloat16
 
 
 def up_to(number, multiple):
     return -(-number // multiple) * multiple
+
+
+def slots_of(frames, n_frame):
+    return min(2 * ((frames + n_frame - 1) // n_frame), frames - n_frame + 1)
 
 
 def silu(values):
@@ -319,7 +324,234 @@
     sent_ref[...] = whole_ref[:, pl.ds((1 - core) * half, half)]
 
 
-def per_device(
+def pick_frames_body(counts_ref, video_ref, out_ref):
+    frames = video_ref.shape[0]
+    n_owner = counts_ref.shape[0]
+    frames_sent = out_ref.shape[1]
+    n_pair = out_ref.shape[0] // (2 * n_owner)
+    each = frames_sent - 1
+    for owner in range(n_owner):
+        offset = frame_offset(counts_ref, owner)
+        for pair in range(n_pair):
+            for core in range(2):
+                for place in range(frames_sent):
+                    first = 2 * each * pair
+                    slot = first + (2 * each - 1 - place if core else place - 2)
+                    frame = offset + slot
+                    values = video_ref[jnp.clip(frame, 0, frames - 1)]
+                    if slot < 0:
+                        values = jnp.where(frame >= 0, values, jnp.zeros_like(values))
+                    out_ref[(owner * n_pair + pair) * 2 + core, place] = values
+
+
+def group_scale(values, gain_ref, shift_ref):
+    cells, channels = values.shape
+    width_group = channels // GROUPS
+    sample = 1.0 / (cells * width_group)
+    mean = group_total(jnp.sum(values, axis=0, keepdims=True), width_group) * sample
+    centered = values - mean
+    squares = jnp.sum(centered * centered, axis=0, keepdims=True)
+    variance = group_total(squares, width_group) * sample
+    scale = lax.rsqrt(variance + EPS) * gain_ref[...]
+    return scale, shift_ref[...] - mean * scale
+
+
+def frames_body(
+    counts_ref, part_ref, swapped_ref, temporal_ref, same_ref, other_ref,
+    temporal_bias_ref, first_gain_ref, first_shift_ref, first_bias_ref,
+    second_gain_ref, second_shift_ref, second_bias_ref,
+    out_ref,
+    raw_ref, taps_ref, normed_ref, total_ref, blended_ref, weights_ref, sems,
+):
+    n_height, each, rows, width, channels = out_ref.shape
+    n_pair = n_height // 2
+    n_frame = part_ref.shape[0] // n_height
+    columns = width // n_frame
+    all_rows = n_height * rows
+    depth = 3 * channels
+    cells = all_rows * width
+    pair, core = lax.axis_index("pair"), lax.axis_index("core")
+    span = same_ref.shape[2]
+    copies = []
+    for which in range(2):
+        for step in range(n_pair):
+            source = lax.rem(pair - step + n_pair, n_pair)
+            for side, (parts_ref, of_core) in enumerate(((same_ref, core), (other_ref, 1 - core))):
+                copies.append(
+                    pltpu.make_async_copy(
+                        parts_ref.at[step, which],
+                        weights_ref.at[which, source * 2 + of_core],
+                        sems.at[which, step, side],
+                    )
+                )
+    for copy in copies:
+        copy.start()
+
+    border = jnp.zeros((width, depth), BF16)
+    for place in range(each + 2):
+        taps_ref[place, 0] = border
+        taps_ref[place, all_rows + 1] = border
+    for place in range(each):
+        normed_ref[place, 0] = border
+        normed_ref[place, all_rows + 1] = border
+
+    def lay(place, load):
+        for height in range(n_height):
+            pieces = [load(peer * n_height + height).astype(F32) for peer in range(n_frame)]
+            for row in range(rows):
+                values = jnp.concatenate(
+                    [piece[row * columns : (row + 1) * columns] for piece in pieces], axis=0
+                )
+                raw_ref[place, height * rows + row] = values.astype(BF16)
+                taps_ref[place, height * rows + row + 1] = with_column_taps(silu(values))
+
+    def lay_part(place, _):
+        lay(place, lambda source: part_ref[source, place])
+        return 0
+
+    lax.fori_loop(0, each + 1, lay_part, 0)
+    lay(each + 1, lambda source: swapped_ref[source])
+
+    def convolve(source_ref, weight_of, start):
+        summed = None
+        for row_tap in range(3):
+            patches = source_ref[start, row_tap : row_tap + all_rows]
+            product = jnp.dot(
+                patches.reshape(each * cells, depth),
+                weight_of(row_tap),
+                preferred_element_type=F32,
+            )
+            summed = product if summed is None else summed + product
+        return summed.reshape(each, cells, channels)
+
+    for time_tap in range(3):
+        start = time_tap + core * (2 - 2 * time_tap)
+        product = convolve(
+            taps_ref,
+            lambda row_tap: temporal_ref[
+                (time_tap * 3 + row_tap) * depth : (time_tap * 3 + row_tap + 1) * depth
+            ],
+            pl.ds(start, each),
+        )
+        if time_tap == 0:
+            total_ref[...] = product
+        else:
+            total_ref[...] += product
+
+    def norm(place, values, gain_ref, shift_ref):
+        scale, offset = group_scale(values, gain_ref, shift_ref)
+        for row in range(all_rows):
+            line = values[row * width : (row + 1) * width] * scale + offset
+            normed_ref[place, row + 1] = with_column_taps(silu(line))
+
+    def norm_first(place, _):
+        raw = raw_ref[place + 2 - 2 * core].astype(F32).reshape(cells, channels)
+        blended = (raw + total_ref[place] + temporal_bias_ref[...]).astype(BF16)
+        blended_ref[place] = blended
+        norm(place, blended.astype(F32), first_gain_ref, first_shift_ref)
+        return 0
+
+    lax.fori_loop(0, each, norm_first, 0)
+    for copy in copies[: len(copies) // 2]:
+        copy.wait()
+
+    def weight_of(which):
+        weight = weights_ref[which].reshape(2 * n_pair * span, channels)
+        return lambda row_tap: weight[row_tap * depth : (row_tap + 1) * depth]
+
+    total_ref[...] = convolve(normed_ref, weight_of(0), slice(None))
+
+    def norm_second(place, _):
+        values = (total_ref[place] + first_bias_ref[...]).astype(BF16).astype(F32)
+        norm(place, values, second_gain_ref, second_shift_ref)
+        return 0
+
+    lax.fori_loop(0, each, norm_second, 0)
+    for copy in copies[len(copies) // 2 :]:
+        copy.wait()
+    total_ref[...] = convolve(normed_ref, weight_of(1), slice(None))
+    count = counts_ref[lax.axis_index("frame")]
+
+    def finish(place, _):
+        at = place + core * (each - 1 - 2 * place)
+        live = pair * 2 * each + core * each + at < count
+        decoded = blended_ref[place].astype(F32) + (total_ref[place] + second_bias_ref[...])
+        decoded = jnp.where(live, decoded, 0.0).astype(BF16)
+        decoded = decoded.reshape(n_height, rows, width, channels)
+        for height in range(n_height):
+            out_ref[height, at] = decoded[height]
+        return 0
+
+    lax.fori_loop(0, each, finish, 0)
+
+
+def ring(size, step):
+    return [(i, (i + step) % size) for i in range(size)]
+
+
+def whole_frames(
+    video, frame_counts, temporal_weight, temporal_bias, first_gain, first_shift, first_weight,
+    first_bias, second_gain, second_shift, second_weight, second_bias,
+):
+    frames, rows, columns, channels = video.shape
+    n_frame, n_pair = lax.axis_size("frame"), lax.axis_size("pair")
+    n_height = 2 * n_pair
+    width = columns * n_frame
+    all_rows = rows * n_height
+    capacity = slots_of(frames, n_frame)
+    each = -(-capacity // n_height)
+    params = pltpu.CompilerParams(vmem_limit_bytes=40 * 1024 * 1024)
+    swap = [(0, 1), (1, 0)]
+
+    picked = pl.pallas_call(
+        pick_frames_body,
+        out_shape=jax.ShapeDtypeStruct(
+            (n_frame * n_height, each + 1, rows * columns, channels), BF16
+        ),
+        in_specs=[SMEM, VMEM],
+        out_specs=VMEM,
+        compiler_params=params,
+        name="pick",
+    )(frame_counts, video.reshape(frames, rows * columns, channels))
+    parts = lax.all_to_all(picked, ("frame", "pair", "core"), split_axis=0, concat_axis=0)
+    swapped = lax.ppermute(parts[:, each], "core", swap)
+
+    own = jnp.stack([first_weight, second_weight])
+    same = jnp.stack(
+        [own] + [lax.ppermute(own, "pair", ring(n_pair, step)) for step in range(1, n_pair)]
+    )
+    other = lax.ppermute(same, "core", swap)
+
+    def row_of(vector):
+        return vector.reshape(1, channels)
+
+    taps = (width, 3 * channels)
+    decoded = pl.pallas_call(
+        frames_body,
+        out_shape=jax.ShapeDtypeStruct((n_height, each, rows, width, channels), BF16),
+        in_specs=[SMEM] + [VMEM] * 3 + [HBM] * 2 + [VMEM] * 7,
+        out_specs=VMEM,
+        scratch_shapes=[
+            pltpu.VMEM((each + 2, all_rows, width, channels), BF16),
+            pltpu.VMEM((each + 2, all_rows + 2) + taps, BF16),
+            pltpu.VMEM((each, all_rows + 2) + taps, BF16),
+            pltpu.VMEM((each, all_rows * width, channels), F32),
+            pltpu.VMEM((each, all_rows * width, channels), BF16),
+            pltpu.VMEM((2, n_height) + first_weight.shape, BF16),
+            pltpu.SemaphoreType.DMA((2, n_pair, 2)),
+        ],
+        compiler_params=params,
+        name="frames",
+    )(
+        frame_counts, parts, swapped, temporal_weight, same, other,
+        row_of(temporal_bias), row_of(first_gain), row_of(first_shift), row_of(first_bias),
+        row_of(second_gain), row_of(second_shift), row_of(second_bias),
+    )
+    owned = lax.all_to_all(decoded, ("pair", "core"), split_axis=0, concat_axis=0)
+    return owned.reshape((n_height * each,) + owned.shape[2:])[:capacity]
+
+
+def split_rows(
     video,
     frame_counts,
     temporal_weight,
@@ -336,13 +568,13 @@
     frames, rows, columns, channels = video.shape
     n_frame, n_pair = lax.axis_size("frame"), lax.axis_size("pair")
     width = columns * n_frame
-    capacity = min(2 * ((frames + n_frame - 1) // n_frame), frames - n_frame + 1)
+    capacity = slots_of(frames, n_frame)
     frames_each = up_to(capacity, 2) // 2
     slots = frames_each + 2
     all_rows = 2 * rows
     edge = frames_each * width
     span = up_to(2 * frames_each, 16)
-    params = pltpu.CompilerParams(vmem_limit_bytes=48 * 1024 * 1024)
+    params = pltpu.CompilerParams(vmem_limit_bytes=20 * 1024 * 1024)
 
     def ring(step):
         return [(i, (i + step) % n_pair) for i in range(n_pair)]
@@ -463,6 +695,13 @@
     return jnp.concatenate([early, late], axis=0)[:capacity]
 
 
+def per_device(video, *rest):
+    n_height = lax.axis_size("pair") * lax.axis_size("core")
+    if slots_of(video.shape[0], lax.axis_size("frame")) >= n_height:
+        return whole_frames(video, *rest)
+    return split_rows(video, *rest)
+
+
 def solution(mesh):
     n_frame, n_height = mesh.devices.shape
     split = Mesh(mesh.devices.reshape(n_frame, n_height // 2, 2), ("frame", "pair", "core"))

time: 80.9 us -> 87.3 us (1.079)
  blocking collectives: 0 us -> 15.8 us
  Pallas kernels: 18.9 us -> 29.1 us
  starting transfers between devices: 22.3 us -> 12.7 us
  waiting for transfers between devices: 29.5 us -> 24.6 us
  other arithmetic: 2.85 us -> 0.19 us
  local copies, waits for them, and re-layouts: 6.69 us -> 4.54 us
    all_to_all x0 -> x1, blocking collectives: none -> 15.8 us  [whole_frames(): lax.all_to_all(decoded, ('pair', 'core'), split_axis=0, concat_axis=0)]
    ppermute x13 -> x5, starting transfers between devices: 16 us -> 5.38 us  [the longest x3 4.76 us: whole_frames(): lax.ppermute(own, 'pair', ring(n_pair, step))]
    pallas_call x5 -> x2, Pallas kernels: 18.9 us -> 29.1 us  [the longest x1 27.4 us: whole_frames(): pl.pallas_call(frames_body, out_shape=jax.ShapeDtypeStruct((n_height, eac...]
    ppermute x13 -> x5, waiting for transfers between devices: 29 us -> 24.6 us  [the longest x3 22 us: whole_frames(): lax.ppermute(own, 'pair', ring(n_pair, step))]
    another operation x2, other arithmetic: 1.94 us -> 0.19 us  [whole_frames(): jnp.stack([own] + [lax.ppermute(own, 'pair', ring(n_pair, step)) for step...]
    unnamed x37 -> x26, local copies, waits for them, and re-layouts: 4.98 us -> 3.65 us
    all_to_all x1, starting transfers between devices: 6.33 us -> 7.3 us  [whole_frames(): lax.all_to_all(picked, ('frame', 'pair', 'core'), split_axis=0, concat_ax...]
  transfers between devices with their start and end apart: 14 -> 6, of which waited for: 10 -> 4; matrix products, arithmetic and copies ran while one was open for 5% -> 0% of each run, Pallas kernels for 10% -> 0%
where the time goes in v2:
time: 87.3 us; the launch traced here: 87 us
  Pallas kernels  29.1 us (33%)
  waiting for transfers between devices  24.6 us (28%)
  blocking collectives  15.8 us (18%)
  starting transfers between devices  12.7 us (15%)
  local copies, waits for them, and re-layouts  4.54 us (5%)
    pallas_call x1, Pallas kernels, whole_frames(): pl.pallas_call(frames_body, out_shape=jax.ShapeDtypeStruct((n_height, eac...  27.4 us
    ppermute x3, waiting for transfers between devices, whole_frames(): lax.ppermute(own, 'pair', ring(n_pair, step))  22 us
    all_to_all x1, blocking collectives, whole_frames(): lax.all_to_all(decoded, ('pair', 'core'), split_axis=0, concat_axis=0)  15.8 us
    all_to_all x1, starting transfers between devices, whole_frames(): lax.all_to_all(picked, ('frame', 'pair', 'core'), split_axis=0, concat_ax...  7.3 us
    ppermute x3, starting transfers between devices, whole_frames(): lax.ppermute(own, 'pair', ring(n_pair, step))  4.76 us
    unnamed x26, local copies, waits for them, and re-layouts  3.65 us
    ppermute x1, waiting for transfers between devices, whole_frames(): other = lax.ppermute(same, 'core', swap)  2.25 us
  transfers between devices with their start and end apart: 6, of which 4 were waited for; matrix products, arithmetic and copies ran while one was open for 0% of the time, Pallas kernels for 0%

profile of v2, /device:TPU:0, one launch (start us, length us, event | category | flops | bytes accessed | tf_op | source)
XLA Modules:
  0.0 87.0 jit_solution(7339288271882982839)
XLA Ops:
  0.0 0.0 copy-start.1
  0.0 1.0 %copy-done.1 = bf16[33,2,8,256]{3,2,1,0:T(8,128)(2,1)S(1)} copy-done((bf16[33,2,8,256]{3,2,1,0:T(8,128)(2,1)S(1)}, bf16[33,2,8,256]{3,2,1,0:T(8,128)(2,1)}, u32[]{:S(2)}) %copy-start.1) | copy-done | bytes 270360
  1.0 0.0 copy-start.2
  1.0 0.7 copy-done.2
  1.6 1.7 %pick.1 = bf16[32,4,16,256]{3,2,1,0:T(8,128)(2,1)} custom-call(s32[4]{0:T(128)S(1)} %copy-done.2, bf16[33,16,256]{2,1,0:T(8,128)(2,1)S(1)} %bitcast.20), custom_call_target="tpu_custom_call" | custom-call | tf_op jit(solution)/shard_map/pick/pallas_call | solution.py:506
  3.3 0.0 copy-start.11
  3.3 0.0 copy-start.12
  3.3 7.3 %all-to-all-start = ((bf16[32,4,16,256]{3,2,1,0:T(8,128)(2,1)}), bf16[32,4,16,256]{3,2,1,0:T(8,128)(2,1)S(1)}, u32[]{:S(2)}, u32[]{:S(2)}) async-start(bf16[32,4,16,256]{3,2,1,0:T(8,128)(2,1)} %pick.1), calls=%async_computation | async-start | bytes 2097152 | tf_op jit(solution)/shard_map/all_to_all | solution.py:516
  10.6 0.0 copy-done.11
  10.6 0.0 copy-done.12
  10.7 1.8 %collective-permute-start.2 = (bf16[2,288,256]{2,1,0:T(8,128)(2,1)S(1)}, bf16[2,288,256]{2,1,0:T(8,128)(2,1)S(1)}, u32[]{:S(2)}, u32[]{:S(2)}) collective-permute-start(bf16[2,288,256]{2,1,0:T(8,128)(2,1)S(1)} %get-tuple-element.6), channel_id=1, source_target_pairs={{0,4},{2,6},{4,0},{6,2},{1,5},{3,7},{5,1},{7,3},{8,12},{10,14},{12... | collective-permute-start | bytes 884744 | tf_op jit(solution)/shard_map/ppermute | solution.py:521
  12.5 1.5 %collective-permute-start.1 = (bf16[2,288,256]{2,1,0:T(8,128)(2,1)S(1)}, bf16[2,288,256]{2,1,0:T(8,128)(2,1)S(1)}, u32[]{:S(2)}, u32[]{:S(2)}) collective-permute-start(bf16[2,288,256]{2,1,0:T(8,128)(2,1)S(1)} %get-tuple-element.6), channel_id=1, source_target_pairs={{0,2},{2,4},{4,6},{6,0},{1,3},{3,5},{5,7},{7,1},{8,10},{10,12},{12... | collective-permute-start | bytes 884744 | tf_op jit(solution)/shard_map/ppermute | solution.py:521
  14.0 1.5 %collective-permute-start.3 = (bf16[2,288,256]{2,1,0:T(8,128)(2,1)S(1)}, bf16[2,288,256]{2,1,0:T(8,128)(2,1)S(1)}, u32[]{:S(2)}, u32[]{:S(2)}) collective-permute-start(bf16[2,288,256]{2,1,0:T(8,128)(2,1)S(1)} %get-tuple-element.6), channel_id=1, source_target_pairs={{0,6},{2,0},{4,2},{6,4},{1,7},{3,1},{5,3},{7,5},{8,14},{10,8},{12,... | collective-permute-start | bytes 884744 | tf_op jit(solution)/shard_map/ppermute | solution.py:521
  15.4 21.9 %collective-permute-done.2 = bf16[2,288,256]{2,1,0:T(8,128)(2,1)S(1)} collective-permute-done((bf16[2,288,256]{2,1,0:T(8,128)(2,1)S(1)}, bf16[2,288,256]{2,1,0:T(8,128)(2,1)S(1)}, u32[]{:S(2)}, u32[]{:S(2)}) %collective-permute-start.2) | collective-permute-done | bytes 294944 | tf_op jit(solution)/shard_map/ppermute | solution.py:521
  37.4 0.0 collective-permute-done.1
  37.4 0.1 collective-permute-done.3
  37.5 0.0 copy-start.3
  37.5 0.0 copy-start.4
  37.5 0.0 copy-start.5
  37.5 0.0 copy-start.6
  37.5 0.0 copy-start.7
  37.5 0.0 copy-start.8
  37.5 0.0 copy-start.9
  37.5 0.0 copy-start.10
  37.5 0.2 pad_maximum_fusion.same_ref
  37.7 0.1 collective-permute-start.4
  37.7 0.0 all-to-all-done.part_ref
  37.8 0.6 collective-permute-start
  38.3 2.2 %collective-permute-done.4.other_ref = bf16[4,2,288,256]{3,2,1,0:T(8,128)(2,1)S(1)} collective-permute-done((bf16[4,2,288,256]{3,2,1,0:T(8,128)(2,1)S(1)}, bf16[4,2,288,256]{3,2,1,0:T(8,128)(2,1)S(1)}, u32[]{:S(2)}, u32[]{:S(2)}) %collective-permute-start.4) | collective-permute-done | bytes 1179680 | tf_op jit(solution)/shard_map/ppermute | solution.py:523
  40.6 0.4 collective-permute-done.swapped_ref
  41.0 0.0 copy-done.3
  41.0 0.0 copy-done.4
  41.0 0.0 copy-done.5
  41.0 0.0 copy-done.6
  41.0 0.0 copy-done.7
  41.0 0.0 copy-done.8
  41.0 0.0 copy-done.9
  41.0 0.0 copy-done.10
  41.0 0.0 copy-start
  41.0 2.0 %copy-done = bf16[6912,256]{1,0:T(8,128)(2,1)S(1)} copy-done((bf16[6912,256]{1,0:T(8,128)(2,1)S(1)}, bf16[6912,256]{1,0:T(8,128)(2,1)}, u32[]{:S(2)}) %copy-start) | copy-done | bytes 3538968
  43.0 27.4 %frames.1 = bf16[8,3,2,32,256]{4,3,2,1,0:T(8,128)(2,1)S(1)} custom-call(s32[4]{0:T(128)S(1)} %copy-done.3, bf16[32,4,16,256]{3,2,1,0:T(8,128)(2,1)S(1)} %all-to-all-done.part_ref, bf16[32,16,256]{2,1,0:T(8,128)(2,1)S(1)} %collective-permute-done.swapped_ref, bf16[6912,256]{1,0:T(8,128)(2,1)S(1)} %copy-done, ...), custom_call_target="tpu_custom_call" | custom-call | tf_op jit(solution)/shard_map/frames/pallas_call | solution.py:529
  70.4 15.8 %all_to_all.10 = bf16[8,3,2,32,256]{4,3,2,1,0:T(8,128)(2,1)S(1)} all-to-all(bf16[8,3,2,32,256]{4,3,2,1,0:T(8,128)(2,1)S(1)} %frames.1), channel_id=1, replica_groups=mesh['frame'=4,'pair'=4,'core'=2] {'pair','core'}, dimensions={0} | all-to-all | bytes 1572864 | tf_op jit(solution)/shard_map/all_to_all | solution.py:550
  86.2 0.9 slice.13
  (2 shorter events, 0.1 us)
Async XLA Ops:
  0.0 1.0 %copy-start.1 = (bf16[33,2,8,256]{3,2,1,0:T(8,128)(2,1)S(1)}, bf16[33,2,8,256]{3,2,1,0:T(8,128)(2,1)}, u32[]{:S(2)}) copy-start(bf16[33,2,8,256]{3,2,1,0:T(8,128)(2,1)} %param.12) | copy-start | bytes 811012
  1.0 0.7 copy-start.2
  3.3 7.3 %copy-start.11 = (bf16[288,256]{1,0:T(8,128)(2,1)S(1)}, bf16[288,256]{1,0:T(8,128)(2,1)}, u32[]{:S(2)}) copy-start(bf16[288,256]{1,0:T(8,128)(2,1)} %param.22) | copy-start | bytes 442372
  3.3 7.3 %copy-start.12 = (bf16[288,256]{1,0:T(8,128)(2,1)S(1)}, bf16[288,256]{1,0:T(8,128)(2,1)}, u32[]{:S(2)}) copy-start(bf16[288,256]{1,0:T(8,128)(2,1)} %param.18) | copy-start | bytes 442372
  3.3 34.4 %all-to-all-start = ((bf16[32,4,16,256]{3,2,1,0:T(8,128)(2,1)}), bf16[32,4,16,256]{3,2,1,0:T(8,128)(2,1)S(1)}, u32[]{:S(2)}, u32[]{:S(2)}) async-start(bf16[32,4,16,256]{3,2,1,0:T(8,128)(2,1)} %pick.1), calls=%async_computation | async-start | bytes 2097152 | tf_op jit(solution)/shard_map/all_to_all | solution.py:516
  10.7 26.7 %collective-permute-start.2 = (bf16[2,288,256]{2,1,0:T(8,128)(2,1)S(1)}, bf16[2,288,256]{2,1,0:T(8,128)(2,1)S(1)}, u32[]{:S(2)}, u32[]{:S(2)}) collective-permute-start(bf16[2,288,256]{2,1,0:T(8,128)(2,1)S(1)} %get-tuple-element.6), channel_id=1, source_target_pairs={{0,4},{2,6},{4,0},{6,2},{1,5},{3,7},{5,1},{7,3},{8,12},{10,14},{12... | collective-permute-start | bytes 884744 | tf_op jit(solution)/shard_map/ppermute | solution.py:521
  12.5 24.8 %collective-permute-start.1 = (bf16[2,288,256]{2,1,0:T(8,128)(2,1)S(1)}, bf16[2,288,256]{2,1,0:T(8,128)(2,1)S(1)}, u32[]{:S(2)}, u32[]{:S(2)}) collective-permute-start(bf16[2,288,256]{2,1,0:T(8,128)(2,1)S(1)} %get-tuple-element.6), channel_id=1, source_target_pairs={{0,2},{2,4},{4,6},{6,0},{1,3},{3,5},{5,7},{7,1},{8,10},{10,12},{12... | collective-permute-start | bytes 884744 | tf_op jit(solution)/shard_map/ppermute | solution.py:521
  14.0 23.5 %collective-permute-start.3 = (bf16[2,288,256]{2,1,0:T(8,128)(2,1)S(1)}, bf16[2,288,256]{2,1,0:T(8,128)(2,1)S(1)}, u32[]{:S(2)}, u32[]{:S(2)}) collective-permute-start(bf16[2,288,256]{2,1,0:T(8,128)(2,1)S(1)} %get-tuple-element.6), channel_id=1, source_target_pairs={{0,6},{2,0},{4,2},{6,4},{1,7},{3,1},{5,3},{7,5},{8,14},{10,8},{12,... | collective-permute-start | bytes 884744 | tf_op jit(solution)/shard_map/ppermute | solution.py:521
  37.5 3.5 %copy-start.3 = (s32[4]{0:T(128)S(1)}, s32[4]{0:T(128)}, u32[]{:S(2)}) copy-start(s32[4]{0:T(128)} %counts_ref.3) | copy-start | bytes 52
  37.5 3.5 %copy-start.4 = (f32[256]{0:T(256)S(1)}, f32[256]{0:T(256)}, u32[]{:S(2)}) copy-start(f32[256]{0:T(256)} %param.15) | copy-start | bytes 3076
  37.5 3.5 %copy-start.5 = (f32[256]{0:T(256)S(1)}, f32[256]{0:T(256)}, u32[]{:S(2)}) copy-start(f32[256]{0:T(256)} %param.16) | copy-start | bytes 3076
  37.5 3.5 %copy-start.6 = (f32[256]{0:T(256)S(1)}, f32[256]{0:T(256)}, u32[]{:S(2)}) copy-start(f32[256]{0:T(256)} %param.17) | copy-start | bytes 3076
  37.5 3.5 %copy-start.7 = (f32[256]{0:T(256)S(1)}, f32[256]{0:T(256)}, u32[]{:S(2)}) copy-start(f32[256]{0:T(256)} %param.19) | copy-start | bytes 3076
  37.5 3.5 %copy-start.8 = (f32[256]{0:T(256)S(1)}, f32[256]{0:T(256)}, u32[]{:S(2)}) copy-start(f32[256]{0:T(256)} %param.20) | copy-start | bytes 3076
  37.5 3.5 %copy-start.9 = (f32[256]{0:T(256)S(1)}, f32[256]{0:T(256)}, u32[]{:S(2)}) copy-start(f32[256]{0:T(256)} %param.21) | copy-start | bytes 3076
  37.5 3.5 %copy-start.10 = (f32[256]{0:T(256)S(1)}, f32[256]{0:T(256)}, u32[]{:S(2)}) copy-start(f32[256]{0:T(256)} %param.23) | copy-start | bytes 3076
  37.7 2.9 %collective-permute-start.4 = (bf16[4,2,288,256]{3,2,1,0:T(8,128)(2,1)S(1)}, bf16[4,2,288,256]{3,2,1,0:T(8,128)(2,1)S(1)}, u32[]{:S(2)}, u32[]{:S(2)}) collective-permute-start(bf16[4,2,288,256]{3,2,1,0:T(8,128)(2,1)S(1)} %pad_maximum_fusion.same_ref), channel_id=1, source_target_pairs={{0,1},{1,0},{2,3},{3,2},{4,5},{5,4},{6,7},{7,6},{8,9},{9,8},{10,11... | collective-permute-start | bytes 3538952 | tf_op jit(solution)/shard_map/ppermute | solution.py:523
  37.8 3.2 %collective-permute-start = (bf16[32,16,256]{2,1,0:T(8,128)(2,1)S(1)}, bf16[32,16,256]{2,1,0:T(8,128)(2,1)S(1)}, u32[]{:S(2)}, u32[]{:S(2)}) collective-permute-start(bf16[32,16,256]{2,1,0:T(8,128)(2,1)S(1)} %slice_bitcast_fusion), channel_id=1, source_target_pairs={{0,1},{1,0},{2,3},{3,2},{4,5},{5,4},{6,7},{7,6},{8,9},{9,8},{10,11... | collective-permute-start | bytes 786440 | tf_op jit(solution)/shard_map/ppermute | solution.py:517
  41.0 2.0 %copy-start = (bf16[6912,256]{1,0:T(8,128)(2,1)S(1)}, bf16[6912,256]{1,0:T(8,128)(2,1)}, u32[]{:S(2)}) copy-start(bf16[6912,256]{1,0:T(8,128)(2,1)} %temporal_ref.1) | copy-start | bytes 10616836

commit v3 on v2

--- a/solution.py
+++ b/solution.py
@@ -344,16 +344,16 @@
                     out_ref[(owner * n_pair + pair) * 2 + core, place] = values
 
 
-def group_scale(values, gain_ref, shift_ref):
-    cells, channels = values.shape
-    width_group = channels // GROUPS
-    sample = 1.0 / (cells * width_group)
-    mean = group_total(jnp.sum(values, axis=0, keepdims=True), width_group) * sample
-    centered = values - mean
-    squares = jnp.sum(centered * centered, axis=0, keepdims=True)
-    variance = group_total(squares, width_group) * sample
-    scale = lax.rsqrt(variance + EPS) * gain_ref[...]
-    return scale, shift_ref[...] - mean * scale
+def group_spread(values, width_group):
+    lane = lax.broadcasted_iota(jnp.int32, values.shape, 1) % width_group
+    size, total = values.shape[1], values
+    for step in range(1, width_group):
+        total = total + jnp.where(
+            lane >= step,
+            pltpu.roll(values, step, 1),
+            pltpu.roll(values, size - width_group + step, 1),
+        )
+    return total
 
 
 def frames_body(
@@ -361,128 +361,184 @@
     temporal_bias_ref, first_gain_ref, first_shift_ref, first_bias_ref,
     second_gain_ref, second_shift_ref, second_bias_ref,
     out_ref,
-    raw_ref, taps_ref, normed_ref, total_ref, blended_ref, weights_ref, sems,
+    *refs,
 ):
     n_height, each, rows, width, channels = out_ref.shape
+    places = each + 2
+    taps_refs, refs = refs[:places], refs[places:]
+    normed_refs, refs = refs[:each], refs[each:]
+    total_refs, refs = refs[:each], refs[each:]
+    blended_refs, refs = refs[:each], refs[each:]
+    field_refs, refs = refs[:each], refs[each:]
+    landed_ref, raw_ref, time_ref, weights_ref, land_sems, time_sems, sems = refs
     n_pair = n_height // 2
     n_frame = part_ref.shape[0] // n_height
     columns = width // n_frame
     all_rows = n_height * rows
     depth = 3 * channels
     cells = all_rows * width
+    width_group = channels // GROUPS
     pair, core = lax.axis_index("pair"), lax.axis_index("core")
     span = same_ref.shape[2]
+
+    landings = [
+        pltpu.make_async_copy(
+            part_ref.at[:, place] if place <= each else swapped_ref,
+            landed_ref.at[place],
+            land_sems.at[place],
+        )
+        for place in range(places)
+    ]
+    time_copies = [
+        pltpu.make_async_copy(
+            temporal_ref.at[pl.ds(tap * 3 * depth, 3 * depth)],
+            time_ref.at[tap],
+            time_sems.at[tap],
+        )
+        for tap in range(3)
+    ]
     copies = []
     for which in range(2):
+        of_weight = []
         for step in range(n_pair):
             source = lax.rem(pair - step + n_pair, n_pair)
             for side, (parts_ref, of_core) in enumerate(((same_ref, core), (other_ref, 1 - core))):
-                copies.append(
+                start = pl.multiple_of((source * 2 + of_core) * span, span)
+                of_weight.append(
                     pltpu.make_async_copy(
                         parts_ref.at[step, which],
-                        weights_ref.at[which, source * 2 + of_core],
+                        weights_ref.at[which, pl.ds(start, span)],
                         sems.at[which, step, side],
                     )
                 )
-    for copy in copies:
+        copies.append(of_weight)
+    for copy in landings[:3] + time_copies + landings[3:] + copies[0] + copies[1]:
         copy.start()
 
     border = jnp.zeros((width, depth), BF16)
-    for place in range(each + 2):
-        taps_ref[place, 0] = border
-        taps_ref[place, all_rows + 1] = border
-    for place in range(each):
-        normed_ref[place, 0] = border
-        normed_ref[place, all_rows + 1] = border
-
-    def lay(place, load):
+    for ref in taps_refs + normed_refs:
+        ref[0] = border
+        ref[all_rows + 1] = border
+
+    def lay(place):
+        landings[place].wait()
         for height in range(n_height):
-            pieces = [load(peer * n_height + height).astype(F32) for peer in range(n_frame)]
+            pieces = [
+                landed_ref[place, peer * n_height + height].astype(F32) for peer in range(n_frame)
+            ]
             for row in range(rows):
                 values = jnp.concatenate(
                     [piece[row * columns : (row + 1) * columns] for piece in pieces], axis=0
                 )
                 raw_ref[place, height * rows + row] = values.astype(BF16)
-                taps_ref[place, height * rows + row + 1] = with_column_taps(silu(values))
-
-    def lay_part(place, _):
-        lay(place, lambda source: part_ref[source, place])
-        return 0
-
-    lax.fori_loop(0, each + 1, lay_part, 0)
-    lay(each + 1, lambda source: swapped_ref[source])
-
-    def convolve(source_ref, weight_of, start):
+                taps_refs[place][height * rows + row + 1] = with_column_taps(silu(values))
+
+    def convolved(source_ref, weight_ref):
         summed = None
         for row_tap in range(3):
-            patches = source_ref[start, row_tap : row_tap + all_rows]
             product = jnp.dot(
-                patches.reshape(each * cells, depth),
-                weight_of(row_tap),
+                source_ref[row_tap : row_tap + all_rows].reshape(cells, depth),
+                weight_ref[row_tap * depth : (row_tap + 1) * depth],
                 preferred_element_type=F32,
             )
             summed = product if summed is None else summed + product
-        return summed.reshape(each, cells, channels)
-
-    for time_tap in range(3):
-        start = time_tap + core * (2 - 2 * time_tap)
-        product = convolve(
-            taps_ref,
-            lambda row_tap: temporal_ref[
-                (time_tap * 3 + row_tap) * depth : (time_tap * 3 + row_tap + 1) * depth
-            ],
-            pl.ds(start, each),
-        )
-        if time_tap == 0:
-            total_ref[...] = product
-        else:
-            total_ref[...] += product
-
-    def norm(place, values, gain_ref, shift_ref):
-        scale, offset = group_scale(values, gain_ref, shift_ref)
+        return summed
+
+    def temporal(place):
+        for step in range(3):
+            tap = step + core * (2 - 2 * step)
+            product = convolved(taps_refs[place + step], time_ref.at[tap])
+            if step == 0:
+                total_refs[place][...] = product
+            else:
+                total_refs[place][...] += product
+
+    def field_and_scale(field_ref, row_of, gain_ref, shift_ref):
+        pivot = None
+        sums = squares = jnp.zeros((8, channels), F32)
         for row in range(all_rows):
-            line = values[row * width : (row + 1) * width] * scale + offset
-            normed_ref[place, row + 1] = with_column_taps(silu(line))
-
-    def norm_first(place, _):
-        raw = raw_ref[place + 2 - 2 * core].astype(F32).reshape(cells, channels)
-        blended = (raw + total_ref[place] + temporal_bias_ref[...]).astype(BF16)
-        blended_ref[place] = blended
-        norm(place, blended.astype(F32), first_gain_ref, first_shift_ref)
-        return 0
-
-    lax.fori_loop(0, each, norm_first, 0)
-    for copy in copies[: len(copies) // 2]:
-        copy.wait()
-
-    def weight_of(which):
-        weight = weights_ref[which].reshape(2 * n_pair * span, channels)
-        return lambda row_tap: weight[row_tap * depth : (row_tap + 1) * depth]
-
-    total_ref[...] = convolve(normed_ref, weight_of(0), slice(None))
-
-    def norm_second(place, _):
-        values = (total_ref[place] + first_bias_ref[...]).astype(BF16).astype(F32)
-        norm(place, values, second_gain_ref, second_shift_ref)
-        return 0
-
-    lax.fori_loop(0, each, norm_second, 0)
-    for copy in copies[len(copies) // 2 :]:
-        copy.wait()
-    total_ref[...] = convolve(normed_ref, weight_of(1), slice(None))
+            rounded = row_of(row).astype(BF16)
+            field_ref[row] = rounded
+            values = rounded.astype(F32)
+            if pivot is None:
+                pivot = values[:1]
+            apart = (values - pivot).reshape(width // 8, 8, channels)
+            sums = sums + jnp.sum(apart, axis=0)
+            squares = squares + jnp.sum(apart * apart, axis=0)
+        sums = jnp.sum(sums, axis=0, keepdims=True)
+        squares = jnp.sum(squares, axis=0, keepdims=True)
+        own = sums * (1.0 / cells)
+        sample = 1.0 / width_group
+        mean = group_spread(own + pivot, width_group) * sample
+        off = own + pivot - mean
+        spread = squares * (1.0 / cells) - own * own + off * off
+        variance = jnp.maximum(group_spread(spread, width_group) * sample, 0.0)
+        scale = lax.rsqrt(variance + EPS) * gain_ref[...]
+        return 0.5 * scale, 0.5 * (shift_ref[...] - mean * scale)
+
+    def norm(place, field_ref, row_of, gain_ref, shift_ref):
+        scale, offset = field_and_scale(field_ref, row_of, gain_ref, shift_ref)
+        for row in range(all_rows):
+            half = field_ref[row].astype(F32) * scale + offset
+            normed_refs[place][row + 1] = with_column_taps(half + half * jnp.tanh(half))
+
+    def first_norm(place):
+        raw_at = place + 2 - 2 * core
+
+        def row_of(row):
+            product = total_refs[place][row * width : (row + 1) * width]
+            return raw_ref[raw_at, row].astype(F32) + product + temporal_bias_ref[...]
+
+        norm(place, blended_refs[place], row_of, first_gain_ref, first_shift_ref)
+
     count = counts_ref[lax.axis_index("frame")]
 
-    def finish(place, _):
+    def first_conv(place):
+        total_refs[place][...] = convolved(normed_refs[place], weights_ref.at[0])
+
+    def second_norm(place):
+        def row_of(row):
+            return total_refs[place][row * width : (row + 1) * width] + first_bias_ref[...]
+
+        norm(place, field_refs[place], row_of, second_gain_ref, second_shift_ref)
+
+    def second_conv(place):
+        total_refs[place][...] = convolved(normed_refs[place], weights_ref.at[1])
+
+    def finish(place):
         at = place + core * (each - 1 - 2 * place)
         live = pair * 2 * each + core * each + at < count
-        decoded = blended_ref[place].astype(F32) + (total_ref[place] + second_bias_ref[...])
-        decoded = jnp.where(live, decoded, 0.0).astype(BF16)
-        decoded = decoded.reshape(n_height, rows, width, channels)
-        for height in range(n_height):
-            out_ref[height, at] = decoded[height]
-        return 0
-
-    lax.fori_loop(0, each, finish, 0)
+        for row in range(all_rows):
+            product = total_refs[place][row * width : (row + 1) * width] + second_bias_ref[...]
+            decoded = blended_refs[place][row].astype(F32) + product
+            out_ref[row // rows, at, row % rows] = jnp.where(live, decoded, 0.0).astype(BF16)
+
+    def ready(which):
+        for copy in which:
+            copy.wait()
+
+    for place in range(3):
+        lay(place)
+    ready(time_copies)
+    temporal(0)
+    for place in range(3, places):
+        lay(place)
+    for place in range(1, each):
+        temporal(place)
+        first_norm(place - 1)
+    ready(copies[0])
+    ready(copies[1])
+    first_norm(each - 1)
+    for place in range(each):
+        first_conv(place)
+        if place > 0:
+            second_norm(place - 1)
+    second_norm(each - 1)
+    for place in range(each):
+        second_conv(place)
+        if place > 0:
+            finish(place - 1)
+    finish(each - 1)
 
 
 def ring(size, step):
@@ -529,15 +585,18 @@
     decoded = pl.pallas_call(
         frames_body,
         out_shape=jax.ShapeDtypeStruct((n_height, each, rows, width, channels), BF16),
-        in_specs=[SMEM] + [VMEM] * 3 + [HBM] * 2 + [VMEM] * 7,
+        in_specs=[SMEM] + [HBM] * 5 + [VMEM] * 7,
         out_specs=VMEM,
-        scratch_shapes=[
+        scratch_shapes=[pltpu.VMEM((all_rows + 2,) + taps, BF16)] * (2 * each + 2)
+        + [pltpu.VMEM((all_rows * width, channels), F32)] * each
+        + [pltpu.VMEM((all_rows, width, channels), BF16)] * (2 * each)
+        + [
+            pltpu.VMEM((each + 2, n_frame * n_height, rows * columns, channels), BF16),
             pltpu.VMEM((each + 2, all_rows, width, channels), BF16),
-            pltpu.VMEM((each + 2, all_rows + 2) + taps, BF16),
-            pltpu.VMEM((each, all_rows + 2) + taps, BF16),
-            pltpu.VMEM((each, all_rows * width, channels), F32),
-            pltpu.VMEM((each, all_rows * width, channels), BF16),
-            pltpu.VMEM((2, n_height) + first_weight.shape, BF16),
+            pltpu.VMEM((3, 9 * channels, channels), BF16),
+            pltpu.VMEM((2, 9 * channels, channels), BF16),
+            pltpu.SemaphoreType.DMA((each + 2,)),
+            pltpu.SemaphoreType.DMA((3,)),
             pltpu.SemaphoreType.DMA((2, n_pair, 2)),
         ],
         compiler_params=params,

time: 87.3 us -> 78.8 us (0.903)
  Pallas kernels: 29.1 us -> 20.6 us
    pallas_call x1, Pallas kernels: 27.4 us -> 18.9 us  [whole_frames(): pl.pallas_call(frames_body, out_shape=jax.ShapeDtypeStruct((n_height, eac...]
where the time goes in v3:
time: 78.8 us; the launch traced here: 78.5 us
  waiting for transfers between devices  24.6 us (31%)
  Pallas kernels  20.6 us (26%)
  blocking collectives  15.8 us (20%)
  starting transfers between devices  12.7 us (16%)
  local copies, waits for them, and re-layouts  4.54 us (6%)
    ppermute x3, waiting for transfers between devices, whole_frames(): lax.ppermute(own, 'pair', ring(n_pair, step))  22 us
    pallas_call x1, Pallas kernels, whole_frames(): pl.pallas_call(frames_body, out_shape=jax.ShapeDtypeStruct((n_height, eac...  18.9 us
    all_to_all x1, blocking collectives, whole_frames(): lax.all_to_all(decoded, ('pair', 'core'), split_axis=0, concat_axis=0)  15.8 us
    all_to_all x1, starting transfers between devices, whole_frames(): lax.all_to_all(picked, ('frame', 'pair', 'core'), split_axis=0, concat_ax...  7.3 us
    ppermute x3, starting transfers between devices, whole_frames(): lax.ppermute(own, 'pair', ring(n_pair, step))  4.76 us
    unnamed x26, local copies, waits for them, and re-layouts  3.65 us
    ppermute x1, waiting for transfers between devices, whole_frames(): other = lax.ppermute(same, 'core', swap)  2.25 us
    pallas_call x1, Pallas kernels, whole_frames(): pl.pallas_call(pick_frames_body, out_shape=jax.ShapeDtypeStruct((n_frame...  1.7 us
  transfers between devices with their start and end apart: 6, of which 4 were waited for; matrix products, arithmetic and copies ran while one was open for 0% of the time, Pallas kernels for 0%

profile of v3, /device:TPU:0, one launch (start us, length us, event | category | flops | bytes accessed | tf_op | source)
XLA Modules:
  0.0 78.5 jit_solution(815313648202774848)
XLA Ops:
  0.0 0.0 copy-start.1
  0.0 1.0 %copy-done.1 = bf16[33,2,8,256]{3,2,1,0:T(8,128)(2,1)S(1)} copy-done((bf16[33,2,8,256]{3,2,1,0:T(8,128)(2,1)S(1)}, bf16[33,2,8,256]{3,2,1,0:T(8,128)(2,1)}, u32[]{:S(2)}) %copy-start.1) | copy-done | bytes 270360
  1.0 0.0 copy-start.2
  1.0 0.7 copy-done.2
  1.6 1.7 %pick.1 = bf16[32,4,16,256]{3,2,1,0:T(8,128)(2,1)} custom-call(s32[4]{0:T(128)S(1)} %copy-done.2, bf16[33,16,256]{2,1,0:T(8,128)(2,1)S(1)} %bitcast.20), custom_call_target="tpu_custom_call" | custom-call | tf_op jit(solution)/shard_map/pick/pallas_call | solution.py:562
  3.3 0.0 copy-start.11
  3.3 0.0 copy-start.12
  3.3 7.3 %all-to-all-start = ((bf16[32,4,16,256]{3,2,1,0:T(8,128)(2,1)}), bf16[32,4,16,256]{3,2,1,0:T(8,128)(2,1)S(1)}, u32[]{:S(2)}, u32[]{:S(2)}) async-start(bf16[32,4,16,256]{3,2,1,0:T(8,128)(2,1)} %pick.1), calls=%async_computation | async-start | bytes 2097152 | tf_op jit(solution)/shard_map/all_to_all | solution.py:572
  10.6 0.0 copy-done.11
  10.6 0.0 copy-done.12
  10.7 1.8 %collective-permute-start.2 = (bf16[2,288,256]{2,1,0:T(8,128)(2,1)S(1)}, bf16[2,288,256]{2,1,0:T(8,128)(2,1)S(1)}, u32[]{:S(2)}, u32[]{:S(2)}) collective-permute-start(bf16[2,288,256]{2,1,0:T(8,128)(2,1)S(1)} %get-tuple-element.6), channel_id=1, source_target_pairs={{0,4},{2,6},{4,0},{6,2},{1,5},{3,7},{5,1},{7,3},{8,12},{10,14},{12... | collective-permute-start | bytes 884744 | tf_op jit(solution)/shard_map/ppermute | solution.py:577
  12.5 1.5 %collective-permute-start.1 = (bf16[2,288,256]{2,1,0:T(8,128)(2,1)S(1)}, bf16[2,288,256]{2,1,0:T(8,128)(2,1)S(1)}, u32[]{:S(2)}, u32[]{:S(2)}) collective-permute-start(bf16[2,288,256]{2,1,0:T(8,128)(2,1)S(1)} %get-tuple-element.6), channel_id=1, source_target_pairs={{0,2},{2,4},{4,6},{6,0},{1,3},{3,5},{5,7},{7,1},{8,10},{10,12},{12... | collective-permute-start | bytes 884744 | tf_op jit(solution)/shard_map/ppermute | solution.py:577
  14.0 1.5 %collective-permute-start.3 = (bf16[2,288,256]{2,1,0:T(8,128)(2,1)S(1)}, bf16[2,288,256]{2,1,0:T(8,128)(2,1)S(1)}, u32[]{:S(2)}, u32[]{:S(2)}) collective-permute-start(bf16[2,288,256]{2,1,0:T(8,128)(2,1)S(1)} %get-tuple-element.6), channel_id=1, source_target_pairs={{0,6},{2,0},{4,2},{6,4},{1,7},{3,1},{5,3},{7,5},{8,14},{10,8},{12,... | collective-permute-start | bytes 884744 | tf_op jit(solution)/shard_map/ppermute | solution.py:577
  15.4 21.9 %collective-permute-done.2 = bf16[2,288,256]{2,1,0:T(8,128)(2,1)S(1)} collective-permute-done((bf16[2,288,256]{2,1,0:T(8,128)(2,1)S(1)}, bf16[2,288,256]{2,1,0:T(8,128)(2,1)S(1)}, u32[]{:S(2)}, u32[]{:S(2)}) %collective-permute-start.2) | collective-permute-done | bytes 294944 | tf_op jit(solution)/shard_map/ppermute | solution.py:577
  37.4 0.0 collective-permute-done.1
  37.4 0.1 collective-permute-done.3
  37.5 0.0 copy-start.3
  37.5 0.0 copy-start.4
  37.5 0.0 copy-start.5
  37.5 0.0 copy-start.6
  37.5 0.0 copy-start.7
  37.5 0.0 copy-start.8
  37.5 0.0 copy-start.9
  37.5 0.0 copy-start.10
  37.5 0.2 pad_maximum_fusion.same_ref
  37.7 0.1 collective-permute-start.4
  37.7 0.0 all-to-all-done.part_ref
  37.8 0.6 collective-permute-start
  38.3 2.2 %collective-permute-done.4.other_ref = bf16[4,2,288,256]{3,2,1,0:T(8,128)(2,1)S(1)} collective-permute-done((bf16[4,2,288,256]{3,2,1,0:T(8,128)(2,1)S(1)}, bf16[4,2,288,256]{3,2,1,0:T(8,128)(2,1)S(1)}, u32[]{:S(2)}, u32[]{:S(2)}) %collective-permute-start.4) | collective-permute-done | bytes 1179680 | tf_op jit(solution)/shard_map/ppermute | solution.py:579
  40.6 0.4 collective-permute-done.swapped_ref
  41.0 0.0 copy-done.3
  41.0 0.0 copy-done.4
  41.0 0.0 copy-done.5
  41.0 0.0 copy-done.6
  41.0 0.0 copy-done.7
  41.0 0.0 copy-done.8
  41.0 0.0 copy-done.9
  41.0 0.0 copy-done.10
  41.0 0.0 copy-start
  41.0 2.0 %copy-done = bf16[6912,256]{1,0:T(8,128)(2,1)S(1)} copy-done((bf16[6912,256]{1,0:T(8,128)(2,1)S(1)}, bf16[6912,256]{1,0:T(8,128)(2,1)}, u32[]{:S(2)}) %copy-start) | copy-done | bytes 3538968
  43.0 18.9 %frames.1 = bf16[8,3,2,32,256]{4,3,2,1,0:T(8,128)(2,1)S(1)} custom-call(s32[4]{0:T(128)S(1)} %copy-done.3, bf16[32,4,16,256]{3,2,1,0:T(8,128)(2,1)S(1)} %all-to-all-done.part_ref, bf16[32,16,256]{2,1,0:T(8,128)(2,1)S(1)} %collective-permute-done.swapped_ref, bf16[6912,256]{1,0:T(8,128)(2,1)S(1)} %copy-done, ...), custom_call_target="tpu_custom_call" | custom-call | tf_op jit(solution)/shard_map/frames/pallas_call | solution.py:585
  61.9 15.8 %all_to_all.10 = bf16[8,3,2,32,256]{4,3,2,1,0:T(8,128)(2,1)S(1)} all-to-all(bf16[8,3,2,32,256]{4,3,2,1,0:T(8,128)(2,1)S(1)} %frames.1), channel_id=1, replica_groups=mesh['frame'=4,'pair'=4,'core'=2] {'pair','core'}, dimensions={0} | all-to-all | bytes 1572864 | tf_op jit(solution)/shard_map/all_to_all | solution.py:609
  77.7 0.9 %slice.13 = bf16[6,3,2,32,256]{4,3,2,1,0:T(8,128)(2,1)} slice(bf16[8,3,2,32,256]{4,3,2,1,0:T(8,128)(2,1)S(1)} %all_to_all.10), slice={[0:6], [0:3], [0:2], [0:32], [0:256]} | slice | bytes 1179648 | tf_op jit(solution)/shard_map/slice | solution.py:610
  (2 shorter events, 0.1 us)
Async XLA Ops:
  0.0 1.0 %copy-start.1 = (bf16[33,2,8,256]{3,2,1,0:T(8,128)(2,1)S(1)}, bf16[33,2,8,256]{3,2,1,0:T(8,128)(2,1)}, u32[]{:S(2)}) copy-start(bf16[33,2,8,256]{3,2,1,0:T(8,128)(2,1)} %param.12) | copy-start | bytes 811012
  1.0 0.7 copy-start.2
  3.3 7.3 %copy-start.11 = (bf16[288,256]{1,0:T(8,128)(2,1)S(1)}, bf16[288,256]{1,0:T(8,128)(2,1)}, u32[]{:S(2)}) copy-start(bf16[288,256]{1,0:T(8,128)(2,1)} %param.22) | copy-start | bytes 442372
  3.3 7.3 %copy-start.12 = (bf16[288,256]{1,0:T(8,128)(2,1)S(1)}, bf16[288,256]{1,0:T(8,128)(2,1)}, u32[]{:S(2)}) copy-start(bf16[288,256]{1,0:T(8,128)(2,1)} %param.18) | copy-start | bytes 442372
  3.3 34.4 %all-to-all-start = ((bf16[32,4,16,256]{3,2,1,0:T(8,128)(2,1)}), bf16[32,4,16,256]{3,2,1,0:T(8,128)(2,1)S(1)}, u32[]{:S(2)}, u32[]{:S(2)}) async-start(bf16[32,4,16,256]{3,2,1,0:T(8,128)(2,1)} %pick.1), calls=%async_computation | async-start | bytes 2097152 | tf_op jit(solution)/shard_map/all_to_all | solution.py:572
  10.7 26.7 %collective-permute-start.2 = (bf16[2,288,256]{2,1,0:T(8,128)(2,1)S(1)}, bf16[2,288,256]{2,1,0:T(8,128)(2,1)S(1)}, u32[]{:S(2)}, u32[]{:S(2)}) collective-permute-start(bf16[2,288,256]{2,1,0:T(8,128)(2,1)S(1)} %get-tuple-element.6), channel_id=1, source_target_pairs={{0,4},{2,6},{4,0},{6,2},{1,5},{3,7},{5,1},{7,3},{8,12},{10,14},{12... | collective-permute-start | bytes 884744 | tf_op jit(solution)/shard_map/ppermute | solution.py:577
  12.5 24.8 %collective-permute-start.1 = (bf16[2,288,256]{2,1,0:T(8,128)(2,1)S(1)}, bf16[2,288,256]{2,1,0:T(8,128)(2,1)S(1)}, u32[]{:S(2)}, u32[]{:S(2)}) collective-permute-start(bf16[2,288,256]{2,1,0:T(8,128)(2,1)S(1)} %get-tuple-element.6), channel_id=1, source_target_pairs={{0,2},{2,4},{4,6},{6,0},{1,3},{3,5},{5,7},{7,1},{8,10},{10,12},{12... | collective-permute-start | bytes 884744 | tf_op jit(solution)/shard_map/ppermute | solution.py:577
  14.0 23.5 %collective-permute-start.3 = (bf16[2,288,256]{2,1,0:T(8,128)(2,1)S(1)}, bf16[2,288,256]{2,1,0:T(8,128)(2,1)S(1)}, u32[]{:S(2)}, u32[]{:S(2)}) collective-permute-start(bf16[2,288,256]{2,1,0:T(8,128)(2,1)S(1)} %get-tuple-element.6), channel_id=1, source_target_pairs={{0,6},{2,0},{4,2},{6,4},{1,7},{3,1},{5,3},{7,5},{8,14},{10,8},{12,... | collective-permute-start | bytes 884744 | tf_op jit(solution)/shard_map/ppermute | solution.py:577
  37.5 3.5 %copy-start.3 = (s32[4]{0:T(128)S(1)}, s32[4]{0:T(128)}, u32[]{:S(2)}) copy-start(s32[4]{0:T(128)} %counts_ref.3) | copy-start | bytes 52
  37.5 3.5 %copy-start.4 = (f32[256]{0:T(256)S(1)}, f32[256]{0:T(256)}, u32[]{:S(2)}) copy-start(f32[256]{0:T(256)} %param.15) | copy-start | bytes 3076
  37.5 3.5 %copy-start.5 = (f32[256]{0:T(256)S(1)}, f32[256]{0:T(256)}, u32[]{:S(2)}) copy-start(f32[256]{0:T(256)} %param.16) | copy-start | bytes 3076
  37.5 3.5 %copy-start.6 = (f32[256]{0:T(256)S(1)}, f32[256]{0:T(256)}, u32[]{:S(2)}) copy-start(f32[256]{0:T(256)} %param.17) | copy-start | bytes 3076
  37.5 3.5 %copy-start.7 = (f32[256]{0:T(256)S(1)}, f32[256]{0:T(256)}, u32[]{:S(2)}) copy-start(f32[256]{0:T(256)} %param.19) | copy-start | bytes 3076
  37.5 3.5 %copy-start.8 = (f32[256]{0:T(256)S(1)}, f32[256]{0:T(256)}, u32[]{:S(2)}) copy-start(f32[256]{0:T(256)} %param.20) | copy-start | bytes 3076
  37.5 3.5 %copy-start.9 = (f32[256]{0:T(256)S(1)}, f32[256]{0:T(256)}, u32[]{:S(2)}) copy-start(f32[256]{0:T(256)} %param.21) | copy-start | bytes 3076
  37.5 3.5 %copy-start.10 = (f32[256]{0:T(256)S(1)}, f32[256]{0:T(256)}, u32[]{:S(2)}) copy-start(f32[256]{0:T(256)} %param.23) | copy-start | bytes 3076
  37.7 2.9 %collective-permute-start.4 = (bf16[4,2,288,256]{3,2,1,0:T(8,128)(2,1)S(1)}, bf16[4,2,288,256]{3,2,1,0:T(8,128)(2,1)S(1)}, u32[]{:S(2)}, u32[]{:S(2)}) collective-permute-start(bf16[4,2,288,256]{3,2,1,0:T(8,128)(2,1)S(1)} %pad_maximum_fusion.same_ref), channel_id=1, source_target_pairs={{0,1},{1,0},{2,3},{3,2},{4,5},{5,4},{6,7},{7,6},{8,9},{9,8},{10,11... | collective-permute-start | bytes 3538952 | tf_op jit(solution)/shard_map/ppermute | solution.py:579
  37.8 3.2 %collective-permute-start = (bf16[32,16,256]{2,1,0:T(8,128)(2,1)S(1)}, bf16[32,16,256]{2,1,0:T(8,128)(2,1)S(1)}, u32[]{:S(2)}, u32[]{:S(2)}) collective-permute-start(bf16[32,16,256]{2,1,0:T(8,128)(2,1)S(1)} %slice_bitcast_fusion), channel_id=1, source_target_pairs={{0,1},{1,0},{2,3},{3,2},{4,5},{5,4},{6,7},{7,6},{8,9},{9,8},{10,11... | collective-permute-start | bytes 786440 | tf_op jit(solution)/shard_map/ppermute | solution.py:573
  41.0 2.0 %copy-start = (bf16[6912,256]{1,0:T(8,128)(2,1)S(1)}, bf16[6912,256]{1,0:T(8,128)(2,1)}, u32[]{:S(2)}) copy-start(bf16[6912,256]{1,0:T(8,128)(2,1)} %temporal_ref.1) | copy-start | bytes 10616836

commit v4 on v3

--- a/solution.py
+++ b/solution.py
@@ -324,24 +324,32 @@
     sent_ref[...] = whole_ref[:, pl.ds((1 - core) * half, half)]
 
 
-def pick_frames_body(counts_ref, video_ref, out_ref):
-    frames = video_ref.shape[0]
+def pick_frames_body(counts_ref, video_ref, out_ref, held_ref, placed_ref, held_sem, sems):
+    load = pltpu.make_async_copy(video_ref, held_ref, held_sem)
+    load.start()
+    frames, (parts, sent) = video_ref.shape[0], out_ref.shape[:2]
     n_owner = counts_ref.shape[0]
-    frames_sent = out_ref.shape[1]
-    n_pair = out_ref.shape[0] // (2 * n_owner)
-    each = frames_sent - 1
+    span, each = parts // n_owner, sent - 1
+    load.wait()
+    copies = []
     for owner in range(n_owner):
         offset = frame_offset(counts_ref, owner)
-        for pair in range(n_pair):
-            for core in range(2):
-                for place in range(frames_sent):
-                    first = 2 * each * pair
-                    slot = first + (2 * each - 1 - place if core else place - 2)
-                    frame = offset + slot
-                    values = video_ref[jnp.clip(frame, 0, frames - 1)]
-                    if slot < 0:
-                        values = jnp.where(frame >= 0, values, jnp.zeros_like(values))
-                    out_ref[(owner * n_pair + pair) * 2 + core, place] = values
+        for part in range(span):
+            pair, core = part // 2, part % 2
+            for place in range(sent):
+                slot = 2 * each * pair + (2 * each - 1 - place if core else place - 2)
+                frame = offset + slot
+                values = held_ref[jnp.clip(frame, 0, frames - 1)]
+                if slot < 0:
+                    values = jnp.where(frame >= 0, values, jnp.zeros_like(values))
+                placed_ref[owner * span + part, place] = values
+        rows = pl.ds(owner * span, span)
+        copies.append(
+            pltpu.make_async_copy(placed_ref.at[rows], out_ref.at[rows], sems.at[owner])
+        )
+        copies[-1].start()
+    for copy in copies:
+        copy.wait()
 
 
 def group_spread(values, width_group):
@@ -356,13 +364,18 @@
     return total
 
 
+def interleave(main, side, pace):
+    for _ in main:
+        for _ in range(pace):
+            next(side, None)
+    for _ in side:
+        pass
+
+
 def frames_body(
-    counts_ref, part_ref, swapped_ref, temporal_ref, same_ref, other_ref,
-    temporal_bias_ref, first_gain_ref, first_shift_ref, first_bias_ref,
-    second_gain_ref, second_shift_ref, second_bias_ref,
-    out_ref,
-    *refs,
+    counts_ref, part_ref, swapped_ref, temporal_ref, same_ref, other_ref, *refs
 ):
+    vectors, (out_ref, *refs) = refs[:7], refs[7:]
     n_height, each, rows, width, channels = out_ref.shape
     places = each + 2
     taps_refs, refs = refs[:places], refs[places:]
@@ -370,7 +383,9 @@
     total_refs, refs = refs[:each], refs[each:]
     blended_refs, refs = refs[:each], refs[each:]
     field_refs, refs = refs[:each], refs[each:]
-    landed_ref, raw_ref, time_ref, weights_ref, land_sems, time_sems, sems = refs
+    landed_refs, refs = refs[:places], refs[places:]
+    raw_ref, time_ref, weights_ref, done_ref, vectors_ref, held_ref, *refs = refs
+    land_sems, time_sems, sems, out_sems, vector_sems, held_sem = refs
     n_pair = n_height // 2
     n_frame = part_ref.shape[0] // n_height
     columns = width // n_frame
@@ -378,41 +393,46 @@
     depth = 3 * channels
     cells = all_rows * width
     width_group = channels // GROUPS
-    pair, core = lax.axis_index("pair"), lax.axis_index("core")
+    owner, pair, core = lax.axis_index("frame"), lax.axis_index("pair"), lax.axis_index("core")
     span = same_ref.shape[2]
-
     landings = [
         pltpu.make_async_copy(
             part_ref.at[:, place] if place <= each else swapped_ref,
-            landed_ref.at[place],
+            landed_refs[place],
             land_sems.at[place],
         )
         for place in range(places)
     ]
-    time_copies = [
-        pltpu.make_async_copy(
-            temporal_ref.at[pl.ds(tap * 3 * depth, 3 * depth)],
-            time_ref.at[tap],
-            time_sems.at[tap],
+    time_copies = []
+    for step in range(3):
+        tap = step + core * (2 - 2 * step)
+        begin = pl.multiple_of(tap * 3 * depth, 3 * depth)
+        time_copies.append(
+            pltpu.make_async_copy(
+                temporal_ref.at[pl.ds(begin, 3 * depth)], time_ref.at[step], time_sems.at[step]
+            )
         )
-        for tap in range(3)
+    vector_copies = [
+        pltpu.make_async_copy(ref, vectors_ref.at[line], vector_sems.at[line])
+        for line, ref in enumerate(vectors)
     ]
+    vector_copies.append(pltpu.make_async_copy(counts_ref, held_ref, held_sem))
     copies = []
     for which in range(2):
         of_weight = []
         for step in range(n_pair):
             source = lax.rem(pair - step + n_pair, n_pair)
             for side, (parts_ref, of_core) in enumerate(((same_ref, core), (other_ref, 1 - core))):
-                start = pl.multiple_of((source * 2 + of_core) * span, span)
+                begin = pl.multiple_of((source * 2 + of_core) * span, span)
                 of_weight.append(
                     pltpu.make_async_copy(
                         parts_ref.at[step, which],
-                        weights_ref.at[which, pl.ds(start, span)],
+                        weights_ref.at[which, pl.ds(begin, span)],
                         sems.at[which, step, side],
                     )
                 )
         copies.append(of_weight)
-    for copy in landings[:3] + time_copies + landings[3:] + copies[0] + copies[1]:
+    for copy in landings[:3] + time_copies + landings[3:] + vector_copies + copies[0] + copies[1]:
         copy.start()
 
     border = jnp.zeros((width, depth), BF16)
@@ -424,7 +444,8 @@
         landings[place].wait()
         for height in range(n_height):
             pieces = [
-                landed_ref[place, peer * n_height + height].astype(F32) for peer in range(n_frame)
+                landed_refs[place][peer * n_height + height].astype(F32)
+                for peer in range(n_frame)
             ]
             for row in range(rows):
                 values = jnp.concatenate(
@@ -432,28 +453,44 @@
                 )
                 raw_ref[place, height * rows + row] = values.astype(BF16)
                 taps_refs[place][height * rows + row + 1] = with_column_taps(silu(values))
-
-    def convolved(source_ref, weight_ref):
+            yield
+
+    parts_of_field = 2
+    part_rows = all_rows // parts_of_field
+    part_cells = part_rows * width
+
+    def products(source_ref, weight_ref, part):
         summed = None
         for row_tap in range(3):
+            low = part * part_rows + row_tap
             product = jnp.dot(
-                source_ref[row_tap : row_tap + all_rows].reshape(cells, depth),
+                source_ref[low : low + part_rows].reshape(part_cells, depth),
                 weight_ref[row_tap * depth : (row_tap + 1) * depth],
                 preferred_element_type=F32,
             )
             summed = product if summed is None else summed + product
-        return summed
+            yield summed
 
     def temporal(place):
         for step in range(3):
-            tap = step + core * (2 - 2 * step)
-            product = convolved(taps_refs[place + step], time_ref.at[tap])
-            if step == 0:
-                total_refs[place][...] = product
-            else:
-                total_refs[place][...] += product
-
-    def field_and_scale(field_ref, row_of, gain_ref, shift_ref):
+            if place == 0:
+                time_copies[step].wait()
+            for part in range(parts_of_field):
+                for summed in products(taps_refs[place + step], time_ref.at[step], part):
+                    yield
+                cut = slice(part * part_cells, (part + 1) * part_cells)
+                if step == 0:
+                    total_refs[place][cut] = summed
+                else:
+                    total_refs[place][cut] += summed
+
+    def convolve(place, which):
+        for part in range(parts_of_field):
+            for summed in products(normed_refs[place], weights_ref.at[which], part):
+                yield
+            total_refs[place][part * part_cells : (part + 1) * part_cells] = summed
+
+    def norm(place, field_ref, row_of, gain, shift):
         pivot = None
         sums = squares = jnp.zeros((8, channels), F32)
         for row in range(all_rows):
@@ -465,80 +502,90 @@
             apart = (values - pivot).reshape(width // 8, 8, channels)
             sums = sums + jnp.sum(apart, axis=0)
             squares = squares + jnp.sum(apart * apart, axis=0)
-        sums = jnp.sum(sums, axis=0, keepdims=True)
-        squares = jnp.sum(squares, axis=0, keepdims=True)
-        own = sums * (1.0 / cells)
+            if row % 4 == 3:
+                yield
+        own = jnp.sum(sums, axis=0, keepdims=True) * (1.0 / cells)
+        squares = jnp.sum(squares, axis=0, keepdims=True) * (1.0 / cells)
         sample = 1.0 / width_group
         mean = group_spread(own + pivot, width_group) * sample
         off = own + pivot - mean
-        spread = squares * (1.0 / cells) - own * own + off * off
+        spread = squares - own * own + off * off
         variance = jnp.maximum(group_spread(spread, width_group) * sample, 0.0)
-        scale = lax.rsqrt(variance + EPS) * gain_ref[...]
-        return 0.5 * scale, 0.5 * (shift_ref[...] - mean * scale)
-
-    def norm(place, field_ref, row_of, gain_ref, shift_ref):
-        scale, offset = field_and_scale(field_ref, row_of, gain_ref, shift_ref)
+        scale = lax.rsqrt(variance + EPS) * gain
+        offset = 0.5 * (shift - mean * scale)
+        scale = 0.5 * scale
+        yield
         for row in range(all_rows):
             half = field_ref[row].astype(F32) * scale + offset
             normed_refs[place][row + 1] = with_column_taps(half + half * jnp.tanh(half))
+            if row % 2 == 1:
+                yield
 
     def first_norm(place):
         raw_at = place + 2 - 2 * core
 
         def row_of(row):
             product = total_refs[place][row * width : (row + 1) * width]
-            return raw_ref[raw_at, row].astype(F32) + product + temporal_bias_ref[...]
-
-        norm(place, blended_refs[place], row_of, first_gain_ref, first_shift_ref)
-
-    count = counts_ref[lax.axis_index("frame")]
-
-    def first_conv(place):
-        total_refs[place][...] = convolved(normed_refs[place], weights_ref.at[0])
+            return raw_ref[raw_at, row].astype(F32) + product + temporal_bias
+
+        return norm(place, blended_refs[place], row_of, first_gain, first_shift)
 
     def second_norm(place):
         def row_of(row):
-            return total_refs[place][row * width : (row + 1) * width] + first_bias_ref[...]
-
-        norm(place, field_refs[place], row_of, second_gain_ref, second_shift_ref)
-
-    def second_conv(place):
-        total_refs[place][...] = convolved(normed_refs[place], weights_ref.at[1])
+            return total_refs[place][row * width : (row + 1) * width] + first_bias
+
+        return norm(place, field_refs[place], row_of, second_gain, second_shift)
 
     def finish(place):
+        count = held_ref[owner]
         at = place + core * (each - 1 - 2 * place)
         live = pair * 2 * each + core * each + at < count
         for row in range(all_rows):
-            product = total_refs[place][row * width : (row + 1) * width] + second_bias_ref[...]
+            product = total_refs[place][row * width : (row + 1) * width] + second_bias
             decoded = blended_refs[place][row].astype(F32) + product
-            out_ref[row // rows, at, row % rows] = jnp.where(live, decoded, 0.0).astype(BF16)
+            done_ref[place, row // rows, row % rows] = jnp.where(live, decoded, 0.0).astype(BF16)
+            if row % 4 == 3:
+                yield
+        store = pltpu.make_async_copy(
+            done_ref.at[place], out_ref.at[:, at], out_sems.at[place]
+        )
+        store.start()
+        stores.append(store)
+
+    stores = []
 
     def ready(which):
         for copy in which:
             copy.wait()
 
+    def both(one, other):
+        yield from one
+        yield from other
+
+    nothing = iter(())
     for place in range(3):
-        lay(place)
-    ready(time_copies)
-    temporal(0)
+        interleave(lay(place), nothing, 0)
+    laying = nothing
     for place in range(3, places):
-        lay(place)
+        laying = both(laying, lay(place))
+    interleave(temporal(0), laying, 1)
+    ready(vector_copies)
+    (
+        temporal_bias, first_gain, first_shift, first_bias, second_gain, second_shift, second_bias
+    ) = [vectors_ref[line] for line in range(7)]
     for place in range(1, each):
-        temporal(place)
-        first_norm(place - 1)
+        interleave(temporal(place), first_norm(place - 1), 1)
     ready(copies[0])
+    pending = first_norm(each - 1)
+    for place in range(each):
+        interleave(convolve(place, 0), pending, 3)
+        pending = second_norm(place)
     ready(copies[1])
-    first_norm(each - 1)
     for place in range(each):
-        first_conv(place)
-        if place > 0:
-            second_norm(place - 1)
-    second_norm(each - 1)
-    for place in range(each):
-        second_conv(place)
-        if place > 0:
-            finish(place - 1)
-    finish(each - 1)
+        interleave(convolve(place, 1), pending, 3)
+        pending = finish(place)
+    interleave(pending, nothing, 0)
+    ready(stores)
 
 
 def ring(size, step):
@@ -556,7 +603,7 @@
     all_rows = rows * n_height
     capacity = slots_of(frames, n_frame)
     each = -(-capacity // n_height)
-    params = pltpu.CompilerParams(vmem_limit_bytes=40 * 1024 * 1024)
+    params = pltpu.CompilerParams(vmem_limit_bytes=60 * 1024 * 1024)
     swap = [(0, 1), (1, 0)]
 
     picked = pl.pallas_call(
@@ -564,8 +611,14 @@
         out_shape=jax.ShapeDtypeStruct(
             (n_frame * n_height, each + 1, rows * columns, channels), BF16
         ),
-        in_specs=[SMEM, VMEM],
-        out_specs=VMEM,
+        in_specs=[SMEM, HBM],
+        out_specs=HBM,
+        scratch_shapes=[
+            pltpu.VMEM((frames, rows * columns, channels), BF16),
+            pltpu.VMEM((n_frame * n_height, each + 1, rows * columns, channels), BF16),
+            pltpu.SemaphoreType.DMA(()),
+            pltpu.SemaphoreType.DMA((n_frame,)),
+        ],
         compiler_params=params,
         name="pick",
     )(frame_counts, video.reshape(frames, rows * columns, channels))
@@ -578,33 +631,39 @@
     )
     other = lax.ppermute(same, "core", swap)
 
-    def row_of(vector):
-        return vector.reshape(1, channels)
-
-    taps = (width, 3 * channels)
+    vectors = (
+        temporal_bias, first_gain, first_shift, first_bias, second_gain, second_shift, second_bias
+    )
+    field = (all_rows, width, channels)
+    taps = (all_rows + 2, width, 3 * channels)
     decoded = pl.pallas_call(
         frames_body,
         out_shape=jax.ShapeDtypeStruct((n_height, each, rows, width, channels), BF16),
-        in_specs=[SMEM] + [HBM] * 5 + [VMEM] * 7,
-        out_specs=VMEM,
-        scratch_shapes=[pltpu.VMEM((all_rows + 2,) + taps, BF16)] * (2 * each + 2)
+        in_specs=[HBM] * 13,
+        out_specs=HBM,
+        scratch_shapes=[pltpu.VMEM(taps, BF16)] * (2 * each + 2)
         + [pltpu.VMEM((all_rows * width, channels), F32)] * each
-        + [pltpu.VMEM((all_rows, width, channels), BF16)] * (2 * each)
+        + [pltpu.VMEM(field, BF16)] * (2 * each)
+        + [pltpu.VMEM((n_frame * n_height, rows * columns, channels), BF16)] * (each + 2)
         + [
-            pltpu.VMEM((each + 2, n_frame * n_height, rows * columns, channels), BF16),
-            pltpu.VMEM((each + 2, all_rows, width, channels), BF16),
+            pltpu.VMEM((each + 2,) + field, BF16),
             pltpu.VMEM((3, 9 * channels, channels), BF16),
             pltpu.VMEM((2, 9 * channels, channels), BF16),
+            pltpu.VMEM((each, n_height, rows, width, channels), BF16),
+            pltpu.VMEM((7, 1, channels), F32),
+            pltpu.SMEM(frame_counts.shape, jnp.int32),
             pltpu.SemaphoreType.DMA((each + 2,)),
             pltpu.SemaphoreType.DMA((3,)),
             pltpu.SemaphoreType.DMA((2, n_pair, 2)),
+            pltpu.SemaphoreType.DMA((each,)),
+            pltpu.SemaphoreType.DMA((7,)),
+            pltpu.SemaphoreType.DMA(()),
         ],
         compiler_params=params,
         name="frames",
     )(
         frame_counts, parts, swapped, temporal_weight, same, other,
-        row_of(temporal_bias), row_of(first_gain), row_of(first_shift), row_of(first_bias),
-        row_of(second_gain), row_of(second_shift), row_of(second_bias),
+        *[vector.reshape(1, channels) for vector in vectors],
     )
     owned = lax.all_to_all(decoded, ("pair", "core"), split_axis=0, concat_axis=0)
     return owned.reshape((n_height * each,) + owned.shape[2:])[:capacity]

time: 78.8 us -> 73.7 us (0.935)
  local copies, waits for them, and re-layouts: 4.54 us -> 1.62 us
  Pallas kernels: 20.6 us -> 18.2 us
    pallas_call x1, Pallas kernels: 18.9 us -> 15.5 us  [whole_frames(): pl.pallas_call(frames_body, out_shape=jax.ShapeDtypeStruct((n_height, eac...]
    unnamed x26 -> x12, local copies, waits for them, and re-layouts: 3.65 us -> 0.73 us
    pallas_call x1, Pallas kernels: 1.7 us -> 2.65 us  [whole_frames(): pl.pallas_call(pick_frames_body, out_shape=jax.ShapeDtypeStruct((n_frame...]
where the time goes in v4:
time: 73.7 us; the launch traced here: 73.4 us
  waiting for transfers between devices  24.6 us (33%)
  Pallas kernels  18.2 us (25%)
  blocking collectives  16 us (22%)
  starting transfers between devices  12.7 us (17%)
  local copies, waits for them, and re-layouts  1.62 us (2%)
    ppermute x3, waiting for transfers between devices, whole_frames(): lax.ppermute(own, 'pair', ring(n_pair, step))  22 us
    all_to_all x1, blocking collectives, whole_frames(): lax.all_to_all(decoded, ('pair', 'core'), split_axis=0, concat_axis=0)  16 us
    pallas_call x1, Pallas kernels, whole_frames(): pl.pallas_call(frames_body, out_shape=jax.ShapeDtypeStruct((n_height, eac...  15.5 us
    all_to_all x1, starting transfers between devices, whole_frames(): lax.all_to_all(picked, ('frame', 'pair', 'core'), split_axis=0, concat_ax...  7.3 us
    ppermute x3, starting transfers between devices, whole_frames(): lax.ppermute(own, 'pair', ring(n_pair, step))  4.76 us
    pallas_call x1, Pallas kernels, whole_frames(): pl.pallas_call(pick_frames_body, out_shape=jax.ShapeDtypeStruct((n_frame...  2.65 us
    ppermute x1, waiting for transfers between devices, whole_frames(): other = lax.ppermute(same, 'core', swap)  2.24 us
  transfers between devices with their start and end apart: 6, of which 4 were waited for; matrix products, arithmetic and copies ran while one was open for 0% of the time, Pallas kernels for 0%

profile of v4, /device:TPU:0, one launch (start us, length us, event | category | flops | bytes accessed | tf_op | source)
XLA Modules:
  0.0 73.4 jit_solution(11738424902998051231)
XLA Ops:
  0.0 2.6 %pick.1 = bf16[32,4,16,256]{3,2,1,0:T(8,128)(2,1)} custom-call(s32[4]{0:T(128)} %counts_ref.3, bf16[33,16,256]{2,1,0:T(8,128)(2,1)} %bitcast.23), custom_call_target="tpu_custom_call" | custom-call | tf_op jit(solution)/shard_map/pick/pallas_call | solution.py:609
  2.7 0.0 copy-start.4
  2.7 0.0 copy-start.5
  2.7 7.3 %all-to-all-start = ((bf16[32,4,16,256]{3,2,1,0:T(8,128)(2,1)}), bf16[32,4,16,256]{3,2,1,0:T(8,128)(2,1)S(1)}, u32[]{:S(2)}, u32[]{:S(2)}) async-start(bf16[32,4,16,256]{3,2,1,0:T(8,128)(2,1)} %pick.1), calls=%async_computation | async-start | bytes 2097152 | tf_op jit(solution)/shard_map/all_to_all | solution.py:625
  10.0 0.0 copy-done.4
  10.0 0.0 copy-done.5
  10.1 1.8 %collective-permute-start.2 = (bf16[2,288,256]{2,1,0:T(8,128)(2,1)S(1)}, bf16[2,288,256]{2,1,0:T(8,128)(2,1)S(1)}, u32[]{:S(2)}, u32[]{:S(2)}) collective-permute-start(bf16[2,288,256]{2,1,0:T(8,128)(2,1)S(1)} %get-tuple-element.6), channel_id=1, source_target_pairs={{0,4},{2,6},{4,0},{6,2},{1,5},{3,7},{5,1},{7,3},{8,12},{10,14},{12... | collective-permute-start | bytes 884744 | tf_op jit(solution)/shard_map/ppermute | solution.py:630
  11.9 1.5 %collective-permute-start.1 = (bf16[2,288,256]{2,1,0:T(8,128)(2,1)S(1)}, bf16[2,288,256]{2,1,0:T(8,128)(2,1)S(1)}, u32[]{:S(2)}, u32[]{:S(2)}) collective-permute-start(bf16[2,288,256]{2,1,0:T(8,128)(2,1)S(1)} %get-tuple-element.6), channel_id=1, source_target_pairs={{0,2},{2,4},{4,6},{6,0},{1,3},{3,5},{5,7},{7,1},{8,10},{10,12},{12... | collective-permute-start | bytes 884744 | tf_op jit(solution)/shard_map/ppermute | solution.py:630
  13.4 1.5 %collective-permute-start.3 = (bf16[2,288,256]{2,1,0:T(8,128)(2,1)S(1)}, bf16[2,288,256]{2,1,0:T(8,128)(2,1)S(1)}, u32[]{:S(2)}, u32[]{:S(2)}) collective-permute-start(bf16[2,288,256]{2,1,0:T(8,128)(2,1)S(1)} %get-tuple-element.6), channel_id=1, source_target_pairs={{0,6},{2,0},{4,2},{6,4},{1,7},{3,1},{5,3},{7,5},{8,14},{10,8},{12,... | collective-permute-start | bytes 884744 | tf_op jit(solution)/shard_map/ppermute | solution.py:630
  14.8 21.9 %collective-permute-done.2 = bf16[2,288,256]{2,1,0:T(8,128)(2,1)S(1)} collective-permute-done((bf16[2,288,256]{2,1,0:T(8,128)(2,1)S(1)}, bf16[2,288,256]{2,1,0:T(8,128)(2,1)S(1)}, u32[]{:S(2)}, u32[]{:S(2)}) %collective-permute-start.2) | collective-permute-done | bytes 294944 | tf_op jit(solution)/shard_map/ppermute | solution.py:630
  36.7 0.0 collective-permute-done.1
  36.7 0.1 collective-permute-done.3
  36.8 0.1 pad_maximum_fusion.same_ref
  37.0 0.0 copy-start.1
  37.0 0.1 collective-permute-start.4
  37.1 0.0 all-to-all-done.part_ref
  37.1 0.0 copy-start
  37.1 0.5 collective-permute-start
  37.7 2.2 %collective-permute-done.4.other_ref = bf16[4,2,288,256]{3,2,1,0:T(8,128)(2,1)S(1)} collective-permute-done((bf16[4,2,288,256]{3,2,1,0:T(8,128)(2,1)S(1)}, bf16[4,2,288,256]{3,2,1,0:T(8,128)(2,1)S(1)}, u32[]{:S(2)}, u32[]{:S(2)}) %collective-permute-start.4) | collective-permute-done | bytes 1179680 | tf_op jit(solution)/shard_map/ppermute | solution.py:632
  39.9 0.0 copy-start.2
  39.9 0.4 collective-permute-done.swapped_ref
  40.3 0.0 copy-start.3
  40.3 0.0 copy-done.1
  40.3 0.0 copy-done
  40.3 0.6 copy-done.2
  40.9 0.1 copy-done.3
  41.0 15.5 %frames.1 = bf16[8,3,2,32,256]{4,3,2,1,0:T(8,128)(2,1)} custom-call(s32[4]{0:T(128)} %counts_ref.3, bf16[32,4,16,256]{3,2,1,0:T(8,128)(2,1)} %copy-done, bf16[32,16,256]{2,1,0:T(8,128)(2,1)} %copy-done.3, bf16[6912,256]{1,0:T(8,128)(2,1)} %temporal_ref.1, bf16[4,2,288,256]{3,2,1,0:T(8,128)(2,1)} %copy-done.1, bf16[4,2,288,256]{3,2,1,0:T(8,128)(2,1)} %copy-done.2, ...), custom_call_target="tpu_custom_call" | custom-call | tf_op jit(solution)/shard_map/frames/pallas_call | solution.py:639
  56.5 16.0 %all_to_all.10 = bf16[8,3,2,32,256]{4,3,2,1,0:T(8,128)(2,1)S(1)} all-to-all(bf16[8,3,2,32,256]{4,3,2,1,0:T(8,128)(2,1)} %frames.1), channel_id=1, replica_groups=mesh['frame'=4,'pair'=4,'core'=2] {'pair','core'}, dimensions={0} | all-to-all | bytes 1572864 | tf_op jit(solution)/shard_map/all_to_all | solution.py:668
  72.6 0.9 %slice.13 = bf16[6,3,2,32,256]{4,3,2,1,0:T(8,128)(2,1)} slice(bf16[8,3,2,32,256]{4,3,2,1,0:T(8,128)(2,1)S(1)} %all_to_all.10), slice={[0:6], [0:3], [0:2], [0:32], [0:256]} | slice | bytes 1179648 | tf_op jit(solution)/shard_map/slice | solution.py:669
  (2 shorter events, 0.1 us)
Async XLA Ops:
  2.7 7.3 %copy-start.4 = (bf16[288,256]{1,0:T(8,128)(2,1)S(1)}, bf16[288,256]{1,0:T(8,128)(2,1)}, u32[]{:S(2)}) copy-start(bf16[288,256]{1,0:T(8,128)(2,1)} %param.22) | copy-start | bytes 442372
  2.7 7.3 %copy-start.5 = (bf16[288,256]{1,0:T(8,128)(2,1)S(1)}, bf16[288,256]{1,0:T(8,128)(2,1)}, u32[]{:S(2)}) copy-start(bf16[288,256]{1,0:T(8,128)(2,1)} %param.18) | copy-start | bytes 442372
  2.7 34.4 %all-to-all-start = ((bf16[32,4,16,256]{3,2,1,0:T(8,128)(2,1)}), bf16[32,4,16,256]{3,2,1,0:T(8,128)(2,1)S(1)}, u32[]{:S(2)}, u32[]{:S(2)}) async-start(bf16[32,4,16,256]{3,2,1,0:T(8,128)(2,1)} %pick.1), calls=%async_computation | async-start | bytes 2097152 | tf_op jit(solution)/shard_map/all_to_all | solution.py:625
  10.1 26.7 %collective-permute-start.2 = (bf16[2,288,256]{2,1,0:T(8,128)(2,1)S(1)}, bf16[2,288,256]{2,1,0:T(8,128)(2,1)S(1)}, u32[]{:S(2)}, u32[]{:S(2)}) collective-permute-start(bf16[2,288,256]{2,1,0:T(8,128)(2,1)S(1)} %get-tuple-element.6), channel_id=1, source_target_pairs={{0,4},{2,6},{4,0},{6,2},{1,5},{3,7},{5,1},{7,3},{8,12},{10,14},{12... | collective-permute-start | bytes 884744 | tf_op jit(solution)/shard_map/ppermute | solution.py:630
  11.9 24.8 %collective-permute-start.1 = (bf16[2,288,256]{2,1,0:T(8,128)(2,1)S(1)}, bf16[2,288,256]{2,1,0:T(8,128)(2,1)S(1)}, u32[]{:S(2)}, u32[]{:S(2)}) collective-permute-start(bf16[2,288,256]{2,1,0:T(8,128)(2,1)S(1)} %get-tuple-element.6), channel_id=1, source_target_pairs={{0,2},{2,4},{4,6},{6,0},{1,3},{3,5},{5,7},{7,1},{8,10},{10,12},{12... | collective-permute-start | bytes 884744 | tf_op jit(solution)/shard_map/ppermute | solution.py:630
  13.4 23.5 %collective-permute-start.3 = (bf16[2,288,256]{2,1,0:T(8,128)(2,1)S(1)}, bf16[2,288,256]{2,1,0:T(8,128)(2,1)S(1)}, u32[]{:S(2)}, u32[]{:S(2)}) collective-permute-start(bf16[2,288,256]{2,1,0:T(8,128)(2,1)S(1)} %get-tuple-element.6), channel_id=1, source_target_pairs={{0,6},{2,0},{4,2},{6,4},{1,7},{3,1},{5,3},{7,5},{8,14},{10,8},{12,... | collective-permute-start | bytes 884744 | tf_op jit(solution)/shard_map/ppermute | solution.py:630
  37.0 3.3 %copy-start.1 = (bf16[4,2,288,256]{3,2,1,0:T(8,128)(2,1)}, bf16[4,2,288,256]{3,2,1,0:T(8,128)(2,1)S(1)}, u32[]{:S(2)}) copy-start(bf16[4,2,288,256]{3,2,1,0:T(8,128)(2,1)S(1)} %pad_maximum_fusion.same_ref) | copy-start | bytes 3538948
  37.0 2.9 %collective-permute-start.4 = (bf16[4,2,288,256]{3,2,1,0:T(8,128)(2,1)S(1)}, bf16[4,2,288,256]{3,2,1,0:T(8,128)(2,1)S(1)}, u32[]{:S(2)}, u32[]{:S(2)}) collective-permute-start(bf16[4,2,288,256]{3,2,1,0:T(8,128)(2,1)S(1)} %pad_maximum_fusion.same_ref), channel_id=1, source_target_pairs={{0,1},{1,0},{2,3},{3,2},{4,5},{5,4},{6,7},{7,6},{8,9},{9,8},{10,11... | collective-permute-start | bytes 3538952 | tf_op jit(solution)/shard_map/ppermute | solution.py:632
  37.1 3.2 %copy-start = (bf16[32,4,16,256]{3,2,1,0:T(8,128)(2,1)}, bf16[32,4,16,256]{3,2,1,0:T(8,128)(2,1)S(1)}, u32[]{:S(2)}) copy-start(bf16[32,4,16,256]{3,2,1,0:T(8,128)(2,1)S(1)} %all-to-all-done.part_ref) | copy-start | bytes 3145732
  37.1 3.2 %collective-permute-start = (bf16[32,16,256]{2,1,0:T(8,128)(2,1)S(1)}, bf16[32,16,256]{2,1,0:T(8,128)(2,1)S(1)}, u32[]{:S(2)}, u32[]{:S(2)}) collective-permute-start(bf16[32,16,256]{2,1,0:T(8,128)(2,1)S(1)} %slice_bitcast_fusion), channel_id=1, source_target_pairs={{0,1},{1,0},{2,3},{3,2},{4,5},{5,4},{6,7},{7,6},{8,9},{9,8},{10,11... | collective-permute-start | bytes 786440 | tf_op jit(solution)/shard_map/ppermute | solution.py:626
  39.9 1.0 %copy-start.2 = (bf16[4,2,288,256]{3,2,1,0:T(8,128)(2,1)}, bf16[4,2,288,256]{3,2,1,0:T(8,128)(2,1)S(1)}, u32[]{:S(2)}) copy-start(bf16[4,2,288,256]{3,2,1,0:T(8,128)(2,1)S(1)} %collective-permute-done.4.other_ref) | copy-start | bytes 3538948
  40.3 0.7 copy-start.3

commit v5 on v4

--- a/solution.py
+++ b/solution.py
@@ -324,23 +324,39 @@
     sent_ref[...] = whole_ref[:, pl.ds((1 - core) * half, half)]
 
 
-def pick_frames_body(counts_ref, video_ref, out_ref, held_ref, placed_ref, held_sem, sems):
+def extremes(counts_ref):
+    most = least = jnp.int32(0)
+    high = low = counts_ref[0]
+    for owner in range(1, counts_ref.shape[0]):
+        count = counts_ref[owner]
+        most, high = jnp.where(count > high, owner, most), jnp.maximum(count, high)
+        least, low = jnp.where(count < low, owner, least), jnp.minimum(count, low)
+    return most, least
+
+
+def pick_frames_body(
+    capacity, counts_ref, video_ref, out_ref, held_ref, placed_ref, held_sem, sems
+):
     load = pltpu.make_async_copy(video_ref, held_ref, held_sem)
     load.start()
     frames, (parts, sent) = video_ref.shape[0], out_ref.shape[:2]
     n_owner = counts_ref.shape[0]
     span, each = parts // n_owner, sent - 1
+    most, least = extremes(counts_ref)
+    last = frame_offset(counts_ref, most) + (capacity - 2 * each)
     load.wait()
     copies = []
     for owner in range(n_owner):
         offset = frame_offset(counts_ref, owner)
         for part in range(span):
             pair, core = part // 2, part % 2
+            base = offset + 2 * each * pair
+            if pair == span // 2 - 1:
+                base = jnp.where(least == owner, last, base)
             for place in range(sent):
-                slot = 2 * each * pair + (2 * each - 1 - place if core else place - 2)
-                frame = offset + slot
+                frame = base + (2 * each - 1 - place if core else place - 2)
                 values = held_ref[jnp.clip(frame, 0, frames - 1)]
-                if slot < 0:
+                if not core and place < 2:
                     values = jnp.where(frame >= 0, values, jnp.zeros_like(values))
                 placed_ref[owner * span + part, place] = values
         rows = pl.ds(owner * span, span)
@@ -373,7 +389,7 @@
 
 
 def frames_body(
-    counts_ref, part_ref, swapped_ref, temporal_ref, same_ref, other_ref, *refs
+    part_ref, swapped_ref, temporal_ref, same_ref, other_ref, *refs
 ):
     vectors, (out_ref, *refs) = refs[:7], refs[7:]
     n_height, each, rows, width, channels = out_ref.shape
@@ -384,8 +400,8 @@
     blended_refs, refs = refs[:each], refs[each:]
     field_refs, refs = refs[:each], refs[each:]
     landed_refs, refs = refs[:places], refs[places:]
-    raw_ref, time_ref, weights_ref, done_ref, vectors_ref, held_ref, *refs = refs
-    land_sems, time_sems, sems, out_sems, vector_sems, held_sem = refs
+    raw_ref, time_ref, weights_ref, done_ref, vectors_ref, *refs = refs
+    land_sems, time_sems, sems, out_sems, vector_sems = refs
     n_pair = n_height // 2
     n_frame = part_ref.shape[0] // n_height
     columns = width // n_frame
@@ -393,7 +409,7 @@
     depth = 3 * channels
     cells = all_rows * width
     width_group = channels // GROUPS
-    owner, pair, core = lax.axis_index("frame"), lax.axis_index("pair"), lax.axis_index("core")
+    pair, core = lax.axis_index("pair"), lax.axis_index("core")
     span = same_ref.shape[2]
     landings = [
         pltpu.make_async_copy(
@@ -416,7 +432,6 @@
         pltpu.make_async_copy(ref, vectors_ref.at[line], vector_sems.at[line])
         for line, ref in enumerate(vectors)
     ]
-    vector_copies.append(pltpu.make_async_copy(counts_ref, held_ref, held_sem))
     copies = []
     for which in range(2):
         of_weight = []
@@ -537,13 +552,11 @@
         return norm(place, field_refs[place], row_of, second_gain, second_shift)
 
     def finish(place):
-        count = held_ref[owner]
         at = place + core * (each - 1 - 2 * place)
-        live = pair * 2 * each + core * each + at < count
         for row in range(all_rows):
             product = total_refs[place][row * width : (row + 1) * width] + second_bias
             decoded = blended_refs[place][row].astype(F32) + product
-            done_ref[place, row // rows, row % rows] = jnp.where(live, decoded, 0.0).astype(BF16)
+            done_ref[place, row // rows, row % rows] = decoded.astype(BF16)
             if row % 4 == 3:
                 yield
         store = pltpu.make_async_copy(
@@ -602,12 +615,13 @@
     width = columns * n_frame
     all_rows = rows * n_height
     capacity = slots_of(frames, n_frame)
-    each = -(-capacity // n_height)
+    each = capacity // n_height
+    extra = capacity - each * n_height
     params = pltpu.CompilerParams(vmem_limit_bytes=60 * 1024 * 1024)
     swap = [(0, 1), (1, 0)]
 
     picked = pl.pallas_call(
-        pick_frames_body,
+        functools.partial(pick_frames_body, capacity),
         out_shape=jax.ShapeDtypeStruct(
             (n_frame * n_height, each + 1, rows * columns, channels), BF16
         ),
@@ -639,7 +653,7 @@
     decoded = pl.pallas_call(
         frames_body,
         out_shape=jax.ShapeDtypeStruct((n_height, each, rows, width, channels), BF16),
-        in_specs=[HBM] * 13,
+        in_specs=[HBM] * 12,
         out_specs=HBM,
         scratch_shapes=[pltpu.VMEM(taps, BF16)] * (2 * each + 2)
         + [pltpu.VMEM((all_rows * width, channels), F32)] * each
@@ -651,22 +665,42 @@
             pltpu.VMEM((2, 9 * channels, channels), BF16),
             pltpu.VMEM((each, n_height, rows, width, channels), BF16),
             pltpu.VMEM((7, 1, channels), F32),
-            pltpu.SMEM(frame_counts.shape, jnp.int32),
             pltpu.SemaphoreType.DMA((each + 2,)),
             pltpu.SemaphoreType.DMA((3,)),
             pltpu.SemaphoreType.DMA((2, n_pair, 2)),
             pltpu.SemaphoreType.DMA((each,)),
             pltpu.SemaphoreType.DMA((7,)),
-            pltpu.SemaphoreType.DMA(()),
         ],
-        compiler_params=params,
+        compiler_params=pltpu.CompilerParams(vmem_limit_bytes=52 * 1024 * 1024),
         name="frames",
     )(
-        frame_counts, parts, swapped, temporal_weight, same, other,
+        parts, swapped, temporal_weight, same, other,
         *[vector.reshape(1, channels) for vector in vectors],
     )
     owned = lax.all_to_all(decoded, ("pair", "core"), split_axis=0, concat_axis=0)
-    return owned.reshape((n_height * each,) + owned.shape[2:])[:capacity]
+    owned = owned.reshape((n_height * each,) + owned.shape[2:])
+    if extra:
+        most, least = jnp.argmax(frame_counts), jnp.argmin(frame_counts)
+
+        def homeward(route):
+            source, target = route % n_frame, route // n_frame
+            if source == target:
+                return jnp.zeros_like
+            return lambda rows: lax.ppermute(rows, "frame", [(source, target)])
+
+        owned = jnp.concatenate(
+            [
+                owned,
+                lax.switch(
+                    most * n_frame + least,
+                    [homeward(route) for route in range(n_frame * n_frame)],
+                    owned[-extra:],
+                ),
+            ]
+        )
+    mine = lax.dynamic_index_in_dim(frame_counts, lax.axis_index("frame"), keepdims=False)
+    live = jnp.arange(capacity) < mine
+    return jnp.where(live[:, None, None, None], owned, jnp.zeros_like(owned))
 
 
 def split_rows(
@@ -814,8 +848,13 @@
 
 
 def per_device(video, *rest):
+    frames, n_frame = video.shape[0], lax.axis_size("frame")
     n_height = lax.axis_size("pair") * lax.axis_size("core")
-    if slots_of(video.shape[0], lax.axis_size("frame")) >= n_height:
+    capacity = slots_of(frames, n_frame)
+    each, extra = divmod(capacity, n_height)
+    room = each * (n_height - 2)
+    fits = each > 0 and extra <= 2 * each and n_frame > 1
+    if fits and 2 * (each * n_height + 1) > frames and frames - capacity < n_frame * room:
         return whole_frames(video, *rest)
     return split_rows(video, *rest)
 

time: 73.7 us -> 70 us (0.950)
  the two profiles are of different devices: /device:TPU:0 before, /device:TPU:24 now
where the time goes in v5:
time: 70 us; the launch traced here: 69.7 us
  waiting for transfers between devices  36.2 us (52%)
  starting transfers between devices  14.9 us (21%)
  Pallas kernels  12.5 us (18%)
  other arithmetic  3.96 us (6%)
  between operations  1.41 us (2%)
    ppermute x3, waiting for transfers between devices, whole_frames(): lax.ppermute(own, 'pair', ring(n_pair, step))  20.9 us
    pallas_call x1, Pallas kernels, whole_frames(): pl.pallas_call(frames_body, out_shape=jax.ShapeDtypeStruct((n_height, eac...  9.84 us
    ppermute x1, waiting for transfers between devices, homeward(): return lambda rows: lax.ppermute(rows, 'frame', [(source, target)])  6.76 us
    all_to_all x1, starting transfers between devices, whole_frames(): lax.all_to_all(picked, ('frame', 'pair', 'core'), split_axis=0, concat_ax...  5.87 us
    all_to_all x1, waiting for transfers between devices, whole_frames(): lax.all_to_all(decoded, ('pair', 'core'), split_axis=0, concat_axis=0)  5.85 us
    ppermute x3, starting transfers between devices, whole_frames(): lax.ppermute(own, 'pair', ring(n_pair, step))  3.57 us
    all_to_all x1, starting transfers between devices, whole_frames(): lax.all_to_all(decoded, ('pair', 'core'), split_axis=0, concat_axis=0)  3.51 us
    ppermute x1, waiting for transfers between devices, whole_frames(): other = lax.ppermute(same, 'core', swap)  2.75 us
  transfers between devices with their start and end apart: 8, of which 5 were waited for; matrix products, arithmetic and copies ran while one was open for 4% of the time, Pallas kernels for 0%

profile of v5, /device:TPU:24, one launch (start us, length us, event | category | flops | bytes accessed | tf_op | source)
XLA Modules:
  0.0 69.7 jit_solution(3504435127974034884)
XLA Ops:
  0.0 0.0 copy-start.8
  0.0 0.0 copy-start.9
  0.0 2.7 %pick.1 = bf16[32,3,16,256]{3,2,1,0:T(8,128)(2,1)} custom-call(s32[4]{0:T(128)} %counts_ref.1, bf16[33,16,256]{2,1,0:T(8,128)(2,1)} %bitcast.56), custom_call_target="tpu_custom_call" | custom-call | tf_op jit(solution)/shard_map/pick/pallas_call | solution.py:623
  2.7 5.9 %all-to-all-start = ((bf16[32,3,16,256]{3,2,1,0:T(8,128)(2,1)}), bf16[32,3,16,256]{3,2,1,0:T(8,128)(2,1)S(1)}, u32[]{:S(2)}, u32[]{:S(2)}) async-start(bf16[32,3,16,256]{3,2,1,0:T(8,128)(2,1)} %pick.1), calls=%async_computation | async-start | bytes 1572864 | tf_op jit(solution)/shard_map/all_to_all | solution.py:639
  8.6 0.0 copy-done.8
  8.6 0.0 copy-done.9
  8.7 2.5 %collective-permute-start.15 = (bf16[2,288,256]{2,1,0:T(8,128)(2,1)S(1)}, bf16[2,288,256]{2,1,0:T(8,128)(2,1)S(1)}, u32[]{:S(2)}, u32[]{:S(2)}) collective-permute-start(bf16[2,288,256]{2,1,0:T(8,128)(2,1)S(1)} %get-tuple-element.63), channel_id=1, source_target_pairs={{0,6},{2,0},{4,2},{6,4},{1,7},{3,1},{5,3},{7,5},{8,14},{10,8},{12,... | collective-permute-start | bytes 884744 | tf_op jit(solution)/shard_map/ppermute | solution.py:644
  11.1 0.5 collective-permute-start.14
  11.7 0.6 collective-permute-start.13
  12.2 13.3 %collective-permute-done.15 = bf16[2,288,256]{2,1,0:T(8,128)(2,1)S(1)} collective-permute-done((bf16[2,288,256]{2,1,0:T(8,128)(2,1)S(1)}, bf16[2,288,256]{2,1,0:T(8,128)(2,1)S(1)}, u32[]{:S(2)}, u32[]{:S(2)}) %collective-permute-start.15) | collective-permute-done | bytes 294944 | tf_op jit(solution)/shard_map/ppermute | solution.py:644
  25.5 0.0 collective-permute-done.14
  25.5 7.6 %collective-permute-done.13 = bf16[2,288,256]{2,1,0:T(8,128)(2,1)S(1)} collective-permute-done((bf16[2,288,256]{2,1,0:T(8,128)(2,1)S(1)}, bf16[2,288,256]{2,1,0:T(8,128)(2,1)S(1)}, u32[]{:S(2)}, u32[]{:S(2)}) %collective-permute-start.13) | collective-permute-done | bytes 294944 | tf_op jit(solution)/shard_map/ppermute | solution.py:644
  33.1 0.0 copy-start
  33.1 0.0 copy-start.1
  33.1 0.0 copy-start.2
  33.1 0.0 copy-start.3
  33.1 0.0 copy-start.4
  33.1 0.0 copy-start.5
  33.1 0.0 copy-start.6
  33.1 0.2 pad_maximum_fusion.same_ref
  33.3 0.0 copy-start.7
  33.3 0.1 collective-permute-start.16
  33.4 0.0 all-to-all-done.part_ref
  33.4 0.5 collective-permute-start.12
  34.0 2.8 %collective-permute-done.16.other_ref = bf16[4,2,288,256]{3,2,1,0:T(8,128)(2,1)} collective-permute-done((bf16[4,2,288,256]{3,2,1,0:T(8,128)(2,1)S(1)}, bf16[4,2,288,256]{3,2,1,0:T(8,128)(2,1)}, u32[]{:S(2)}, u32[]{:S(2)}) %collective-permute-start.16) | collective-permute-done | bytes 1179680 | tf_op jit(solution)/shard_map/ppermute | solution.py:646
  36.7 0.0 collective-permute-done.12.swapped_ref
  36.7 0.0 copy-done.7
  36.7 0.0 copy-done
  36.7 0.0 copy-done.1
  36.8 0.0 copy-done.2
  36.8 0.0 copy-done.3
  36.8 0.0 copy-done.4
  36.8 0.0 copy-done.5
  36.8 0.0 copy-done.6
  36.8 0.0 copy-start.10
  36.8 9.8 %frames.1 = bf16[8,2,2,32,256]{4,3,2,1,0:T(8,128)(2,1)} custom-call(bf16[32,3,16,256]{3,2,1,0:T(8,128)(2,1)S(1)} %all-to-all-done.part_ref, bf16[32,16,256]{2,1,0:T(8,128)(2,1)S(1)} %collective-permute-done.12.swapped_ref, bf16[6912,256]{1,0:T(8,128)(2,1)} %temporal_ref.1, bf16[4,2,288,256]{3,2,1,0:T(8,128)(2,1)} %copy-done.7, ...), custom_call_target="tpu_custom_call" | custom-call | tf_op jit(solution)/shard_map/frames/pallas_call | solution.py:653
  46.7 3.5 %all-to-all-start.1 = ((bf16[8,2,2,32,256]{4,3,2,1,0:T(8,128)(2,1)}), bf16[8,2,2,32,256]{4,3,2,1,0:T(8,128)(2,1)S(1)}, u32[]{:S(2)}, u32[]{:S(2)}) async-start(bf16[8,2,2,32,256]{4,3,2,1,0:T(8,128)(2,1)} %frames.1), calls=%async_computation.1 | async-start | bytes 1048576 | tf_op jit(solution)/shard_map/all_to_all | solution.py:680
  50.2 0.0 copy-done.10
  50.2 0.7 iota_reduce_fusion.1
  51.4 0.6 dynamic_slice.4
  52.0 0.7 iota_reduce_fusion
  53.4 0.6 iota_compare_fusion
  54.0 5.9 %all-to-all-done.1 = bf16[8,2,2,32,256]{4,3,2,1,0:T(8,128)(2,1)S(1)} async-done(((bf16[8,2,2,32,256]{4,3,2,1,0:T(8,128)(2,1)}), bf16[8,2,2,32,256]{4,3,2,1,0:T(8,128)(2,1)S(1)}, u32[]{:S(2)}, u32[]{:S(2)}) %all-to-all-start.1) | async-done | bytes 524320 | tf_op jit(solution)/shard_map/all_to_all | solution.py:680
  59.9 8.1 %conditional.1 = (bf16[2,2,32,256]{3,2,1,0:T(8,128)(2,1)}) conditional(s32[]{:T(128)} %clamp.3, () %tuple.57, bf16[8,2,2,32,256]{4,3,2,1,0:T(8,128)(2,1)S(1)} %all-to-all-done.1, bf16[8,2,2,32,256]{4,3,2,1,0:T(8,128)(2,1)S(1)} %all-to-all-done.1, bf16[8,2,2,32,256]{4,3,2,1,0:T(8,128)(2,1)S(1)} %all-to-all-done.1, ...), branch_computations={%region_2.3_spmd, %region_3.4_spmd, %region_4.5_spmd, %region_5.6_... | conditional | bytes 393264 | solution.py:694
  59.9 1.3 %collective-permute-start.9 = (bf16[2,2,32,256]{3,2,1,0:T(8,128)(2,1)S(1)}, bf16[2,2,32,256]{3,2,1,0:T(8,128)(2,1)}, u32[]{:S(2)}, u32[]{:S(2)}) collective-permute-start(bf16[2,2,32,256]{3,2,1,0:T(8,128)(2,1)S(1)} %slice_bitcast_fusion.9), channel_id=1, source_target_pairs={{0,24},{1,25},{2,26},{3,27},{4,28},{5,29},{6,30},{7,31}} | collective-permute-start | bytes 196616 | tf_op jit(solution)/shard_map/cond/branch_12_fun/ppermute | solution.py:689
  61.1 6.8 %collective-permute-done.9 = bf16[2,2,32,256]{3,2,1,0:T(8,128)(2,1)} collective-permute-done((bf16[2,2,32,256]{3,2,1,0:T(8,128)(2,1)S(1)}, bf16[2,2,32,256]{3,2,1,0:T(8,128)(2,1)}, u32[]{:S(2)}, u32[]{:S(2)}) %collective-permute-start.9) | collective-permute-done | bytes 65568 | tf_op jit(solution)/shard_map/cond/branch_12_fun/ppermute | solution.py:689
  67.9 1.8 %maximum_select_fusion = bf16[18,2,32,256]{3,2,1,0:T(8,128)(2,1)} fusion(bf16[2,2,32,256]{3,2,1,0:T(8,128)(2,1)} %get-tuple-element.64, bf16[16,2,32,256]{3,2,1,0:T(8,128)(2,1)S(1)} %bitcast.52, pred[18]{0:T(512)(128)(4,1)S(1)} %iota_compare_fusion), kind=kLoop, calls=%fused_computation.13 | loop fusion | flops 589824 | bytes 1179666 | tf_op jit(solution)/shard_map/jit(_where)/select_n | solution.py:703
  (3 shorter events, 0.1 us)
Async XLA Ops:
  0.0 8.6 %copy-start.8 = (bf16[288,256]{1,0:T(8,128)(2,1)S(1)}, bf16[288,256]{1,0:T(8,128)(2,1)}, u32[]{:S(2)}) copy-start(bf16[288,256]{1,0:T(8,128)(2,1)} %param.38) | copy-start | bytes 442372
  0.0 8.6 %copy-start.9 = (bf16[288,256]{1,0:T(8,128)(2,1)S(1)}, bf16[288,256]{1,0:T(8,128)(2,1)}, u32[]{:S(2)}) copy-start(bf16[288,256]{1,0:T(8,128)(2,1)} %param.34) | copy-start | bytes 442372
  2.7 30.7 %all-to-all-start = ((bf16[32,3,16,256]{3,2,1,0:T(8,128)(2,1)}), bf16[32,3,16,256]{3,2,1,0:T(8,128)(2,1)S(1)}, u32[]{:S(2)}, u32[]{:S(2)}) async-start(bf16[32,3,16,256]{3,2,1,0:T(8,128)(2,1)} %pick.1), calls=%async_computation | async-start | bytes 1572864 | tf_op jit(solution)/shard_map/all_to_all | solution.py:639
  8.7 16.8 %collective-permute-start.15 = (bf16[2,288,256]{2,1,0:T(8,128)(2,1)S(1)}, bf16[2,288,256]{2,1,0:T(8,128)(2,1)S(1)}, u32[]{:S(2)}, u32[]{:S(2)}) collective-permute-start(bf16[2,288,256]{2,1,0:T(8,128)(2,1)S(1)} %get-tuple-element.63), channel_id=1, source_target_pairs={{0,6},{2,0},{4,2},{6,4},{1,7},{3,1},{5,3},{7,5},{8,14},{10,8},{12,... | collective-permute-start | bytes 884744 | tf_op jit(solution)/shard_map/ppermute | solution.py:644
  11.1 14.4 %collective-permute-start.14 = (bf16[2,288,256]{2,1,0:T(8,128)(2,1)S(1)}, bf16[2,288,256]{2,1,0:T(8,128)(2,1)S(1)}, u32[]{:S(2)}, u32[]{:S(2)}) collective-permute-start(bf16[2,288,256]{2,1,0:T(8,128)(2,1)S(1)} %get-tuple-element.63), channel_id=1, source_target_pairs={{0,4},{2,6},{4,0},{6,2},{1,5},{3,7},{5,1},{7,3},{8,12},{10,14},{12... | collective-permute-start | bytes 884744 | tf_op jit(solution)/shard_map/ppermute | solution.py:644
  11.7 21.4 %collective-permute-start.13 = (bf16[2,288,256]{2,1,0:T(8,128)(2,1)S(1)}, bf16[2,288,256]{2,1,0:T(8,128)(2,1)S(1)}, u32[]{:S(2)}, u32[]{:S(2)}) collective-permute-start(bf16[2,288,256]{2,1,0:T(8,128)(2,1)S(1)} %get-tuple-element.63), channel_id=1, source_target_pairs={{0,2},{2,4},{4,6},{6,0},{1,3},{3,5},{5,7},{7,1},{8,10},{10,12},{12... | collective-permute-start | bytes 884744 | tf_op jit(solution)/shard_map/ppermute | solution.py:644
  33.1 3.6 %copy-start = (f32[256]{0:T(256)S(1)}, f32[256]{0:T(256)}, u32[]{:S(2)}) copy-start(f32[256]{0:T(256)} %param.31) | copy-start | bytes 3076
  33.1 3.6 %copy-start.1 = (f32[256]{0:T(256)S(1)}, f32[256]{0:T(256)}, u32[]{:S(2)}) copy-start(f32[256]{0:T(256)} %param.32) | copy-start | bytes 3076
  33.1 3.7 %copy-start.2 = (f32[256]{0:T(256)S(1)}, f32[256]{0:T(256)}, u32[]{:S(2)}) copy-start(f32[256]{0:T(256)} %param.33) | copy-start | bytes 3076
  33.1 3.7 %copy-start.3 = (f32[256]{0:T(256)S(1)}, f32[256]{0:T(256)}, u32[]{:S(2)}) copy-start(f32[256]{0:T(256)} %param.35) | copy-start | bytes 3076
  33.1 3.7 %copy-start.4 = (f32[256]{0:T(256)S(1)}, f32[256]{0:T(256)}, u32[]{:S(2)}) copy-start(f32[256]{0:T(256)} %param.36) | copy-start | bytes 3076
  33.1 3.7 %copy-start.5 = (f32[256]{0:T(256)S(1)}, f32[256]{0:T(256)}, u32[]{:S(2)}) copy-start(f32[256]{0:T(256)} %param.37) | copy-start | bytes 3076
  33.1 3.7 %copy-start.6 = (f32[256]{0:T(256)S(1)}, f32[256]{0:T(256)}, u32[]{:S(2)}) copy-start(f32[256]{0:T(256)} %param.39) | copy-start | bytes 3076
  33.3 3.4 %copy-start.7 = (bf16[4,2,288,256]{3,2,1,0:T(8,128)(2,1)}, bf16[4,2,288,256]{3,2,1,0:T(8,128)(2,1)S(1)}, u32[]{:S(2)}) copy-start(bf16[4,2,288,256]{3,2,1,0:T(8,128)(2,1)S(1)} %pad_maximum_fusion.same_ref) | copy-start | bytes 3538948
  33.3 3.4 %collective-permute-start.16 = (bf16[4,2,288,256]{3,2,1,0:T(8,128)(2,1)S(1)}, bf16[4,2,288,256]{3,2,1,0:T(8,128)(2,1)}, u32[]{:S(2)}, u32[]{:S(2)}) collective-permute-start(bf16[4,2,288,256]{3,2,1,0:T(8,128)(2,1)S(1)} %pad_maximum_fusion.same_ref), channel_id=1, source_target_pairs={{0,1},{1,0},{2,3},{3,2},{4,5},{5,4},{6,7},{7,6},{8,9},{9,8},{10,11... | collective-permute-start | bytes 3538952 | tf_op jit(solution)/shard_map/ppermute | solution.py:646
  33.4 3.3 %collective-permute-start.12 = (bf16[32,16,256]{2,1,0:T(8,128)(2,1)S(1)}, bf16[32,16,256]{2,1,0:T(8,128)(2,1)S(1)}, u32[]{:S(2)}, u32[]{:S(2)}) collective-permute-start(bf16[32,16,256]{2,1,0:T(8,128)(2,1)S(1)} %slice_bitcast_fusion.12), channel_id=1, source_target_pairs={{0,1},{1,0},{2,3},{3,2},{4,5},{5,4},{6,7},{7,6},{8,9},{9,8},{10,11... | collective-permute-start | bytes 786440 | tf_op jit(solution)/shard_map/ppermute | solution.py:640
  36.8 13.4 %copy-start.10 = (s32[4]{0:T(128)S(1)}, s32[4]{0:T(128)}, u32[]{:S(2)}) copy-start(s32[4]{0:T(128)} %counts_ref.1) | copy-start | bytes 52
  46.7 13.2 %all-to-all-start.1 = ((bf16[8,2,2,32,256]{4,3,2,1,0:T(8,128)(2,1)}), bf16[8,2,2,32,256]{4,3,2,1,0:T(8,128)(2,1)S(1)}, u32[]{:S(2)}, u32[]{:S(2)}) async-start(bf16[8,2,2,32,256]{4,3,2,1,0:T(8,128)(2,1)} %frames.1), calls=%async_computation.1 | async-start | bytes 1048576 | tf_op jit(solution)/shard_map/all_to_all | solution.py:680
  59.9 8.1 %collective-permute-start.9 = (bf16[2,2,32,256]{3,2,1,0:T(8,128)(2,1)S(1)}, bf16[2,2,32,256]{3,2,1,0:T(8,128)(2,1)}, u32[]{:S(2)}, u32[]{:S(2)}) collective-permute-start(bf16[2,2,32,256]{3,2,1,0:T(8,128)(2,1)S(1)} %slice_bitcast_fusion.9), channel_id=1, source_target_pairs={{0,24},{1,25},{2,26},{3,27},{4,28},{5,29},{6,30},{7,31}} | collective-permute-start | bytes 196616 | tf_op jit(solution)/shard_map/cond/branch_12_fun/ppermute | solution.py:689

commit v6 on v5

--- a/solution.py
+++ b/solution.py
@@ -1,4 +1,5 @@
 import functools
+import itertools
 
 import jax
 import jax.numpy as jnp
@@ -388,37 +389,94 @@
         pass
 
 
-def frames_body(
-    part_ref, swapped_ref, temporal_ref, same_ref, other_ref, *refs
-):
-    vectors, (out_ref, *refs) = refs[:7], refs[7:]
-    n_height, each, rows, width, channels = out_ref.shape
+def dot_pieces(source_ref, weight_ref, total_ref, add, parts=2):
+    rows, width, depth = source_ref.shape
+    part_rows = (rows - 2) // parts
+    cells = part_rows * width
+    for part in range(parts):
+        summed = None
+        for row_tap in range(3):
+            low = part * part_rows + row_tap
+            product = jnp.dot(
+                source_ref[low : low + part_rows].reshape(cells, depth),
+                weight_ref[row_tap * depth : (row_tap + 1) * depth],
+                preferred_element_type=F32,
+            )
+            summed = product if summed is None else summed + product
+            yield
+        if add:
+            total_ref[part * cells : (part + 1) * cells] += summed
+        else:
+            total_ref[part * cells : (part + 1) * cells] = summed
+
+
+def norm_pieces(field_ref, normed_ref, row_of, gain, shift):
+    all_rows, width, channels = field_ref.shape
+    cells, width_group = all_rows * width, channels // GROUPS
+    pivot = None
+    sums = squares = jnp.zeros((8, channels), F32)
+    for row in range(all_rows):
+        if row_of is None:
+            values = field_ref[row].astype(F32)
+        else:
+            rounded = row_of(row).astype(BF16)
+            field_ref[row] = rounded
+            values = rounded.astype(F32)
+        if pivot is None:
+            pivot = values[:1]
+        apart = (values - pivot).reshape(width // 8, 8, channels)
+        sums = sums + jnp.sum(apart, axis=0)
+        squares = squares + jnp.sum(apart * apart, axis=0)
+        if row % 4 == 3:
+            yield
+    own = jnp.sum(sums, axis=0, keepdims=True) * (1.0 / cells)
+    squares = jnp.sum(squares, axis=0, keepdims=True) * (1.0 / cells)
+    sample = 1.0 / width_group
+    mean = group_spread(own + pivot, width_group) * sample
+    off = own + pivot - mean
+    spread = squares - own * own + off * off
+    variance = jnp.maximum(group_spread(spread, width_group) * sample, 0.0)
+    scale = lax.rsqrt(variance + EPS) * gain
+    offset = 0.5 * (shift - mean * scale)
+    scale = 0.5 * scale
+    yield
+    for row in range(all_rows):
+        half = field_ref[row].astype(F32) * scale + offset
+        normed_ref[row + 1] = with_column_taps(half + half * jnp.tanh(half))
+        if row % 2 == 1:
+            yield
+
+
+def clear_borders(refs):
+    for ref in refs:
+        border = jnp.zeros(ref.shape[1:], BF16)
+        ref[0] = border
+        ref[ref.shape[0] - 1] = border
+
+
+def start_all(copies):
+    for copy in copies:
+        copy.start()
+
+
+def wait_all(copies):
+    for copy in copies:
+        copy.wait()
+
+
+def frames_body(n_height, part_ref, swapped_ref, temporal_ref, bias_ref, gain_ref, shift_ref, *refs):
+    normed_out_ref, blended_out_ref, order_ref, *refs = refs
+    order_ref[...] = jnp.zeros_like(order_ref)
+    each, all_rows, width, channels = blended_out_ref.shape
     places = each + 2
     taps_refs, refs = refs[:places], refs[places:]
-    normed_refs, refs = refs[:each], refs[each:]
     total_refs, refs = refs[:each], refs[each:]
-    blended_refs, refs = refs[:each], refs[each:]
-    field_refs, refs = refs[:each], refs[each:]
-    landed_refs, refs = refs[:places], refs[places:]
-    raw_ref, time_ref, weights_ref, done_ref, vectors_ref, *refs = refs
-    land_sems, time_sems, sems, out_sems, vector_sems = refs
-    n_pair = n_height // 2
+    raw_ref, time_ref, time_sems = refs
     n_frame = part_ref.shape[0] // n_height
-    columns = width // n_frame
-    all_rows = n_height * rows
+    columns, rows = width // n_frame, all_rows // n_height
     depth = 3 * channels
-    cells = all_rows * width
-    width_group = channels // GROUPS
-    pair, core = lax.axis_index("pair"), lax.axis_index("core")
-    span = same_ref.shape[2]
-    landings = [
-        pltpu.make_async_copy(
-            part_ref.at[:, place] if place <= each else swapped_ref,
-            landed_refs[place],
-            land_sems.at[place],
-        )
-        for place in range(places)
-    ]
+    core = lax.axis_index("core")
+
     time_copies = []
     for step in range(3):
         tap = step + core * (2 - 2 * step)
@@ -428,39 +486,17 @@
                 temporal_ref.at[pl.ds(begin, 3 * depth)], time_ref.at[step], time_sems.at[step]
             )
         )
-    vector_copies = [
-        pltpu.make_async_copy(ref, vectors_ref.at[line], vector_sems.at[line])
-        for line, ref in enumerate(vectors)
-    ]
-    copies = []
-    for which in range(2):
-        of_weight = []
-        for step in range(n_pair):
-            source = lax.rem(pair - step + n_pair, n_pair)
-            for side, (parts_ref, of_core) in enumerate(((same_ref, core), (other_ref, 1 - core))):
-                begin = pl.multiple_of((source * 2 + of_core) * span, span)
-                of_weight.append(
-                    pltpu.make_async_copy(
-                        parts_ref.at[step, which],
-                        weights_ref.at[which, pl.ds(begin, span)],
-                        sems.at[which, step, side],
-                    )
-                )
-        copies.append(of_weight)
-    for copy in landings[:3] + time_copies + landings[3:] + vector_copies + copies[0] + copies[1]:
-        copy.start()
-
-    border = jnp.zeros((width, depth), BF16)
-    for ref in taps_refs + normed_refs:
-        ref[0] = border
-        ref[all_rows + 1] = border
+    start_all(time_copies)
+    normed_refs = [normed_out_ref.at[place] for place in range(each - 1)]
+    clear_borders(list(taps_refs) + normed_refs)
+
+    def piece_of(place, source):
+        return part_ref[source, place] if place <= each else swapped_ref[source]
 
     def lay(place):
-        landings[place].wait()
         for height in range(n_height):
             pieces = [
-                landed_refs[place][peer * n_height + height].astype(F32)
-                for peer in range(n_frame)
+                piece_of(place, peer * n_height + height).astype(F32) for peer in range(n_frame)
             ]
             for row in range(rows):
                 values = jnp.concatenate(
@@ -470,139 +506,111 @@
                 taps_refs[place][height * rows + row + 1] = with_column_taps(silu(values))
             yield
 
-    parts_of_field = 2
-    part_rows = all_rows // parts_of_field
-    part_cells = part_rows * width
-
-    def products(source_ref, weight_ref, part):
-        summed = None
-        for row_tap in range(3):
-            low = part * part_rows + row_tap
-            product = jnp.dot(
-                source_ref[low : low + part_rows].reshape(part_cells, depth),
-                weight_ref[row_tap * depth : (row_tap + 1) * depth],
-                preferred_element_type=F32,
-            )
-            summed = product if summed is None else summed + product
-            yield summed
-
-    def temporal(place):
-        for step in range(3):
-            if place == 0:
-                time_copies[step].wait()
-            for part in range(parts_of_field):
-                for summed in products(taps_refs[place + step], time_ref.at[step], part):
-                    yield
-                cut = slice(part * part_cells, (part + 1) * part_cells)
-                if step == 0:
-                    total_refs[place][cut] = summed
-                else:
-                    total_refs[place][cut] += summed
-
-    def convolve(place, which):
-        for part in range(parts_of_field):
-            for summed in products(normed_refs[place], weights_ref.at[which], part):
-                yield
-            total_refs[place][part * part_cells : (part + 1) * part_cells] = summed
-
-    def norm(place, field_ref, row_of, gain, shift):
-        pivot = None
-        sums = squares = jnp.zeros((8, channels), F32)
-        for row in range(all_rows):
-            rounded = row_of(row).astype(BF16)
-            field_ref[row] = rounded
-            values = rounded.astype(F32)
-            if pivot is None:
-                pivot = values[:1]
-            apart = (values - pivot).reshape(width // 8, 8, channels)
-            sums = sums + jnp.sum(apart, axis=0)
-            squares = squares + jnp.sum(apart * apart, axis=0)
-            if row % 4 == 3:
-                yield
-        own = jnp.sum(sums, axis=0, keepdims=True) * (1.0 / cells)
-        squares = jnp.sum(squares, axis=0, keepdims=True) * (1.0 / cells)
-        sample = 1.0 / width_group
-        mean = group_spread(own + pivot, width_group) * sample
-        off = own + pivot - mean
-        spread = squares - own * own + off * off
-        variance = jnp.maximum(group_spread(spread, width_group) * sample, 0.0)
-        scale = lax.rsqrt(variance + EPS) * gain
-        offset = 0.5 * (shift - mean * scale)
-        scale = 0.5 * scale
-        yield
-        for row in range(all_rows):
-            half = field_ref[row].astype(F32) * scale + offset
-            normed_refs[place][row + 1] = with_column_taps(half + half * jnp.tanh(half))
-            if row % 2 == 1:
-                yield
-
-    def first_norm(place):
+    def temporal(place, step):
+        if place == 0:
+            time_copies[step].wait()
+        return dot_pieces(taps_refs[place + step], time_ref.at[step], total_refs[place], step > 0)
+
+    def blended_row(place):
         raw_at = place + 2 - 2 * core
 
         def row_of(row):
             product = total_refs[place][row * width : (row + 1) * width]
-            return raw_ref[raw_at, row].astype(F32) + product + temporal_bias
-
-        return norm(place, blended_refs[place], row_of, first_gain, first_shift)
+            return raw_ref[raw_at, row].astype(F32) + product + bias_ref[...]
+
+        return row_of
+
+    nothing = iter(())
+    for place in range(3):
+        interleave(lay(place), nothing, 0)
+    rest = itertools.chain.from_iterable(lay(place) for place in range(3, places))
+    pieces = itertools.chain.from_iterable(temporal(0, step) for step in range(3))
+    interleave(pieces, rest, 1)
+    for place in range(1, each):
+        norm = norm_pieces(
+            blended_out_ref.at[place - 1], normed_refs[place - 1], blended_row(place - 1),
+            gain_ref[...], shift_ref[...],
+        )
+        pieces = itertools.chain.from_iterable(temporal(place, step) for step in range(3))
+        interleave(pieces, norm, 1)
+    row_of = blended_row(each - 1)
+    for row in range(all_rows):
+        blended_out_ref[each - 1, row] = row_of(row).astype(BF16)
+
+
+def spatial_body(n_pair, normed_ref, blended_ref, order_ref, *refs):
+    same_refs, refs = refs[:n_pair], refs[n_pair:]
+    other_refs, refs = refs[:n_pair], refs[n_pair:]
+    gain_ref, shift_ref, first_bias_ref, second_gain_ref, second_shift_ref, *refs = refs
+    second_bias_ref, out_ref, *refs = refs
+    n_height, each, rows, width, channels = out_ref.shape
+    all_rows = n_height * rows
+    normed_refs, refs = refs[:each], refs[each:]
+    total_refs, refs = refs[:each], refs[each:]
+    field_refs, refs = refs[:each], refs[each:]
+    weights_ref, done_ref, out_sems = refs
+    pair, core = lax.axis_index("pair"), lax.axis_index("core")
+    span = same_refs[0].shape[1]
+
+    def gather(which):
+        for step in range(n_pair):
+            for shard_ref, of_core in ((same_refs[step], core), (other_refs[step], 1 - core)):
+                source = jnp.bitwise_xor(pair, step) * 2 + of_core
+                begin = pl.multiple_of(source * span, span)
+                weights_ref[which, pl.ds(begin, span)] = shard_ref[which]
+                yield
+
+    clear_borders(normed_refs)
+
+    def first_source(place):
+        return normed_ref.at[place] if place < each - 1 else normed_refs[place]
 
     def second_norm(place):
         def row_of(row):
-            return total_refs[place][row * width : (row + 1) * width] + first_bias
-
-        return norm(place, field_refs[place], row_of, second_gain, second_shift)
+            return total_refs[place][row * width : (row + 1) * width] + first_bias_ref[...]
+
+        return norm_pieces(
+            field_refs[place], normed_refs[place], row_of, second_gain_ref[...],
+            second_shift_ref[...],
+        )
 
     def finish(place):
         at = place + core * (each - 1 - 2 * place)
         for row in range(all_rows):
-            product = total_refs[place][row * width : (row + 1) * width] + second_bias
-            decoded = blended_refs[place][row].astype(F32) + product
+            product = total_refs[place][row * width : (row + 1) * width] + second_bias_ref[...]
+            decoded = blended_ref[place, row].astype(F32) + product
             done_ref[place, row // rows, row % rows] = decoded.astype(BF16)
             if row % 4 == 3:
                 yield
-        store = pltpu.make_async_copy(
-            done_ref.at[place], out_ref.at[:, at], out_sems.at[place]
-        )
-        store.start()
-        stores.append(store)
+        stores.append(
+            pltpu.make_async_copy(done_ref.at[place], out_ref.at[:, at], out_sems.at[place])
+        )
+        stores[-1].start()
 
     stores = []
-
-    def ready(which):
-        for copy in which:
-            copy.wait()
-
-    def both(one, other):
-        yield from one
-        yield from other
-
-    nothing = iter(())
-    for place in range(3):
-        interleave(lay(place), nothing, 0)
-    laying = nothing
-    for place in range(3, places):
-        laying = both(laying, lay(place))
-    interleave(temporal(0), laying, 1)
-    ready(vector_copies)
-    (
-        temporal_bias, first_gain, first_shift, first_bias, second_gain, second_shift, second_bias
-    ) = [vectors_ref[line] for line in range(7)]
-    for place in range(1, each):
-        interleave(temporal(place), first_norm(place - 1), 1)
-    ready(copies[0])
-    pending = first_norm(each - 1)
+    pending = norm_pieces(
+        blended_ref.at[each - 1], normed_refs[each - 1], None, gain_ref[...], shift_ref[...]
+    )
+    interleave(gather(0), pending, 1)
+    pending = gather(1)
     for place in range(each):
-        interleave(convolve(place, 0), pending, 3)
+        interleave(
+            dot_pieces(first_source(place), weights_ref.at[0], total_refs[place], False),
+            pending, 3,
+        )
         pending = second_norm(place)
-    ready(copies[1])
     for place in range(each):
-        interleave(convolve(place, 1), pending, 3)
+        interleave(
+            dot_pieces(normed_refs[place], weights_ref.at[1], total_refs[place], False),
+            pending, 3,
+        )
         pending = finish(place)
-    interleave(pending, nothing, 0)
-    ready(stores)
-
-
-def ring(size, step):
-    return [(i, (i + step) % size) for i in range(size)]
+    interleave(pending, iter(()), 0)
+    wait_all(stores)
+
+
+def partners(size, step):
+    return [(i, i ^ step) for i in range(size)]
 
 
 def whole_frames(
@@ -640,42 +648,60 @@
     swapped = lax.ppermute(parts[:, each], "core", swap)
 
     own = jnp.stack([first_weight, second_weight])
-    same = jnp.stack(
-        [own] + [lax.ppermute(own, "pair", ring(n_pair, step)) for step in range(1, n_pair)]
-    )
-    other = lax.ppermute(same, "core", swap)
-
-    vectors = (
-        temporal_bias, first_gain, first_shift, first_bias, second_gain, second_shift, second_bias
-    )
+    same = [own] + [
+        lax.ppermute(own, "pair", partners(n_pair, step)) for step in range(1, n_pair)
+    ]
+
+    def row_of(vector):
+        return vector.reshape(1, channels)
+
     field = (all_rows, width, channels)
     taps = (all_rows + 2, width, 3 * channels)
-    decoded = pl.pallas_call(
-        frames_body,
-        out_shape=jax.ShapeDtypeStruct((n_height, each, rows, width, channels), BF16),
-        in_specs=[HBM] * 12,
-        out_specs=HBM,
-        scratch_shapes=[pltpu.VMEM(taps, BF16)] * (2 * each + 2)
-        + [pltpu.VMEM((all_rows * width, channels), F32)] * each
-        + [pltpu.VMEM(field, BF16)] * (2 * each)
-        + [pltpu.VMEM((n_frame * n_height, rows * columns, channels), BF16)] * (each + 2)
+    total = pltpu.VMEM((all_rows * width, channels), F32)
+    limit = pltpu.CompilerParams(vmem_limit_bytes=50 * 1024 * 1024)
+    normed, blended, order = pl.pallas_call(
+        functools.partial(frames_body, n_height),
+        out_shape=(
+            jax.ShapeDtypeStruct((max(each - 1, 1),) + taps, BF16),
+            jax.ShapeDtypeStruct((each,) + field, BF16),
+            jax.ShapeDtypeStruct((8, 128), F32),
+        ),
+        in_specs=[VMEM, VMEM, HBM] + [VMEM] * 3,
+        out_specs=(VMEM,) * 3,
+        scratch_shapes=[pltpu.VMEM(taps, BF16)] * (each + 2)
+        + [total] * each
         + [
             pltpu.VMEM((each + 2,) + field, BF16),
             pltpu.VMEM((3, 9 * channels, channels), BF16),
+            pltpu.SemaphoreType.DMA((3,)),
+        ],
+        compiler_params=limit,
+        name="frames",
+    )(
+        parts, swapped, temporal_weight,
+        row_of(temporal_bias), row_of(first_gain), row_of(first_shift),
+    )
+    same[1:], order = lax.optimization_barrier((same[1:], order))
+    other = [lax.ppermute(shard, "core", swap) for shard in same]
+    decoded = pl.pallas_call(
+        functools.partial(spatial_body, n_pair),
+        out_shape=jax.ShapeDtypeStruct((n_height, each, rows, width, channels), BF16),
+        in_specs=[VMEM] * (9 + 2 * n_pair),
+        out_specs=HBM,
+        scratch_shapes=[pltpu.VMEM(taps, BF16)] * each
+        + [total] * each
+        + [pltpu.VMEM(field, BF16)] * each
+        + [
             pltpu.VMEM((2, 9 * channels, channels), BF16),
             pltpu.VMEM((each, n_height, rows, width, channels), BF16),
-            pltpu.VMEM((7, 1, channels), F32),
-            pltpu.SemaphoreType.DMA((each + 2,)),
-            pltpu.SemaphoreType.DMA((3,)),
-            pltpu.SemaphoreType.DMA((2, n_pair, 2)),
             pltpu.SemaphoreType.DMA((each,)),
-            pltpu.SemaphoreType.DMA((7,)),
         ],
-        compiler_params=pltpu.CompilerParams(vmem_limit_bytes=52 * 1024 * 1024),
-        name="frames",
+        compiler_params=pltpu.CompilerParams(vmem_limit_bytes=20 * 1024 * 1024),
+        name="spatial",
     )(
-        parts, swapped, temporal_weight, same, other,
-        *[vector.reshape(1, channels) for vector in vectors],
+        normed, blended, order, *same, *other,
+        row_of(first_gain), row_of(first_shift), row_of(first_bias),
+        row_of(second_gain), row_of(second_shift), row_of(second_bias),
     )
     owned = lax.all_to_all(decoded, ("pair", "core"), split_axis=0, concat_axis=0)
     owned = owned.reshape((n_height * each,) + owned.shape[2:])
@@ -853,7 +879,9 @@
     capacity = slots_of(frames, n_frame)
     each, extra = divmod(capacity, n_height)
     room = each * (n_height - 2)
-    fits = each > 0 and extra <= 2 * each and n_frame > 1
+    n_pair = lax.axis_size("pair")
+    fits = each > 0 and extra <= 2 * each and n_frame > 1 and n_pair > 1
+    fits = fits and n_pair & (n_pair - 1) == 0
     if fits and 2 * (each * n_height + 1) > frames and frames - capacity < n_frame * room:
         return whole_frames(video, *rest)
     return split_rows(video, *rest)

time: 70 us -> 67.7 us (0.967)
  the two profiles are of different devices: /device:TPU:24 before, /device:TPU:0 now
where the time goes in v6:
time: 67.7 us; the launch traced here: 68.8 us
  waiting for transfers between devices  31.7 us (47%)
  starting transfers between devices  17.1 us (25%)
  Pallas kernels  13.2 us (19%)
  other arithmetic  4.78 us (7%)
  between operations  1.35 us (2%)
  local copies, waits for them, and re-layouts  0.68 us (1%)
    all_to_all x1, waiting for transfers between devices, whole_frames(): lax.all_to_all(picked, ('frame', 'pair', 'core'), split_axis=0, concat_ax...  16 us
    all_to_all x1, starting transfers between devices, whole_frames(): lax.all_to_all(picked, ('frame', 'pair', 'core'), split_axis=0, concat_ax...  7.31 us
    ppermute x1, waiting for transfers between devices, homeward(): return lambda rows: lax.ppermute(rows, 'frame', [(source, target)])  6.76 us
    all_to_all x1, waiting for transfers between devices, whole_frames(): lax.all_to_all(decoded, ('pair', 'core'), split_axis=0, concat_axis=0)  5.93 us
    pallas_call x1, Pallas kernels, whole_frames(): pl.pallas_call(functools.partial(frames_body, n_height), out_shape=(jax.S...  5.59 us
    pallas_call x1, Pallas kernels, whole_frames(): pl.pallas_call(functools.partial(spatial_body, n_pair), out_shape=jax.Sha...  4.88 us
    all_to_all x1, starting transfers between devices, whole_frames(): lax.all_to_all(decoded, ('pair', 'core'), split_axis=0, concat_axis=0)  3.68 us
    ppermute x3, starting transfers between devices, whole_frames(): lax.ppermute(own, 'pair', partners(n_pair, step))  3.55 us
  transfers between devices with their start and end apart: 11, of which 7 were waited for; matrix products, arithmetic and copies ran while one was open for 5% of the time, Pallas kernels for 8%

profile of v6, /device:TPU:0, one launch (start us, length us, event | category | flops | bytes accessed | tf_op | source)
XLA Modules:
  0.0 68.8 jit_solution(1027589807602137747)
XLA Ops:
  0.0 0.0 copy-start
  0.0 0.0 copy-start.1
  0.0 0.0 copy-start.2
  0.0 2.7 %pick.1 = bf16[32,3,16,256]{3,2,1,0:T(8,128)(2,1)} custom-call(s32[4]{0:T(128)} %counts_ref.1, bf16[33,16,256]{2,1,0:T(8,128)(2,1)} %bitcast.50), custom_call_target="tpu_custom_call" | custom-call | tf_op jit(solution)/shard_map/pick/pallas_call | solution.py:631
  2.7 0.0 copy-start.3
  2.7 0.0 copy-start.4
  2.7 0.0 copy-start.5
  2.7 0.0 copy-start.6
  2.8 7.3 %all-to-all-start = ((bf16[32,3,16,256]{3,2,1,0:T(8,128)(2,1)}), bf16[32,3,16,256]{3,2,1,0:T(8,128)(2,1)S(1)}, u32[]{:S(2)}, u32[]{:S(2)}) async-start(bf16[32,3,16,256]{3,2,1,0:T(8,128)(2,1)} %pick.1), calls=%async_computation | async-start | bytes 1572864 | tf_op jit(solution)/shard_map/all_to_all | solution.py:647
  10.1 1.0 %pad_maximum_fusion.refs_0_ = bf16[2,288,256]{2,1,0:T(8,128)(2,1)S(1)} fusion(bf16[1,288,256]{2,1,0:T(8,128)(2,1)} %bitcast.51, bf16[1,288,256]{2,1,0:T(8,128)(2,1)} %bitcast.52), kind=kLoop, calls=%fused_computation.13 | loop fusion | flops 147456 | bytes 589824 | tf_op jit(solution)/shard_map/stack | solution.py:650
  11.1 1.8 %collective-permute-start.13 = (bf16[2,288,256]{2,1,0:T(8,128)(2,1)S(1)}, bf16[2,288,256]{2,1,0:T(8,128)(2,1)S(1)}, u32[]{:S(2)}, u32[]{:S(2)}) collective-permute-start(bf16[2,288,256]{2,1,0:T(8,128)(2,1)S(1)} %pad_maximum_fusion.refs_0_), channel_id=1, source_target_pairs={{0,2},{2,0},{4,6},{6,4},{1,3},{3,1},{5,7},{7,5},{8,10},{10,8},{12,... | collective-permute-start | bytes 884744 | tf_op jit(solution)/shard_map/ppermute | solution.py:652
  12.9 1.5 %collective-permute-start.14 = (bf16[2,288,256]{2,1,0:T(8,128)(2,1)S(1)}, bf16[2,288,256]{2,1,0:T(8,128)(2,1)S(1)}, u32[]{:S(2)}, u32[]{:S(2)}) collective-permute-start(bf16[2,288,256]{2,1,0:T(8,128)(2,1)S(1)} %pad_maximum_fusion.refs_0_), channel_id=1, source_target_pairs={{0,4},{2,6},{4,0},{6,2},{1,5},{3,7},{5,1},{7,3},{8,12},{10,14},{12... | collective-permute-start | bytes 884744 | tf_op jit(solution)/shard_map/ppermute | solution.py:652
  14.4 0.3 collective-permute-start.15
  14.6 16.0 %all-to-all-done.part_ref = bf16[32,3,16,256]{3,2,1,0:T(8,128)(2,1)S(1)} async-done(((bf16[32,3,16,256]{3,2,1,0:T(8,128)(2,1)}), bf16[32,3,16,256]{3,2,1,0:T(8,128)(2,1)S(1)}, u32[]{:S(2)}, u32[]{:S(2)}) %all-to-all-start) | async-done | bytes 786464 | tf_op jit(solution)/shard_map/all_to_all | solution.py:647
  30.7 0.1 collective-permute-start.12
  30.8 0.5 collective-permute-start.16
  31.3 1.0 %collective-permute-done.12.swapped_ref = bf16[32,16,256]{2,1,0:T(8,128)(2,1)S(1)} collective-permute-done((bf16[32,16,256]{2,1,0:T(8,128)(2,1)S(1)}, bf16[32,16,256]{2,1,0:T(8,128)(2,1)S(1)}, u32[]{:S(2)}, u32[]{:S(2)}) %collective-permute-start.12) | collective-permute-done | bytes 262176 | tf_op jit(solution)/shard_map/ppermute | solution.py:648
  32.3 0.0 copy-done
  32.3 0.0 copy-done.1
  32.3 0.0 copy-done.2
  32.3 5.6 %frames.1 = (bf16[1,18,32,768]{3,2,1,0:T(8,128)(2,1)S(1)}, bf16[2,16,32,256]{3,2,1,0:T(8,128)(2,1)S(1)}, f32[8,128]{1,0:T(8,128)S(1)}) custom-call(bf16[32,3,16,256]{3,2,1,0:T(8,128)(2,1)S(1)} %all-to-all-done.part_ref, bf16[32,16,256]{2,1,0:T(8,128)(2,1)S(1)} %collective-permute-done.12.swapped_ref, bf16[6912,256]{1,0:T(8,128)(2,1)} %temporal_ref.1, ...), custom_call_target="tpu_custom_call" | custom-call | tf_op jit(solution)/shard_map/frames/pallas_call | solution.py:662
  37.9 0.0 copy-start.7
  37.9 0.0 collective-permute-done.13.refs_1_
  37.9 0.0 collective-permute-done.14.refs_2_
  37.9 0.0 collective-permute-done.15.refs_3_
  38.0 0.2 collective-permute-start.17
  38.2 0.4 collective-permute-start.18
  38.5 0.1 collective-permute-start.19
  38.7 0.0 collective-permute-done.16.refs_4_
  38.7 0.9 %collective-permute-done.17.refs_5_ = bf16[2,288,256]{2,1,0:T(8,128)(2,1)S(1)} collective-permute-done((bf16[2,288,256]{2,1,0:T(8,128)(2,1)S(1)}, bf16[2,288,256]{2,1,0:T(8,128)(2,1)S(1)}, u32[]{:S(2)}, u32[]{:S(2)}) %collective-permute-start.17) | collective-permute-done | bytes 294944 | tf_op jit(solution)/shard_map/ppermute | solution.py:685
  39.6 0.4 collective-permute-done.18.refs_6_
  40.0 0.6 collective-permute-done.19.refs_7_
  40.6 0.0 copy-done.3
  40.6 0.0 copy-done.4
  40.6 0.0 copy-done.5
  40.6 0.0 copy-done.6
  40.6 4.9 %spatial.1 = bf16[8,2,2,32,256]{4,3,2,1,0:T(8,128)(2,1)} custom-call(bf16[1,18,32,768]{3,2,1,0:T(8,128)(2,1)S(1)} %get-tuple-element.67.normed_ref, bf16[2,16,32,256]{3,2,1,0:T(8,128)(2,1)S(1)} %get-tuple-element.68.blended_ref, f32[8,128]{1,0:T(8,128)S(1)} %get-tuple-element.70.order_ref, bf16[2,288,256]{2,1,0:T(8,128)(2,1)S(1)} %pad_maximum_fusion.refs_0_, ...), custom_call_target="tpu_custom_call" | custom-call | tf_op jit(solution)/shard_map/spatial/pallas_call | solution.py:686
  45.5 3.7 %all-to-all-start.1 = ((bf16[8,2,2,32,256]{4,3,2,1,0:T(8,128)(2,1)}), bf16[8,2,2,32,256]{4,3,2,1,0:T(8,128)(2,1)S(1)}, u32[]{:S(2)}, u32[]{:S(2)}) async-start(bf16[8,2,2,32,256]{4,3,2,1,0:T(8,128)(2,1)} %spatial.1), calls=%async_computation.1 | async-start | bytes 1048576 | tf_op jit(solution)/shard_map/all_to_all | solution.py:706
  49.2 0.0 copy-done.7
  49.2 0.7 iota_reduce_fusion.1
  50.4 0.6 dynamic_slice.4
  51.0 0.7 iota_reduce_fusion
  52.3 0.6 iota_compare_fusion
  53.0 5.9 %all-to-all-done.1 = bf16[8,2,2,32,256]{4,3,2,1,0:T(8,128)(2,1)S(1)} async-done(((bf16[8,2,2,32,256]{4,3,2,1,0:T(8,128)(2,1)}), bf16[8,2,2,32,256]{4,3,2,1,0:T(8,128)(2,1)S(1)}, u32[]{:S(2)}, u32[]{:S(2)}) %all-to-all-start.1) | async-done | bytes 524320 | tf_op jit(solution)/shard_map/all_to_all | solution.py:706
  58.9 8.1 %conditional.1 = (bf16[2,2,32,256]{3,2,1,0:T(8,128)(2,1)}) conditional(s32[]{:T(128)} %clamp.3, () %tuple.59, bf16[8,2,2,32,256]{4,3,2,1,0:T(8,128)(2,1)S(1)} %all-to-all-done.1, bf16[8,2,2,32,256]{4,3,2,1,0:T(8,128)(2,1)S(1)} %all-to-all-done.1, bf16[8,2,2,32,256]{4,3,2,1,0:T(8,128)(2,1)S(1)} %all-to-all-done.1, ...), branch_computations={%region_2.3_spmd, %region_3.4_spmd, %region_4.5_spmd, %region_5.6_... | conditional | bytes 393264 | solution.py:720
  58.9 1.3 %collective-permute-start.2 = (bf16[2,2,32,256]{3,2,1,0:T(8,128)(2,1)S(1)}, bf16[2,2,32,256]{3,2,1,0:T(8,128)(2,1)}, u32[]{:S(2)}, u32[]{:S(2)}) collective-permute-start(bf16[2,2,32,256]{3,2,1,0:T(8,128)(2,1)S(1)} %slice_bitcast_fusion.2), channel_id=1, source_target_pairs={{24,0},{25,1},{26,2},{27,3},{28,4},{29,5},{30,6},{31,7}} | collective-permute-start | bytes 196616 | tf_op jit(solution)/shard_map/cond/branch_3_fun/ppermute | solution.py:715
  60.2 6.8 %collective-permute-done.2 = bf16[2,2,32,256]{3,2,1,0:T(8,128)(2,1)} collective-permute-done((bf16[2,2,32,256]{3,2,1,0:T(8,128)(2,1)S(1)}, bf16[2,2,32,256]{3,2,1,0:T(8,128)(2,1)}, u32[]{:S(2)}, u32[]{:S(2)}) %collective-permute-start.2) | collective-permute-done | bytes 65568 | tf_op jit(solution)/shard_map/cond/branch_3_fun/ppermute | solution.py:715
  67.0 1.8 %maximum_select_fusion = bf16[18,2,32,256]{3,2,1,0:T(8,128)(2,1)} fusion(bf16[2,2,32,256]{3,2,1,0:T(8,128)(2,1)} %get-tuple-element.76, bf16[16,2,32,256]{3,2,1,0:T(8,128)(2,1)S(1)} %bitcast.49, pred[18]{0:T(512)(128)(4,1)S(1)} %iota_compare_fusion), kind=kLoop, calls=%fused_computation.12 | loop fusion | flops 589824 | bytes 1179666 | tf_op jit(solution)/shard_map/jit(_where)/select_n | solution.py:729
  (2 shorter events, 0.0 us)
Async XLA Ops:
  0.0 32.3 %copy-start = (f32[256]{0:T(256)S(1)}, f32[256]{0:T(256)}, u32[]{:S(2)}) copy-start(f32[256]{0:T(256)} %param.32) | copy-start | bytes 3076
  0.0 32.3 %copy-start.1 = (f32[256]{0:T(256)S(1)}, f32[256]{0:T(256)}, u32[]{:S(2)}) copy-start(f32[256]{0:T(256)} %param.33) | copy-start | bytes 3076
  0.0 32.3 %copy-start.2 = (f32[256]{0:T(256)S(1)}, f32[256]{0:T(256)}, u32[]{:S(2)}) copy-start(f32[256]{0:T(256)} %param.31) | copy-start | bytes 3076
  2.7 37.9 %copy-start.3 = (f32[256]{0:T(256)S(1)}, f32[256]{0:T(256)}, u32[]{:S(2)}) copy-start(f32[256]{0:T(256)} %param.35) | copy-start | bytes 3076
  2.7 37.9 %copy-start.4 = (f32[256]{0:T(256)S(1)}, f32[256]{0:T(256)}, u32[]{:S(2)}) copy-start(f32[256]{0:T(256)} %param.36) | copy-start | bytes 3076
  2.7 37.9 %copy-start.5 = (f32[256]{0:T(256)S(1)}, f32[256]{0:T(256)}, u32[]{:S(2)}) copy-start(f32[256]{0:T(256)} %param.37) | copy-start | bytes 3076
  2.7 37.9 %copy-start.6 = (f32[256]{0:T(256)S(1)}, f32[256]{0:T(256)}, u32[]{:S(2)}) copy-start(f32[256]{0:T(256)} %param.39) | copy-start | bytes 3076
  2.8 27.9 %all-to-all-start = ((bf16[32,3,16,256]{3,2,1,0:T(8,128)(2,1)}), bf16[32,3,16,256]{3,2,1,0:T(8,128)(2,1)S(1)}, u32[]{:S(2)}, u32[]{:S(2)}) async-start(bf16[32,3,16,256]{3,2,1,0:T(8,128)(2,1)} %pick.1), calls=%async_computation | async-start | bytes 1572864 | tf_op jit(solution)/shard_map/all_to_all | solution.py:647
  11.1 26.8 %collective-permute-start.13 = (bf16[2,288,256]{2,1,0:T(8,128)(2,1)S(1)}, bf16[2,288,256]{2,1,0:T(8,128)(2,1)S(1)}, u32[]{:S(2)}, u32[]{:S(2)}) collective-permute-start(bf16[2,288,256]{2,1,0:T(8,128)(2,1)S(1)} %pad_maximum_fusion.refs_0_), channel_id=1, source_target_pairs={{0,2},{2,0},{4,6},{6,4},{1,3},{3,1},{5,7},{7,5},{8,10},{10,8},{12,... | collective-permute-start | bytes 884744 | tf_op jit(solution)/shard_map/ppermute | solution.py:652
  12.9 25.0 %collective-permute-start.14 = (bf16[2,288,256]{2,1,0:T(8,128)(2,1)S(1)}, bf16[2,288,256]{2,1,0:T(8,128)(2,1)S(1)}, u32[]{:S(2)}, u32[]{:S(2)}) collective-permute-start(bf16[2,288,256]{2,1,0:T(8,128)(2,1)S(1)} %pad_maximum_fusion.refs_0_), channel_id=1, source_target_pairs={{0,4},{2,6},{4,0},{6,2},{1,5},{3,7},{5,1},{7,3},{8,12},{10,14},{12... | collective-permute-start | bytes 884744 | tf_op jit(solution)/shard_map/ppermute | solution.py:652
  14.4 23.6 %collective-permute-start.15 = (bf16[2,288,256]{2,1,0:T(8,128)(2,1)S(1)}, bf16[2,288,256]{2,1,0:T(8,128)(2,1)S(1)}, u32[]{:S(2)}, u32[]{:S(2)}) collective-permute-start(bf16[2,288,256]{2,1,0:T(8,128)(2,1)S(1)} %pad_maximum_fusion.refs_0_), channel_id=1, source_target_pairs={{0,6},{2,4},{4,2},{6,0},{1,7},{3,5},{5,3},{7,1},{8,14},{10,12},{12... | collective-permute-start | bytes 884744 | tf_op jit(solution)/shard_map/ppermute | solution.py:652
  30.7 1.6 %collective-permute-start.12 = (bf16[32,16,256]{2,1,0:T(8,128)(2,1)S(1)}, bf16[32,16,256]{2,1,0:T(8,128)(2,1)S(1)}, u32[]{:S(2)}, u32[]{:S(2)}) collective-permute-start(bf16[32,16,256]{2,1,0:T(8,128)(2,1)S(1)} %slice_bitcast_fusion.12), channel_id=1, source_target_pairs={{0,1},{1,0},{2,3},{3,2},{4,5},{5,4},{6,7},{7,6},{8,9},{9,8},{10,11... | collective-permute-start | bytes 786440 | tf_op jit(solution)/shard_map/ppermute | solution.py:648
  30.8 7.9 %collective-permute-start.16 = (bf16[2,288,256]{2,1,0:T(8,128)(2,1)S(1)}, bf16[2,288,256]{2,1,0:T(8,128)(2,1)}, u32[]{:S(2)}, u32[]{:S(2)}) collective-permute-start(bf16[2,288,256]{2,1,0:T(8,128)(2,1)S(1)} %pad_maximum_fusion.refs_0_), channel_id=1, source_target_pairs={{0,1},{1,0},{2,3},{3,2},{4,5},{5,4},{6,7},{7,6},{8,9},{9,8},{10,11... | collective-permute-start | bytes 884744 | tf_op jit(solution)/shard_map/ppermute | solution.py:685
  37.9 11.3 %copy-start.7 = (s32[4]{0:T(128)S(1)}, s32[4]{0:T(128)}, u32[]{:S(2)}) copy-start(s32[4]{0:T(128)} %counts_ref.1) | copy-start | bytes 52
  38.0 1.6 %collective-permute-start.17 = (bf16[2,288,256]{2,1,0:T(8,128)(2,1)S(1)}, bf16[2,288,256]{2,1,0:T(8,128)(2,1)S(1)}, u32[]{:S(2)}, u32[]{:S(2)}) collective-permute-start(bf16[2,288,256]{2,1,0:T(8,128)(2,1)S(1)} %collective-permute-done.13.refs_1_), channel_id=1, source_target_pairs={{0,1},{1,0},{2,3},{3,2},{4,5},{5,4},{6,7},{7,6},{8,9},{9,8},{10,11... | collective-permute-start | bytes 884744 | tf_op jit(solution)/shard_map/ppermute | solution.py:685
  38.2 1.9 %collective-permute-start.18 = (bf16[2,288,256]{2,1,0:T(8,128)(2,1)S(1)}, bf16[2,288,256]{2,1,0:T(8,128)(2,1)S(1)}, u32[]{:S(2)}, u32[]{:S(2)}) collective-permute-start(bf16[2,288,256]{2,1,0:T(8,128)(2,1)S(1)} %collective-permute-done.14.refs_2_), channel_id=1, source_target_pairs={{0,1},{1,0},{2,3},{3,2},{4,5},{5,4},{6,7},{7,6},{8,9},{9,8},{10,11... | collective-permute-start | bytes 884744 | tf_op jit(solution)/shard_map/ppermute | solution.py:685
  38.5 2.0 %collective-permute-start.19 = (bf16[2,288,256]{2,1,0:T(8,128)(2,1)S(1)}, bf16[2,288,256]{2,1,0:T(8,128)(2,1)}, u32[]{:S(2)}, u32[]{:S(2)}) collective-permute-start(bf16[2,288,256]{2,1,0:T(8,128)(2,1)S(1)} %collective-permute-done.15.refs_3_), channel_id=1, source_target_pairs={{0,1},{1,0},{2,3},{3,2},{4,5},{5,4},{6,7},{7,6},{8,9},{9,8},{10,11... | collective-permute-start | bytes 884744 | tf_op jit(solution)/shard_map/ppermute | solution.py:685
  45.5 13.4 %all-to-all-start.1 = ((bf16[8,2,2,32,256]{4,3,2,1,0:T(8,128)(2,1)}), bf16[8,2,2,32,256]{4,3,2,1,0:T(8,128)(2,1)S(1)}, u32[]{:S(2)}, u32[]{:S(2)}) async-start(bf16[8,2,2,32,256]{4,3,2,1,0:T(8,128)(2,1)} %spatial.1), calls=%async_computation.1 | async-start | bytes 1048576 | tf_op jit(solution)/shard_map/all_to_all | solution.py:706
  58.9 8.1 %collective-permute-start.2 = (bf16[2,2,32,256]{3,2,1,0:T(8,128)(2,1)S(1)}, bf16[2,2,32,256]{3,2,1,0:T(8,128)(2,1)}, u32[]{:S(2)}, u32[]{:S(2)}) collective-permute-start(bf16[2,2,32,256]{3,2,1,0:T(8,128)(2,1)S(1)} %slice_bitcast_fusion.2), channel_id=1, source_target_pairs={{24,0},{25,1},{26,2},{27,3},{28,4},{29,5},{30,6},{31,7}} | collective-permute-start | bytes 196616 | tf_op jit(solution)/shard_map/cond/branch_3_fun/ppermute | solution.py:715
